TPU v7x, 128 devices: a whole 4x4x4 slice. The times are simulated.
128 devices in a mesh: row: 32 (over y, x, core), col: 4 (over z).
Axes of the slice: x: 4, y: 4, z: 4, core: 2. Of those that a mesh axis runs over, the one named last changes fastest.
Arguments:
- probe_signs: int32 [32, 8, 1024, 1024], P(None, None, 'row', 'col'), may hold values from 0 to 1
- prior_scale: float32 [8, 1024, 1024], P(None, 'row', 'col'), may hold values from 0.02 to 6
- prior_factor: float32 [8, 8], replicated, may hold values from -3 to 3
- band_mix: float32 [8, 8], replicated, may hold values from -3 to 3
- inverse_noise_variance: float32 [8, 1024, 1024], P(None, 'row', 'col'), may hold values from 0.1 to 1
Outputs:
- basis: float32 [32, 8, 1024, 1024], P(None, None, 'row', 'col')
- r_factor: float32 [32, 32], replicated
All inputs are finite; a program needn't handle non-finite values.
Results may differ from a plain program's by a relative error of at most 0.00022.
Values sent between devices are 32-bit elements; how exact they have to be, the bound alone decides.
No kernel may reach another device: no remote copies, remote signals or barrier semaphores. Data moves between devices by JAX's collectives and lax.ppermute only.
A program may use at most 256 MiB of HBM per device.

v0:
```python
import numpy as np
import jax
import jax.numpy as jnp
from jax import lax
from jax.experimental import pallas as pl
from jax.experimental.pallas import tpu as pltpu
from jax.sharding import PartitionSpec as P

BANDS = 8
HALF = 15
TAPS = 31
ROWS = 32
COLS = 256
CHUNKS = 4
F32 = jnp.float32
BF16 = jnp.bfloat16
HI = lax.Precision.HIGHEST
VMEM = pl.BlockSpec(memory_space=pltpu.VMEM)


def taps_np():
    offsets = np.arange(TAPS) - HALF
    sigma = 1.0 + 0.5 * np.arange(BANDS)
    raw = np.exp(-offsets[None, :] ** 2 / (2.0 * sigma[:, None] ** 2))
    return raw / raw.sum(axis=1, keepdims=True)


def table_np(pos_in, pos_out):
    taps = taps_np()
    offset = np.asarray(pos_in)[:, None] - np.asarray(pos_out)[None, :]
    inside = np.abs(offset) <= HALF
    return np.where(inside[None], taps[:, np.clip(offset + HALF, 0, TAPS - 1)], 0.0)


def split_np(values):
    high = values.astype(BF16)
    low = (values - high.astype(np.float64)).astype(BF16)
    return high, low


def row_constants():
    out = np.arange(ROWS)
    main = table_np(np.arange(ROWS), out)
    above = table_np(np.arange(-HALF, 0), out)
    below = table_np(np.arange(ROWS, ROWS + HALF), out)
    by_out = np.zeros((BANDS, ROWS, 512))
    by_in = np.zeros((BANDS, ROWS, 512))
    pick = np.zeros((BANDS, 512))
    for c in range(BANDS):
        parts = ((c * ROWS, ROWS, main), (256 + c * HALF, HALF, above), (376 + c * HALF, HALF, below))
        for start, size, table in parts:
            by_out[:, :, start:start + size] = table.transpose(0, 2, 1)
            by_in[:, :, start:start + size] = table[c].T[None]
            pick[c, start:start + size] = 1.0
    spread = np.repeat(np.eye(BANDS), ROWS, axis=0)
    same = np.tile(np.eye(ROWS), (BANDS, BANDS))
    return [v.astype(np.float32) for v in (by_out.reshape(256, 512), by_in.reshape(256, 512), pick, spread, same)]


def col_constants():
    out = np.arange(COLS)
    main = table_np(np.arange(COLS), out)
    left = table_np(np.arange(-16, 0), out)
    right = table_np(np.arange(COLS, COLS + 16), out)
    halo = np.zeros((BANDS, 256, COLS))
    for b in range(BANDS):
        halo[b, 16 * b:16 * b + 16] = left[b]
        halo[b, 128 + 16 * b:128 + 16 * b + 16] = right[b]
    return split_np(main) + split_np(halo)


def split(values):
    high = values.astype(BF16)
    return high, (values - high.astype(F32)).astype(BF16)


def dot(a, b, precision=None):
    return lax.dot_general(a, b, (((1,), (0,)), ((), ())), precision=precision, preferred_element_type=F32)


def dot_nt(a, b):
    return lax.dot_general(a, b, (((1,), (1,)), ((), ())), preferred_element_type=F32)


def stacked(values):
    high, low = split(values)
    return jnp.concatenate([high, high, low], axis=0)


def params(mib=40):
    return pltpu.CompilerParams(vmem_limit_bytes=mib * 2**20)


def cost(flops, moved):
    return pl.CostEstimate(flops=int(flops), bytes_accessed=int(moved), transcendentals=0)


def prepare_kernel(factor, mix, by_out, by_in, pick, spread, same, first_m, last_m, mix_m, back_m):
    def expand(small, right):
        return dot(dot(spread[...], small, HI), right, HI)

    def store(out, whole):
        for part in range(whole.shape[1] // 256):
            high, low = split(whole[:, part * 256:part * 256 + 256])
            out[:, part * 768:part * 768 + 256] = high
            out[:, part * 768 + 256:part * 768 + 512] = low
            out[:, part * 768 + 512:part * 768 + 768] = high

    f = factor[...]
    a = mix[...]
    store(first_m, expand(f, pick[...]) * by_out[...])
    store(last_m, expand(f.T, pick[...]) * by_in[...])
    store(mix_m, expand(a, pick[:, :256]) * same[...])
    store(back_m, expand(a.T, pick[:, :256]) * same[...])


def prepare(factor, mix):
    wide = jax.ShapeDtypeStruct((256, 1536), BF16)
    narrow = jax.ShapeDtypeStruct((256, 768), BF16)
    return pl.pallas_call(
        prepare_kernel, out_shape=(wide, wide, narrow, narrow),
        in_specs=[VMEM] * 7, out_specs=(VMEM,) * 4, compiler_params=params(),
        name="prepare",
    )(factor, mix, *[jnp.asarray(v) for v in row_constants()])


def signed(ref_value):
    return 2.0 * ref_value.astype(F32) - 1.0


def store_edges(tile, top, bottom, p):
    for b in range(BANDS):
        top[p, b * HALF:(b + 1) * HALF, :] = tile[b, 0:HALF, :]
        bottom[p, b * HALF:(b + 1) * HALF, :] = tile[b, ROWS - HALF:ROWS, :]


def edge_kernel(signs, scale, top, bottom):
    for p in range(signs.shape[0]):
        store_edges(scale[...] * signed(signs[p]), top, bottom, p)


def edges(signs, scale, chunk, count):
    per = 2
    shape = jax.ShapeDtypeStruct((count, BANDS * HALF, COLS), F32)
    return pl.pallas_call(
        edge_kernel, grid=(count // per,), out_shape=(shape, shape),
        in_specs=[
            pl.BlockSpec((per, BANDS, ROWS, COLS), lambda i: (chunk * (count // per) + i, 0, 0, 0)),
            pl.BlockSpec((BANDS, ROWS, COLS), lambda i: (0, 0, 0)),
        ],
        out_specs=[pl.BlockSpec((per, BANDS * HALF, COLS), lambda i: (i, 0, 0))] * 2,
        compiler_params=params(), cost_estimate=cost(1e6, count * 2**19), name="edges",
    )(signs, scale)


def store_packed(tile, left, right, p):
    lane = lax.broadcasted_iota(jnp.int32, (ROWS, 128), 1) // 16
    low = tile[0, :, :128]
    high = pltpu.roll(tile[0, :, 128:], 16, 1)
    for b in range(1, BANDS):
        low = jnp.where(lane == b, pltpu.roll(tile[b, :, :128], 16 * b, 1), low)
        mine = tile[b, :, 128:]
        if b < BANDS - 1:
            mine = pltpu.roll(mine, 16 * b + 16, 1)
        high = jnp.where(lane == b, mine, high)
    left[p] = low
    right[p] = high


def halo_rows(top, bottom, p):
    return jnp.concatenate([top[p], bottom[p], jnp.zeros((16, COLS), F32)], axis=0)


def first_kernel(signs, scale, top, bottom, matrix, out, left, right):
    scaled = (scale[...] * signed(signs[0])).reshape(256, COLS)
    whole = jnp.concatenate([stacked(scaled), stacked(halo_rows(top, bottom, 0))], axis=0)
    tile = dot(matrix[...], whole).reshape(BANDS, ROWS, COLS)
    out[0] = tile
    store_packed(tile, left, right, 0)


def first_stage(signs, scale, top, bottom, matrix, chunk, count):
    packed = jax.ShapeDtypeStruct((count, ROWS, 128), F32)
    tile = pl.BlockSpec((1, BANDS, ROWS, COLS), lambda i: (i, 0, 0, 0))
    edge = pl.BlockSpec((1, BANDS * HALF, COLS), lambda i: (i, 0, 0))
    pack = pl.BlockSpec((1, ROWS, 128), lambda i: (i, 0, 0))
    return pl.pallas_call(
        first_kernel, grid=(count,),
        out_shape=(jax.ShapeDtypeStruct((count, BANDS, ROWS, COLS), F32), packed, packed),
        in_specs=[
            pl.BlockSpec((1, BANDS, ROWS, COLS), lambda i: (chunk * count + i, 0, 0, 0)),
            pl.BlockSpec((BANDS, ROWS, COLS), lambda i: (0, 0, 0)),
            edge, edge,
            pl.BlockSpec((256, 1536), lambda i: (0, 0)),
        ],
        out_specs=[tile, pack, pack],
        compiler_params=params(), cost_estimate=cost(count * 2 * 256 * 1536 * 256, count * 2**20),
        name="first_stage",
    )(signs, scale, top, bottom, matrix)


def column_blur(tiles, left, right, main_h, main_l, halo_h, halo_l, out):
    count = tiles.shape[0]
    flat = count * ROWS
    eh, el = split(jnp.concatenate([left[...], right[...]], axis=-1).reshape(flat, 256))

    @pl.loop(0, BANDS)
    def _(b):
        uh, ul = split(tiles[:, b].reshape(flat, COLS))
        blurred = dot(uh, main_h[b]) + dot(ul, main_h[b]) + dot(uh, main_l[b])
        blurred += dot(eh, halo_h[b]) + dot(el, halo_h[b]) + dot(eh, halo_l[b])
        out[:, b] = blurred.reshape(count, ROWS, COLS)


def middle_kernel(tiles, left, right, main_h, main_l, halo_h, halo_l, mix, back, weights, out, out_left, out_right, blurred):
    column_blur(tiles, left, right, main_h, main_l, halo_h, halo_l, blurred)
    weight = weights[...].reshape(256, COLS)

    @pl.loop(0, tiles.shape[0])
    def _(p):
        weighted = weight * dot(mix[...], stacked(blurred[p].reshape(256, COLS)))
        tile = dot(back[...], stacked(weighted)).reshape(BANDS, ROWS, COLS)
        out[p] = tile
        store_packed(tile, out_left, out_right, p)


def middle_stage(tiles, left, right, tables, mix, back, weights):
    count = tiles.shape[0]
    whole = jax.ShapeDtypeStruct((count, BANDS, ROWS, COLS), F32)
    packed = jax.ShapeDtypeStruct((count, ROWS, 128), F32)
    return pl.pallas_call(
        middle_kernel, out_shape=(whole, packed, packed),
        in_specs=[VMEM] * 10, out_specs=(VMEM,) * 3,
        scratch_shapes=[pltpu.VMEM((count, BANDS, ROWS, COLS), F32)],
        compiler_params=params(), cost_estimate=cost(count * 12 * 2 * 256**3, count * 2**20),
        name="middle_stage",
    )(tiles, left, right, *tables, mix, back, weights)


def last_column_kernel(tiles, left, right, main_h, main_l, halo_h, halo_l, out, top, bottom):
    column_blur(tiles, left, right, main_h, main_l, halo_h, halo_l, out)

    @pl.loop(0, tiles.shape[0])
    def _(p):
        store_edges(out[p], top, bottom, p)


def last_column_stage(tiles, left, right, tables):
    count = tiles.shape[0]
    whole = jax.ShapeDtypeStruct((count, BANDS, ROWS, COLS), F32)
    edge = jax.ShapeDtypeStruct((count, BANDS * HALF, COLS), F32)
    return pl.pallas_call(
        last_column_kernel, out_shape=(whole, edge, edge),
        in_specs=[VMEM] * 7, out_specs=(VMEM,) * 3,
        compiler_params=params(), cost_estimate=cost(count * 6 * 2 * 256**3, count * 2**20),
        name="last_column_stage",
    )(tiles, left, right, *tables)


def sketch_kernel(tiles, top, bottom, matrix, signs, scale, out):
    whole = jnp.concatenate([stacked(tiles[0].reshape(256, COLS)), stacked(halo_rows(top, bottom, 0))], axis=0)
    mixed = dot(matrix[...], whole).reshape(BANDS, ROWS, COLS)
    out[0] = scale[...] * mixed + signed(signs[0])


def sketch_stage(tiles, top, bottom, matrix, signs, scale, chunk):
    count = tiles.shape[0]
    tile = pl.BlockSpec((1, BANDS, ROWS, COLS), lambda i: (i, 0, 0, 0))
    edge = pl.BlockSpec((1, BANDS * HALF, COLS), lambda i: (i, 0, 0))
    return pl.pallas_call(
        sketch_kernel, grid=(count,),
        out_shape=jax.ShapeDtypeStruct((count, BANDS, ROWS, COLS), F32),
        in_specs=[
            tile, edge, edge,
            pl.BlockSpec((256, 1536), lambda i: (0, 0)),
            pl.BlockSpec((1, BANDS, ROWS, COLS), lambda i: (chunk * count + i, 0, 0, 0)),
            pl.BlockSpec((BANDS, ROWS, COLS), lambda i: (0, 0, 0)),
        ],
        out_specs=tile,
        compiler_params=params(), cost_estimate=cost(count * 2 * 256 * 1536 * 256, count * 2**20),
        name="sketch_stage",
    )(tiles, top, bottom, matrix, signs, scale)


def gather_group(refs, g):
    return jnp.concatenate([r[:, g].reshape(-1, COLS) for r in refs], axis=0)


def same_place(shape):
    return lax.broadcasted_iota(jnp.int32, shape, 0) % 8 == lax.broadcasted_iota(jnp.int32, shape, 1) % 8


def spread_ones(shape, long_dim):
    long = lax.broadcasted_iota(jnp.int32, shape, long_dim) // 8
    short = lax.broadcasted_iota(jnp.int32, shape, 1 - long_dim)
    return (long == short).astype(F32)


def gram_kernel(*refs):
    chunks, out, even, cross = refs[:CHUNKS], refs[CHUNKS], refs[CHUNKS + 1], refs[CHUNKS + 2]
    even[...] = jnp.zeros_like(even)
    cross[...] = jnp.zeros_like(cross)

    @pl.loop(0, chunks[0].shape[1])
    def _(g):
        values = gather_group(chunks, g)
        high, middle = split(values)
        low = (values - high.astype(F32) - middle.astype(F32)).astype(BF16)
        even[...] += dot_nt(high, high) + dot_nt(middle, middle)
        cross[...] += dot_nt(high, middle) + dot_nt(high, low)

    order = even.shape[0]
    keep = same_place((order, order))

    def collapse(table):
        kept = jnp.where(keep, table, 0.0)
        return dot(dot(spread_ones((order // 8, order), 1), kept, HI), spread_ones((order, order // 8), 0), HI)

    mixed = collapse(cross[...])
    out[0] = collapse(even[...]) + (mixed + mixed.T)
    out[1] = jnp.zeros(out.shape[1:], F32)


def gram_stage(chunks):
    probes = sum(c.shape[0] for c in chunks)
    return pl.pallas_call(
        gram_kernel, out_shape=jax.ShapeDtypeStruct((2, probes, probes), F32),
        in_specs=[VMEM] * CHUNKS, out_specs=VMEM,
        scratch_shapes=[pltpu.VMEM((256, 256), F32)] * 2,
        compiler_params=params(), cost_estimate=cost(32 * 4 * 2 * 256**3, 2**23), name="gram_stage",
    )(*chunks)


def two_sum(a, b):
    total = a + b
    part = total - a
    return total, (a - (total - part)) + (b - part)


def quick_sum(a, b):
    total = a + b
    return total, b - (total - a)


def halves(a):
    wide = a * 4097.0
    high = wide - (wide - a)
    return high, a - high


def two_product(a, b):
    product = a * b
    ah, al = halves(a)
    bh, bl = halves(b)
    return product, ((ah * bh - product) + ah * bl + al * bh) + al * bl


def pair_add(a, b):
    total, error = two_sum(a[0], b[0])
    return quick_sum(total, error + (a[1] + b[1]))


def pair_mul(a, b):
    product, error = two_product(a[0], b[0])
    return quick_sum(product, error + (a[0] * b[1] + a[1] * b[0]))


def pair_neg(a):
    return -a[0], -a[1]


def merge_kernel(mine, other, out):
    total = pair_add((mine[0], mine[1]), (other[0], other[1]))
    out[0] = total[0]
    out[1] = total[1]


def merge(mine, other):
    return pl.pallas_call(
        merge_kernel, out_shape=jax.ShapeDtypeStruct(mine.shape, F32),
        in_specs=[VMEM] * 2, out_specs=VMEM, compiler_params=params(8), name="merge",
    )(mine, other)


def sum_over(value, axis):
    count = lax.axis_size(axis)
    bit = 1
    while bit < count:
        value = merge(value, lax.ppermute(value, axis, [(i, i ^ bit) for i in range(count)]))
        bit *= 2
    return value


def factor_kernel(gram, factor, inverse, work, *, norm):
    order = gram.shape[1]
    work[...] = jnp.zeros_like(work)
    row = lax.broadcasted_iota(jnp.int32, (order, 128), 0)
    lane = lax.broadcasted_iota(jnp.int32, (order, 128), 1)
    work[0] = (lane == row + order).astype(F32)
    work[0, :, 0:order] = gram[0]
    work[1, :, 0:order] = gram[1]
    now = (work[0], work[1])
    for k in range(order - 1):
        pivot_row = tuple(v[k:k + 1, :] for v in now)
        pivot = tuple(jnp.broadcast_to(v[:, k:k + 1], (1, 128)) for v in pivot_row)
        first = pivot_row[0] / pivot[0]
        rest = pair_add(pivot_row, pair_neg(pair_mul((first, jnp.zeros_like(first)), pivot)))
        ratio = quick_sum(first, rest[0] / pivot[0])
        column = tuple(
            jnp.where(row > k, jnp.broadcast_to(v[:, k:k + 1], (order, 128)), 0.0) for v in now
        )
        now = pair_add(now, pair_neg(pair_mul(column, ratio)))
    diagonal = jnp.sum(jnp.where(lane == row, now[0], 0.0), axis=1, keepdims=True)
    scaled = now[0] / jnp.sqrt(diagonal)
    factor[...] = jnp.where(lane >= row, scaled, 0.0)[:, 0:order] * (1.0 / norm)
    inverse[...] = scaled[:, order:2 * order] * norm


def factor_stage(gram, norm):
    order = gram.shape[1]
    square = jax.ShapeDtypeStruct((order, order), F32)
    return pl.pallas_call(
        lambda *refs: factor_kernel(*refs, norm=norm), out_shape=(square, square),
        in_specs=[VMEM], out_specs=(VMEM, VMEM), scratch_shapes=[pltpu.VMEM((2, order, 128), F32)],
        compiler_params=params(8), name="factor_stage",
    )(gram)


def basis_kernel(inverse, *refs):
    chunks, out, matrix = refs[:CHUNKS], refs[CHUNKS], refs[CHUNKS + 1]
    order = matrix.shape[0]

    @pl.when(pl.program_id(0) == 0)
    def _():
        wide = dot(dot(spread_ones((order, order // 8), 0), inverse[...], HI), spread_ones((order // 8, order), 1), HI)
        high, low = split(jnp.where(same_place((order, order)), wide, 0.0))
        matrix[:, 0:order] = high
        matrix[:, order:2 * order] = low
        matrix[:, 2 * order:3 * order] = high

    @pl.loop(0, chunks[0].shape[1])
    def _(g):
        values = dot(matrix[...], stacked(gather_group(chunks, g)))
        out[:, g] = values.reshape(-1, 8, COLS)


def basis_stage(inverse, chunks):
    probes = inverse.shape[0]
    groups = chunks[0].shape[1]
    per = 4
    return pl.pallas_call(
        basis_kernel, grid=(groups // per,),
        out_shape=jax.ShapeDtypeStruct((probes, groups, 8, COLS), F32),
        in_specs=[pl.BlockSpec((probes, probes), lambda i: (0, 0))]
        + [pl.BlockSpec((c.shape[0], per, 8, COLS), lambda i: (0, i, 0, 0)) for c in chunks],
        out_specs=pl.BlockSpec((probes, per, 8, COLS), lambda i: (0, i, 0, 0)),
        scratch_shapes=[pltpu.VMEM((256, 768), BF16)],
        compiler_params=params(), cost_estimate=cost(32 * 3 * 2 * 256**3, 2**24), name="basis_stage",
    )(inverse, *chunks)


def both_ways(to_previous, to_next, axis):
    count = lax.axis_size(axis)
    forward = [(i, i + 1) for i in range(count - 1)]
    backward = [(i + 1, i) for i in range(count - 1)]
    return lax.ppermute(to_next, axis, forward), lax.ppermute(to_previous, axis, backward)


def shards(probe_signs, prior_scale, prior_factor, band_mix, inverse_noise_variance):
    probes = probe_signs.shape[0]
    count = probes // CHUNKS
    tables = [jnp.asarray(v) for v in col_constants()]
    rows = []
    for k in range(CHUNKS):
        rows.append(both_ways(*edges(probe_signs, prior_scale, k, count), "row"))
    first_m, last_m, mix_m, back_m = prepare(prior_factor, band_mix)
    sketch = []
    for k in range(CHUNKS):
        tiles, left, right = first_stage(probe_signs, prior_scale, *rows[k], first_m, k, count)
        left, right = both_ways(left, right, "col")
        tiles, left, right = middle_stage(tiles, left, right, tables, mix_m, back_m, inverse_noise_variance)
        left, right = both_ways(left, right, "col")
        tiles, top, bottom = last_column_stage(tiles, left, right, tables)
        top, bottom = both_ways(top, bottom, "row")
        sketch.append(sketch_stage(tiles, top, bottom, last_m, probe_signs, prior_scale, k))
    grouped = [s.reshape(count, BANDS * ROWS // 8, 8, COLS) for s in sketch]
    gram = sum_over(sum_over(gram_stage(grouped), "row"), "col")
    total = BANDS * ROWS * COLS * lax.axis_size("row") * lax.axis_size("col")
    r_factor, inverse = factor_stage(gram, float(np.sqrt(np.float32(total))))
    basis = basis_stage(inverse, grouped)
    return basis.reshape(probes, BANDS, ROWS, COLS), r_factor


def solution(mesh):
    in_specs = (P(None, None, "row", "col"), P(None, "row", "col"), P(), P(), P(None, "row", "col"))
    out_specs = (P(None, None, "row", "col"), P())
    return jax.shard_map(shards, mesh=mesh, in_specs=in_specs, out_specs=out_specs, check_vma=False)
```

profile of v0, /device:TPU:56, one launch (start us, length us, event | category | flops | bytes accessed | tf_op | source)
XLA Modules:
  0.0 305.5 jit_solution(11097172887780673311)
XLA Ops:
  0.6 3.4 %copy-done = s32[32,8,32,256]{3,2,1,0:T(8,128)S(1)} copy-done((s32[32,8,32,256]{3,2,1,0:T(8,128)S(1)}, s32[32,8,32,256]{3,2,1,0:T(8,128)}, u32[]{:S(2)}) %copy-start) | copy-done | bytes 8388632
  8.6 5.8 %collective-permute-start.25 = (f32[8,120,256]{2,1,0:T(8,128)}, f32[8,120,256]{2,1,0:T(8,128)S(1)}, u32[]{:S(2)}, u32[]{:S(2)}) collective-permute-start(f32[8,120,256]{2,1,0:T(8,128)} %get-tuple-element.90), channel_id=1, source_target_pairs={{4,0},{8,4},{12,8},{16,12},{20,16},{24,20},{28,24},{32,28},{36,32}... | collective-permute-start | bytes 2949128 | tf_op jit(solution)/shard_map/ppermute | solution.py:466
  18.2 5.8 %collective-permute-start.17 = (f32[8,120,256]{2,1,0:T(8,128)}, f32[8,120,256]{2,1,0:T(8,128)}, u32[]{:S(2)}, u32[]{:S(2)}) collective-permute-start(f32[8,120,256]{2,1,0:T(8,128)} %get-tuple-element.79), channel_id=1, source_target_pairs={{4,0},{8,4},{12,8},{16,12},{20,16},{24,20},{28,24},{32,28},{36,32}... | collective-permute-start | bytes 2949128 | tf_op jit(solution)/shard_map/ppermute | solution.py:466
  25.9 2.0 collective-permute-start
  28.0 6.0 %collective-permute-start.1 = (f32[8,120,256]{2,1,0:T(8,128)}, f32[8,120,256]{2,1,0:T(8,128)S(1)}, u32[]{:S(2)}, u32[]{:S(2)}) collective-permute-start(f32[8,120,256]{2,1,0:T(8,128)} %get-tuple-element.53), channel_id=1, source_target_pairs={{4,0},{8,4},{12,8},{16,12},{20,16},{24,20},{28,24},{32,28},{36,32}... | collective-permute-start | bytes 2949128 | tf_op jit(solution)/shard_map/ppermute | solution.py:466
  37.0 2.0 collective-permute-start.8
  40.1 5.7 %collective-permute-start.9 = (f32[8,120,256]{2,1,0:T(8,128)}, f32[8,120,256]{2,1,0:T(8,128)S(1)}, u32[]{:S(2)}, u32[]{:S(2)}) collective-permute-start(f32[8,120,256]{2,1,0:T(8,128)} %get-tuple-element.68), channel_id=1, source_target_pairs={{4,0},{8,4},{12,8},{16,12},{20,16},{24,20},{28,24},{32,28},{36,32}... | collective-permute-start | bytes 2949128 | tf_op jit(solution)/shard_map/ppermute | solution.py:466
  48.9 2.7 prepare.1
  53.7 4.7 %first_stage.7 = (f32[8,8,32,256]{3,2,1,0:T(8,128)S(1)}, f32[8,32,128]{2,1,0:T(8,128)}, f32[8,32,128]{2,1,0:T(8,128)}) custom-call(s32[32,8,32,256]{3,2,1,0:T(8,128)S(1)} %bitcast.6, f32[8,32,256]{2,1,0:T(8,128)S(1)} %copy-done.1, f32[8,120,256]{2,1,0:T(8,128)S(1)} %copy-done.13, f32[8,120,256]{2,1,0:T(8,128)S(1)} %copy-done.15, ...), custom_call_target="tpu_custom_call" | custom-call | flops 1610612736 | bytes 8388608 | tf_op jit(solution)/shard_map/first_stage/pallas_call | solution.py:187
  59.8 3.8 %collective-permute-start.26 = (f32[8,32,128]{2,1,0:T(8,128)}, f32[8,32,128]{2,1,0:T(8,128)S(1)}, u32[]{:S(2)}, u32[]{:S(2)}) collective-permute-start(f32[8,32,128]{2,1,0:T(8,128)} %get-tuple-element.92), channel_id=1, source_target_pairs={{0,1},{1,2},{2,3},{4,5},{5,6},{6,7},{8,9},{9,10},{10,11},{12,13},{... | collective-permute-start | bytes 393224 | tf_op jit(solution)/shard_map/ppermute | solution.py:466
  63.6 6.7 %first_stage.6 = (f32[8,8,32,256]{3,2,1,0:T(8,128)S(1)}, f32[8,32,128]{2,1,0:T(8,128)S(1)}, f32[8,32,128]{2,1,0:T(8,128)}) custom-call(s32[32,8,32,256]{3,2,1,0:T(8,128)S(1)} %bitcast.6, f32[8,32,256]{2,1,0:T(8,128)S(1)} %copy-done.1, f32[8,120,256]{2,1,0:T(8,128)S(1)} %copy-done.11, f32[8,120,256]{2,1,0:T(8,128)} %collective-permute-done.17.bottom, ...), custom_call_target="tpu_custom_call" | custom-call | flops 1610612736 | bytes 8388608 | tf_op jit(solution)/shard_map/first_stage/pallas_call | solution.py:187
  71.6 2.0 collective-permute-start.27
  73.7 3.8 %collective-permute-start.18 = (f32[8,32,128]{2,1,0:T(8,128)}, f32[8,32,128]{2,1,0:T(8,128)}, u32[]{:S(2)}, u32[]{:S(2)}) collective-permute-start(f32[8,32,128]{2,1,0:T(8,128)} %get-tuple-element.81), channel_id=1, source_target_pairs={{0,1},{1,2},{2,3},{4,5},{5,6},{6,7},{8,9},{9,10},{10,11},{12,13},{... | collective-permute-start | bytes 393224 | tf_op jit(solution)/shard_map/ppermute | solution.py:466
  77.5 3.7 %first_stage.4 = (f32[8,8,32,256]{3,2,1,0:T(8,128)S(1)}, f32[8,32,128]{2,1,0:T(8,128)S(1)}, f32[8,32,128]{2,1,0:T(8,128)S(1)}) custom-call(s32[32,8,32,256]{3,2,1,0:T(8,128)S(1)} %bitcast.6, f32[8,32,256]{2,1,0:T(8,128)S(1)} %copy-done.1, f32[8,120,256]{2,1,0:T(8,128)S(1)} %collective-permute-done.top, f32[8,120,256]{2,1,0:T(8,128)S(1)} %collective-permute-done.1.bottom, ...), custom_call_target="tpu_custom_call" | custom-call | flops 1610612736 | bytes 8388608 | tf_op jit(solution)/shard_map/first_stage/pallas_call | solution.py:187
  82.5 4.2 %collective-permute-start.2 = (f32[8,32,128]{2,1,0:T(8,128)S(1)}, f32[8,32,128]{2,1,0:T(8,128)S(1)}, u32[]{:S(2)}, u32[]{:S(2)}) collective-permute-start(f32[8,32,128]{2,1,0:T(8,128)S(1)} %get-tuple-element.56), channel_id=1, source_target_pairs={{0,1},{1,2},{2,3},{4,5},{5,6},{6,7},{8,9},{9,10},{10,11},{12,13},{... | collective-permute-start | bytes 393224 | tf_op jit(solution)/shard_map/ppermute | solution.py:466
  86.8 2.2 collective-permute-start.3
  89.0 3.7 %first_stage.5 = (f32[8,8,32,256]{3,2,1,0:T(8,128)S(1)}, f32[8,32,128]{2,1,0:T(8,128)S(1)}, f32[8,32,128]{2,1,0:T(8,128)S(1)}) custom-call(s32[32,8,32,256]{3,2,1,0:T(8,128)S(1)} %bitcast.6, f32[8,32,256]{2,1,0:T(8,128)S(1)} %copy-done.1, f32[8,120,256]{2,1,0:T(8,128)S(1)} %collective-permute-done.8.top, f32[8,120,256]{2,1,0:T(8,128)S(1)} %collective-permute-done.9.bottom, ...), custom_call_target="tpu_custom_call" | custom-call | flops 1610612736 | bytes 8388608 | tf_op jit(solution)/shard_map/first_stage/pallas_call | solution.py:187
  94.0 3.9 %collective-permute-start.10 = (f32[8,32,128]{2,1,0:T(8,128)S(1)}, f32[8,32,128]{2,1,0:T(8,128)S(1)}, u32[]{:S(2)}, u32[]{:S(2)}) collective-permute-start(f32[8,32,128]{2,1,0:T(8,128)S(1)} %get-tuple-element.70), channel_id=1, source_target_pairs={{0,1},{1,2},{2,3},{4,5},{5,6},{6,7},{8,9},{9,10},{10,11},{12,13},{... | collective-permute-start | bytes 393224 | tf_op jit(solution)/shard_map/ppermute | solution.py:466
  101.5 9.0 %middle_stage.4 = (f32[8,8,32,256]{3,2,1,0:T(8,128)S(1)}, f32[8,32,128]{2,1,0:T(8,128)S(1)}, f32[8,32,128]{2,1,0:T(8,128)S(1)}) custom-call(f32[8,8,32,256]{3,2,1,0:T(8,128)S(1)} %copy-done.34, f32[8,32,128]{2,1,0:T(8,128)S(1)} %collective-permute-done.2.left, f32[8,32,128]{2,1,0:T(8,128)S(1)} %collective-permute-done.3.right, ...), custom_call_target="tpu_custom_call" | custom-call | flops 3221225472 | bytes 8388608 | tf_op jit(solution)/shard_map/middle_stage/pallas_call | solution.py:231
  110.5 3.9 %collective-permute-start.4 = (f32[8,32,128]{2,1,0:T(8,128)S(1)}, f32[8,32,128]{2,1,0:T(8,128)S(1)}, u32[]{:S(2)}, u32[]{:S(2)}) collective-permute-start(f32[8,32,128]{2,1,0:T(8,128)S(1)} %get-tuple-element.61), channel_id=1, source_target_pairs={{0,1},{1,2},{2,3},{4,5},{5,6},{6,7},{8,9},{9,10},{10,11},{12,13},{... | collective-permute-start | bytes 393224 | tf_op jit(solution)/shard_map/ppermute | solution.py:466
  116.4 9.0 %middle_stage.5 = (f32[8,8,32,256]{3,2,1,0:T(8,128)S(1)}, f32[8,32,128]{2,1,0:T(8,128)S(1)}, f32[8,32,128]{2,1,0:T(8,128)S(1)}) custom-call(f32[8,8,32,256]{3,2,1,0:T(8,128)S(1)} %copy-done.32, f32[8,32,128]{2,1,0:T(8,128)S(1)} %collective-permute-done.10.left, f32[8,32,128]{2,1,0:T(8,128)S(1)} %collective-permute-done.11.right, ...), custom_call_target="tpu_custom_call" | custom-call | flops 3221225472 | bytes 8388608 | tf_op jit(solution)/shard_map/middle_stage/pallas_call | solution.py:231
  125.4 3.9 %collective-permute-start.12 = (f32[8,32,128]{2,1,0:T(8,128)S(1)}, f32[8,32,128]{2,1,0:T(8,128)S(1)}, u32[]{:S(2)}, u32[]{:S(2)}) collective-permute-start(f32[8,32,128]{2,1,0:T(8,128)S(1)} %get-tuple-element.73), channel_id=1, source_target_pairs={{0,1},{1,2},{2,3},{4,5},{5,6},{6,7},{8,9},{9,10},{10,11},{12,13},{... | collective-permute-start | bytes 393224 | tf_op jit(solution)/shard_map/ppermute | solution.py:466
  131.2 4.5 %last_column_stage.4 = (f32[8,8,32,256]{3,2,1,0:T(8,128)S(1)}, f32[8,120,256]{2,1,0:T(8,128)}, f32[8,120,256]{2,1,0:T(8,128)}) custom-call(f32[8,8,32,256]{3,2,1,0:T(8,128)S(1)} %get-tuple-element.60.tiles, f32[8,32,128]{2,1,0:T(8,128)S(1)} %collective-permute-done.4.left, f32[8,32,128]{2,1,0:T(8,128)S(1)} %collective-permute-done.5.right, ...), custom_call_target="tpu_custom_call" | custom-call | flops 1610612736 | bytes 8388608 | tf_op jit(solution)/shard_map/last_column_stage/pallas_call | solution.py:252
  139.7 4.6 %last_column_stage.5 = (f32[8,8,32,256]{3,2,1,0:T(8,128)S(1)}, f32[8,120,256]{2,1,0:T(8,128)}, f32[8,120,256]{2,1,0:T(8,128)}) custom-call(f32[8,8,32,256]{3,2,1,0:T(8,128)S(1)} %get-tuple-element.72.tiles, f32[8,32,128]{2,1,0:T(8,128)S(1)} %collective-permute-done.12.left, f32[8,32,128]{2,1,0:T(8,128)S(1)} %collective-permute-done.13.right, ...), custom_call_target="tpu_custom_call" | custom-call | flops 1610612736 | bytes 8388608 | tf_op jit(solution)/shard_map/last_column_stage/pallas_call | solution.py:252
  144.9 5.7 %collective-permute-start.7 = (f32[8,120,256]{2,1,0:T(8,128)}, f32[8,120,256]{2,1,0:T(8,128)S(1)}, u32[]{:S(2)}, u32[]{:S(2)}) collective-permute-start(f32[8,120,256]{2,1,0:T(8,128)} %get-tuple-element.65), channel_id=1, source_target_pairs={{4,0},{8,4},{12,8},{16,12},{20,16},{24,20},{28,24},{32,28},{36,32}... | collective-permute-start | bytes 2949128 | tf_op jit(solution)/shard_map/ppermute | solution.py:466
  153.5 10.0 %middle_stage.7 = (f32[8,8,32,256]{3,2,1,0:T(8,128)S(1)}, f32[8,32,128]{2,1,0:T(8,128)S(1)}, f32[8,32,128]{2,1,0:T(8,128)S(1)}) custom-call(f32[8,8,32,256]{3,2,1,0:T(8,128)S(1)} %copy-done.30, f32[8,32,128]{2,1,0:T(8,128)S(1)} %copy-done.42, f32[8,32,128]{2,1,0:T(8,128)} %collective-permute-done.27.right, bf16[8,256,256]{2,1,0:T(8,128)(2,1)S(1)} %copy-done.7, ...), custom_call_target="tpu_custom_call" | custom-call | flops 3221225472 | bytes 8388608 | tf_op jit(solution)/shard_map/middle_stage/pallas_call | solution.py:231
  163.5 3.9 %collective-permute-start.28 = (f32[8,32,128]{2,1,0:T(8,128)S(1)}, f32[8,32,128]{2,1,0:T(8,128)S(1)}, u32[]{:S(2)}, u32[]{:S(2)}) collective-permute-start(f32[8,32,128]{2,1,0:T(8,128)S(1)} %get-tuple-element.95), channel_id=1, source_target_pairs={{0,1},{1,2},{2,3},{4,5},{5,6},{6,7},{8,9},{9,10},{10,11},{12,13},{... | collective-permute-start | bytes 393224 | tf_op jit(solution)/shard_map/ppermute | solution.py:466
  167.5 9.9 %middle_stage.6 = (f32[8,8,32,256]{3,2,1,0:T(8,128)S(1)}, f32[8,32,128]{2,1,0:T(8,128)S(1)}, f32[8,32,128]{2,1,0:T(8,128)S(1)}) custom-call(f32[8,8,32,256]{3,2,1,0:T(8,128)S(1)} %copy-done.28, f32[8,32,128]{2,1,0:T(8,128)} %collective-permute-done.18.left, f32[8,32,128]{2,1,0:T(8,128)S(1)} %collective-permute-done.19.right, ...), custom_call_target="tpu_custom_call" | custom-call | flops 3221225472 | bytes 8388608 | tf_op jit(solution)/shard_map/middle_stage/pallas_call | solution.py:231
  177.4 3.9 %collective-permute-start.20 = (f32[8,32,128]{2,1,0:T(8,128)S(1)}, f32[8,32,128]{2,1,0:T(8,128)S(1)}, u32[]{:S(2)}, u32[]{:S(2)}) collective-permute-start(f32[8,32,128]{2,1,0:T(8,128)S(1)} %get-tuple-element.84), channel_id=1, source_target_pairs={{0,1},{1,2},{2,3},{4,5},{5,6},{6,7},{8,9},{9,10},{10,11},{12,13},{... | collective-permute-start | bytes 393224 | tf_op jit(solution)/shard_map/ppermute | solution.py:466
  186.1 2.0 collective-permute-done.21.right
  188.1 5.2 %collective-permute-start.15 = (f32[8,120,256]{2,1,0:T(8,128)}, f32[8,120,256]{2,1,0:T(8,128)S(1)}, u32[]{:S(2)}, u32[]{:S(2)}) collective-permute-start(f32[8,120,256]{2,1,0:T(8,128)} %get-tuple-element.77), channel_id=1, source_target_pairs={{4,0},{8,4},{12,8},{16,12},{20,16},{24,20},{28,24},{32,28},{36,32}... | collective-permute-start | bytes 2949128 | tf_op jit(solution)/shard_map/ppermute | solution.py:466
  193.3 4.6 %last_column_stage.6 = (f32[8,8,32,256]{3,2,1,0:T(8,128)S(1)}, f32[8,120,256]{2,1,0:T(8,128)}, f32[8,120,256]{2,1,0:T(8,128)}) custom-call(f32[8,8,32,256]{3,2,1,0:T(8,128)S(1)} %get-tuple-element.83.tiles, f32[8,32,128]{2,1,0:T(8,128)S(1)} %collective-permute-done.20.left, f32[8,32,128]{2,1,0:T(8,128)S(1)} %collective-permute-done.21.right, ...), custom_call_target="tpu_custom_call" | custom-call | flops 1610612736 | bytes 8388608 | tf_op jit(solution)/shard_map/last_column_stage/pallas_call | solution.py:252
  199.8 5.8 %collective-permute-start.23 = (f32[8,120,256]{2,1,0:T(8,128)}, f32[8,120,256]{2,1,0:T(8,128)}, u32[]{:S(2)}, u32[]{:S(2)}) collective-permute-start(f32[8,120,256]{2,1,0:T(8,128)} %get-tuple-element.88), channel_id=1, source_target_pairs={{4,0},{8,4},{12,8},{16,12},{20,16},{24,20},{28,24},{32,28},{36,32}... | collective-permute-start | bytes 2949128 | tf_op jit(solution)/shard_map/ppermute | solution.py:466
  205.6 4.5 %last_column_stage.7 = (f32[8,8,32,256]{3,2,1,0:T(8,128)S(1)}, f32[8,120,256]{2,1,0:T(8,128)}, f32[8,120,256]{2,1,0:T(8,128)}) custom-call(f32[8,8,32,256]{3,2,1,0:T(8,128)S(1)} %get-tuple-element.94.tiles, f32[8,32,128]{2,1,0:T(8,128)S(1)} %collective-permute-done.28.left, f32[8,32,128]{2,1,0:T(8,128)S(1)} %collective-permute-done.29.right, ...), custom_call_target="tpu_custom_call" | custom-call | flops 1610612736 | bytes 8388608 | tf_op jit(solution)/shard_map/last_column_stage/pallas_call | solution.py:252
  214.4 5.9 %collective-permute-start.31 = (f32[8,120,256]{2,1,0:T(8,128)}, f32[8,120,256]{2,1,0:T(8,128)S(1)}, u32[]{:S(2)}, u32[]{:S(2)}) collective-permute-start(f32[8,120,256]{2,1,0:T(8,128)} %get-tuple-element.99), channel_id=1, source_target_pairs={{4,0},{8,4},{12,8},{16,12},{20,16},{24,20},{28,24},{32,28},{36,32}... | collective-permute-start | bytes 2949128 | tf_op jit(solution)/shard_map/ppermute | solution.py:466
  221.6 5.8 %sketch_stage.4 = f32[8,8,32,256]{3,2,1,0:T(8,128)S(1)} custom-call(f32[8,8,32,256]{3,2,1,0:T(8,128)S(1)} %get-tuple-element.63.tiles, f32[8,120,256]{2,1,0:T(8,128)S(1)} %collective-permute-done.6.top, f32[8,120,256]{2,1,0:T(8,128)S(1)} %copy-done.17, bf16[256,1536]{1,0:T(8,128)(2,1)S(1)} %get-tuple-element.66.matrix, s32[32,8,32,256]{3,2,1,0:T(8,128)} %signs.23, ...), custom_call_target="tpu_custom_call" | custom-call | flops 1610612736 | bytes 8388608 | tf_op jit(solution)/shard_map/sketch_stage/pallas_call | solution.py:270
  227.4 6.2 %sketch_stage.5 = f32[8,8,32,256]{3,2,1,0:T(8,128)S(1)} custom-call(f32[8,8,32,256]{3,2,1,0:T(8,128)S(1)} %get-tuple-element.75.tiles, f32[8,120,256]{2,1,0:T(8,128)} %collective-permute-done.14.top, f32[8,120,256]{2,1,0:T(8,128)S(1)} %collective-permute-done.15.bottom, bf16[256,1536]{1,0:T(8,128)(2,1)S(1)} %get-tuple-element.66.matrix, ...), custom_call_target="tpu_custom_call" | custom-call | flops 1610612736 | bytes 8388608 | tf_op jit(solution)/shard_map/sketch_stage/pallas_call | solution.py:270
  235.8 6.2 %sketch_stage.6 = f32[8,8,32,256]{3,2,1,0:T(8,128)S(1)} custom-call(f32[8,8,32,256]{3,2,1,0:T(8,128)S(1)} %get-tuple-element.86.tiles, f32[8,120,256]{2,1,0:T(8,128)S(1)} %copy-done.19, f32[8,120,256]{2,1,0:T(8,128)} %collective-permute-done.23.bottom, bf16[256,1536]{1,0:T(8,128)(2,1)S(1)} %get-tuple-element.66.matrix, s32[32,8,32,256]{3,2,1,0:T(8,128)} %signs.23, ...), custom_call_target="tpu_custom_call" | custom-call | flops 1610612736 | bytes 8388608 | tf_op jit(solution)/shard_map/sketch_stage/pallas_call | solution.py:270
  242.1 5.8 %sketch_stage.7 = f32[8,8,32,256]{3,2,1,0:T(8,128)S(1)} custom-call(f32[8,8,32,256]{3,2,1,0:T(8,128)S(1)} %copy-done.9, f32[8,120,256]{2,1,0:T(8,128)S(1)} %collective-permute-done.30.top, f32[8,120,256]{2,1,0:T(8,128)S(1)} %collective-permute-done.31.bottom, bf16[256,1536]{1,0:T(8,128)(2,1)S(1)} %get-tuple-element.66.matrix, s32[32,8,32,256]{3,2,1,0:T(8,128)} %signs.23, ...), custom_call_target="tpu_custom_call" | custom-call | flops 1610612736 | bytes 8388608 | tf_op jit(solution)/shard_map/sketch_stage/pallas_call | solution.py:270
  247.9 11.9 %gram_stage.1.mine = f32[2,32,32]{2,1,0:T(8,128)S(1)} custom-call(f32[8,32,8,256]{3,2,1,0:T(8,128)S(1)} %bitcast.7, f32[8,32,8,256]{3,2,1,0:T(8,128)S(1)} %bitcast.9, f32[8,32,8,256]{3,2,1,0:T(8,128)S(1)} %bitcast.11, f32[8,32,8,256]{3,2,1,0:T(8,128)S(1)} %bitcast.13), custom_call_target="tpu_custom_call" | custom-call | flops 4294967296 | bytes 8388608 | tf_op jit(solution)/shard_map/gram_stage/pallas_call | solution.py:326
  261.2 3.9 %collective-permute-done.33.other = f32[2,32,32]{2,1,0:T(8,128)S(1)} collective-permute-done((f32[2,32,32]{2,1,0:T(8,128)S(1)}, f32[2,32,32]{2,1,0:T(8,128)S(1)}, u32[]{:S(2)}, u32[]{:S(2)}) %collective-permute-start.33) | collective-permute-done | bytes 8224 | tf_op jit(solution)/shard_map/ppermute | solution.py:389
  265.2 5.4 %collective-permute-done.34.other = f32[2,32,32]{2,1,0:T(8,128)S(1)} collective-permute-done((f32[2,32,32]{2,1,0:T(8,128)S(1)}, f32[2,32,32]{2,1,0:T(8,128)S(1)}, u32[]{:S(2)}, u32[]{:S(2)}) %collective-permute-start.34) | collective-permute-done | bytes 8224 | tf_op jit(solution)/shard_map/ppermute | solution.py:389
  271.5 3.2 %collective-permute-done.35.other = f32[2,32,32]{2,1,0:T(8,128)S(1)} collective-permute-done((f32[2,32,32]{2,1,0:T(8,128)S(1)}, f32[2,32,32]{2,1,0:T(8,128)S(1)}, u32[]{:S(2)}, u32[]{:S(2)}) %collective-permute-start.35) | collective-permute-done | bytes 8224 | tf_op jit(solution)/shard_map/ppermute | solution.py:389
  276.0 4.2 %collective-permute-done.36.other = f32[2,32,32]{2,1,0:T(8,128)S(1)} collective-permute-done((f32[2,32,32]{2,1,0:T(8,128)S(1)}, f32[2,32,32]{2,1,0:T(8,128)S(1)}, u32[]{:S(2)}, u32[]{:S(2)}) %collective-permute-start.36) | collective-permute-done | bytes 8224 | tf_op jit(solution)/shard_map/ppermute | solution.py:389
  280.8 3.4 %collective-permute-done.37.other = f32[2,32,32]{2,1,0:T(8,128)S(1)} collective-permute-done((f32[2,32,32]{2,1,0:T(8,128)S(1)}, f32[2,32,32]{2,1,0:T(8,128)S(1)}, u32[]{:S(2)}, u32[]{:S(2)}) %collective-permute-start.37) | collective-permute-done | bytes 8224 | tf_op jit(solution)/shard_map/ppermute | solution.py:389
  284.6 5.1 %collective-permute-done.38.other = f32[2,32,32]{2,1,0:T(8,128)S(1)} collective-permute-done((f32[2,32,32]{2,1,0:T(8,128)S(1)}, f32[2,32,32]{2,1,0:T(8,128)S(1)}, u32[]{:S(2)}, u32[]{:S(2)}) %collective-permute-start.38) | collective-permute-done | bytes 8224 | tf_op jit(solution)/shard_map/ppermute | solution.py:389
  289.7 4.6 %factor_stage.1 = (f32[32,32]{1,0:T(8,128)}, f32[32,32]{1,0:T(8,128)S(1)}) custom-call(f32[2,32,32]{2,1,0:T(8,128)S(1)} %merge.13.refs_0_), custom_call_target="tpu_custom_call" | custom-call | tf_op jit(solution)/shard_map/factor_stage/pallas_call | solution.py:422
  294.3 11.2 %basis_stage.1 = f32[32,32,8,256]{3,2,1,0:T(8,128)} custom-call(f32[32,32]{1,0:T(8,128)S(1)} %get-tuple-element.100.inverse, f32[8,32,8,256]{3,2,1,0:T(8,128)S(1)} %bitcast.8, f32[8,32,8,256]{3,2,1,0:T(8,128)S(1)} %bitcast.10, f32[8,32,8,256]{3,2,1,0:T(8,128)S(1)} %bitcast.12, f32[8,32,8,256]{3,2,1,0:T(8,128)S(1)} %bitcast.14), custom_call_target="tpu_custom_call" | custom-call | flops 3221225472 | bytes 16777216 | tf_op jit(solution)/shard_map/basis_stage/pallas_call | solution.py:451
  (152 shorter events, 58.6 us)
Async XLA Ops:
  6.6 21.3 %collective-permute-start.24 = (f32[8,120,256]{2,1,0:T(8,128)S(1)}, f32[8,120,256]{2,1,0:T(8,128)S(1)}, u32[]{:S(2)}, u32[]{:S(2)}) collective-permute-start(f32[8,120,256]{2,1,0:T(8,128)S(1)} %get-tuple-element.89), channel_id=1, source_target_pairs={{0,4},{4,8},{8,12},{12,16},{16,20},{20,24},{24,28},{28,32},{32,36}... | collective-permute-start | bytes 2949128 | tf_op jit(solution)/shard_map/ppermute | solution.py:466
  8.6 27.5 %collective-permute-start.25 = (f32[8,120,256]{2,1,0:T(8,128)}, f32[8,120,256]{2,1,0:T(8,128)S(1)}, u32[]{:S(2)}, u32[]{:S(2)}) collective-permute-start(f32[8,120,256]{2,1,0:T(8,128)} %get-tuple-element.90), channel_id=1, source_target_pairs={{4,0},{8,4},{12,8},{16,12},{20,16},{24,20},{28,24},{32,28},{36,32}... | collective-permute-start | bytes 2949128 | tf_op jit(solution)/shard_map/ppermute | solution.py:466
  16.3 22.8 %collective-permute-start.16 = (f32[8,120,256]{2,1,0:T(8,128)}, f32[8,120,256]{2,1,0:T(8,128)S(1)}, u32[]{:S(2)}, u32[]{:S(2)}) collective-permute-start(f32[8,120,256]{2,1,0:T(8,128)} %get-tuple-element.78), channel_id=1, source_target_pairs={{0,4},{4,8},{8,12},{12,16},{16,20},{20,24},{24,28},{28,32},{32,36}... | collective-permute-start | bytes 2949128 | tf_op jit(solution)/shard_map/ppermute | solution.py:466
  18.2 41.6 %collective-permute-start.17 = (f32[8,120,256]{2,1,0:T(8,128)}, f32[8,120,256]{2,1,0:T(8,128)}, u32[]{:S(2)}, u32[]{:S(2)}) collective-permute-start(f32[8,120,256]{2,1,0:T(8,128)} %get-tuple-element.79), channel_id=1, source_target_pairs={{4,0},{8,4},{12,8},{16,12},{20,16},{24,20},{28,24},{32,28},{36,32}... | collective-permute-start | bytes 2949128 | tf_op jit(solution)/shard_map/ppermute | solution.py:466
  23.9 28.4 %slice-start = ((s8[8388608]{0:T(1024)(128)(4,1)}), s8[4194304]{0:T(1024)(128)(4,1)S(1)}, s32[]{:S(2)}) async-start(s8[8388608]{0:T(1024)(128)(4,1)} %bitcast.5), calls=%async_computation | async-start | bytes 8388608
  25.9 45.7 %collective-permute-start = (f32[8,120,256]{2,1,0:T(8,128)}, f32[8,120,256]{2,1,0:T(8,128)S(1)}, u32[]{:S(2)}, u32[]{:S(2)}) collective-permute-start(f32[8,120,256]{2,1,0:T(8,128)} %get-tuple-element.52), channel_id=1, source_target_pairs={{0,4},{4,8},{8,12},{12,16},{16,20},{20,24},{24,28},{28,32},{32,36}... | collective-permute-start | bytes 2949128 | tf_op jit(solution)/shard_map/ppermute | solution.py:466
  28.0 17.9 %copy-start.23 = (f32[256,8]{1,0:T(8,128)S(1)}, f32[256,8]{1,0:T(8,128)}, u32[]{:S(2)}) copy-start(f32[256,8]{1,0:T(8,128)} %constant.25.clone.spread) | copy-start | bytes 24580
  28.0 17.9 %copy-start.24 = (f32[8,512]{1,0:T(8,128)S(1)}, f32[8,512]{1,0:T(8,128)}, u32[]{:S(2)}) copy-start(f32[8,512]{1,0:T(8,128)} %constant.24.clone.pick) | copy-start | bytes 49156
  28.0 17.9 %copy-start.25 = (f32[8,8]{1,0:T(8,128)S(1)}, f32[8,8]{1,0:T(8,128)}, u32[]{:S(2)}) copy-start(f32[8,8]{1,0:T(8,128)} %factor.1) | copy-start | bytes 772
  28.0 17.9 %copy-start.26 = (f32[8,8]{1,0:T(8,128)S(1)}, f32[8,8]{1,0:T(8,128)}, u32[]{:S(2)}) copy-start(f32[8,8]{1,0:T(8,128)} %mix.1) | copy-start | bytes 772
  28.0 24.3 %slice-start.1 = ((s8[8388608]{0:T(1024)(128)(4,1)}), s8[4194304]{0:T(1024)(128)(4,1)S(1)}, s32[]{:S(2)}) async-start(s8[8388608]{0:T(1024)(128)(4,1)} %bitcast.5), calls=%async_computation.1 | async-start | bytes 8388608
  28.0 45.6 %collective-permute-start.1 = (f32[8,120,256]{2,1,0:T(8,128)}, f32[8,120,256]{2,1,0:T(8,128)S(1)}, u32[]{:S(2)}, u32[]{:S(2)}) collective-permute-start(f32[8,120,256]{2,1,0:T(8,128)} %get-tuple-element.53), channel_id=1, source_target_pairs={{4,0},{8,4},{12,8},{16,12},{20,16},{24,20},{28,24},{32,28},{36,32}... | collective-permute-start | bytes 2949128 | tf_op jit(solution)/shard_map/ppermute | solution.py:466
  37.0 15.4 %copy-start.13 = (f32[8,120,256]{2,1,0:T(8,128)S(1)}, f32[8,120,256]{2,1,0:T(8,128)}, u32[]{:S(2)}) copy-start(f32[8,120,256]{2,1,0:T(8,128)} %copy-done.12) | copy-start | bytes 2949124
  37.0 45.5 %collective-permute-start.8 = (f32[8,120,256]{2,1,0:T(8,128)}, f32[8,120,256]{2,1,0:T(8,128)S(1)}, u32[]{:S(2)}, u32[]{:S(2)}) collective-permute-start(f32[8,120,256]{2,1,0:T(8,128)} %get-tuple-element.67), channel_id=1, source_target_pairs={{0,4},{4,8},{8,12},{12,16},{16,20},{20,24},{24,28},{28,32},{32,36}... | collective-permute-start | bytes 2949128 | tf_op jit(solution)/shard_map/ppermute | solution.py:466
  40.1 46.6 %collective-permute-start.9 = (f32[8,120,256]{2,1,0:T(8,128)}, f32[8,120,256]{2,1,0:T(8,128)S(1)}, u32[]{:S(2)}, u32[]{:S(2)}) collective-permute-start(f32[8,120,256]{2,1,0:T(8,128)} %get-tuple-element.68), channel_id=1, source_target_pairs={{4,0},{8,4},{12,8},{16,12},{20,16},{24,20},{28,24},{32,28},{36,32}... | collective-permute-start | bytes 2949128 | tf_op jit(solution)/shard_map/ppermute | solution.py:466
  59.8 84.4 %collective-permute-start.26 = (f32[8,32,128]{2,1,0:T(8,128)}, f32[8,32,128]{2,1,0:T(8,128)S(1)}, u32[]{:S(2)}, u32[]{:S(2)}) collective-permute-start(f32[8,32,128]{2,1,0:T(8,128)} %get-tuple-element.92), channel_id=1, source_target_pairs={{0,1},{1,2},{2,3},{4,5},{5,6},{6,7},{8,9},{9,10},{10,11},{12,13},{... | collective-permute-start | bytes 393224 | tf_op jit(solution)/shard_map/ppermute | solution.py:466
  71.6 79.0 %collective-permute-start.27 = (f32[8,32,128]{2,1,0:T(8,128)}, f32[8,32,128]{2,1,0:T(8,128)}, u32[]{:S(2)}, u32[]{:S(2)}) collective-permute-start(f32[8,32,128]{2,1,0:T(8,128)} %get-tuple-element.93), channel_id=1, source_target_pairs={{1,0},{2,1},{3,2},{5,4},{6,5},{7,6},{9,8},{10,9},{11,10},{13,12},{... | collective-permute-start | bytes 393224 | tf_op jit(solution)/shard_map/ppermute | solution.py:466
  73.7 89.9 %collective-permute-start.18 = (f32[8,32,128]{2,1,0:T(8,128)}, f32[8,32,128]{2,1,0:T(8,128)}, u32[]{:S(2)}, u32[]{:S(2)}) collective-permute-start(f32[8,32,128]{2,1,0:T(8,128)} %get-tuple-element.81), channel_id=1, source_target_pairs={{0,1},{1,2},{2,3},{4,5},{5,6},{6,7},{8,9},{9,10},{10,11},{12,13},{... | collective-permute-start | bytes 393224 | tf_op jit(solution)/shard_map/ppermute | solution.py:466
  82.5 11.5 %collective-permute-start.2 = (f32[8,32,128]{2,1,0:T(8,128)S(1)}, f32[8,32,128]{2,1,0:T(8,128)S(1)}, u32[]{:S(2)}, u32[]{:S(2)}) collective-permute-start(f32[8,32,128]{2,1,0:T(8,128)S(1)} %get-tuple-element.56), channel_id=1, source_target_pairs={{0,1},{1,2},{2,3},{4,5},{5,6},{6,7},{8,9},{9,10},{10,11},{12,13},{... | collective-permute-start | bytes 393224 | tf_op jit(solution)/shard_map/ppermute | solution.py:466
  86.8 11.1 %collective-permute-start.3 = (f32[8,32,128]{2,1,0:T(8,128)S(1)}, f32[8,32,128]{2,1,0:T(8,128)S(1)}, u32[]{:S(2)}, u32[]{:S(2)}) collective-permute-start(f32[8,32,128]{2,1,0:T(8,128)S(1)} %get-tuple-element.57), channel_id=1, source_target_pairs={{1,0},{2,1},{3,2},{5,4},{6,5},{7,6},{9,8},{10,9},{11,10},{13,12},{... | collective-permute-start | bytes 393224 | tf_op jit(solution)/shard_map/ppermute | solution.py:466
  94.0 16.5 %collective-permute-start.10 = (f32[8,32,128]{2,1,0:T(8,128)S(1)}, f32[8,32,128]{2,1,0:T(8,128)S(1)}, u32[]{:S(2)}, u32[]{:S(2)}) collective-permute-start(f32[8,32,128]{2,1,0:T(8,128)S(1)} %get-tuple-element.70), channel_id=1, source_target_pairs={{0,1},{1,2},{2,3},{4,5},{5,6},{6,7},{8,9},{9,10},{10,11},{12,13},{... | collective-permute-start | bytes 393224 | tf_op jit(solution)/shard_map/ppermute | solution.py:466
  97.9 16.5 %collective-permute-start.11 = (f32[8,32,128]{2,1,0:T(8,128)S(1)}, f32[8,32,128]{2,1,0:T(8,128)S(1)}, u32[]{:S(2)}, u32[]{:S(2)}) collective-permute-start(f32[8,32,128]{2,1,0:T(8,128)S(1)} %get-tuple-element.71), channel_id=1, source_target_pairs={{1,0},{2,1},{3,2},{5,4},{6,5},{7,6},{9,8},{10,9},{11,10},{13,12},{... | collective-permute-start | bytes 393224 | tf_op jit(solution)/shard_map/ppermute | solution.py:466
  101.5 14.9 %copy-start.6 = (bf16[8,256,256]{2,1,0:T(8,128)(2,1)S(1)}, bf16[8,256,256]{2,1,0:T(8,128)(2,1)}, u32[]{:S(2)}) copy-start(bf16[8,256,256]{2,1,0:T(8,128)(2,1)} %constant.19.clone.main_l) | copy-start | bytes 3145732
  101.5 14.9 %copy-start.32 = (f32[8,8,32,256]{3,2,1,0:T(8,128)S(1)}, f32[8,8,32,256]{3,2,1,0:T(8,128)}, u32[]{:S(2)}) copy-start(f32[8,8,32,256]{3,2,1,0:T(8,128)} %copy-done.31) | copy-start | bytes 6291460
  110.5 14.9 %collective-permute-start.4 = (f32[8,32,128]{2,1,0:T(8,128)S(1)}, f32[8,32,128]{2,1,0:T(8,128)S(1)}, u32[]{:S(2)}, u32[]{:S(2)}) collective-permute-start(f32[8,32,128]{2,1,0:T(8,128)S(1)} %get-tuple-element.61), channel_id=1, source_target_pairs={{0,1},{1,2},{2,3},{4,5},{5,6},{6,7},{8,9},{9,10},{10,11},{12,13},{... | collective-permute-start | bytes 393224 | tf_op jit(solution)/shard_map/ppermute | solution.py:466
  114.4 14.9 %collective-permute-start.5 = (f32[8,32,128]{2,1,0:T(8,128)S(1)}, f32[8,32,128]{2,1,0:T(8,128)S(1)}, u32[]{:S(2)}, u32[]{:S(2)}) collective-permute-start(f32[8,32,128]{2,1,0:T(8,128)S(1)} %get-tuple-element.62), channel_id=1, source_target_pairs={{1,0},{2,1},{3,2},{5,4},{6,5},{7,6},{9,8},{10,9},{11,10},{13,12},{... | collective-permute-start | bytes 393224 | tf_op jit(solution)/shard_map/ppermute | solution.py:466
  125.4 10.4 %collective-permute-start.12 = (f32[8,32,128]{2,1,0:T(8,128)S(1)}, f32[8,32,128]{2,1,0:T(8,128)S(1)}, u32[]{:S(2)}, u32[]{:S(2)}) collective-permute-start(f32[8,32,128]{2,1,0:T(8,128)S(1)} %get-tuple-element.73), channel_id=1, source_target_pairs={{0,1},{1,2},{2,3},{4,5},{5,6},{6,7},{8,9},{9,10},{10,11},{12,13},{... | collective-permute-start | bytes 393224 | tf_op jit(solution)/shard_map/ppermute | solution.py:466
  129.3 8.4 %collective-permute-start.13 = (f32[8,32,128]{2,1,0:T(8,128)S(1)}, f32[8,32,128]{2,1,0:T(8,128)S(1)}, u32[]{:S(2)}, u32[]{:S(2)}) collective-permute-start(f32[8,32,128]{2,1,0:T(8,128)S(1)} %get-tuple-element.74), channel_id=1, source_target_pairs={{1,0},{2,1},{3,2},{5,4},{6,5},{7,6},{9,8},{10,9},{11,10},{13,12},{... | collective-permute-start | bytes 393224 | tf_op jit(solution)/shard_map/ppermute | solution.py:466
  135.8 31.7 %collective-permute-start.19 = (f32[8,32,128]{2,1,0:T(8,128)S(1)}, f32[8,32,128]{2,1,0:T(8,128)S(1)}, u32[]{:S(2)}, u32[]{:S(2)}) collective-permute-start(f32[8,32,128]{2,1,0:T(8,128)S(1)} %get-tuple-element.82), channel_id=1, source_target_pairs={{1,0},{2,1},{3,2},{5,4},{6,5},{7,6},{9,8},{10,9},{11,10},{13,12},{... | collective-permute-start | bytes 393224 | tf_op jit(solution)/shard_map/ppermute | solution.py:466
  137.7 62.1 %collective-permute-start.6 = (f32[8,120,256]{2,1,0:T(8,128)}, f32[8,120,256]{2,1,0:T(8,128)S(1)}, u32[]{:S(2)}, u32[]{:S(2)}) collective-permute-start(f32[8,120,256]{2,1,0:T(8,128)} %get-tuple-element.64), channel_id=1, source_target_pairs={{0,4},{4,8},{8,12},{12,16},{16,20},{20,24},{24,28},{28,32},{32,36}... | collective-permute-start | bytes 2949128 | tf_op jit(solution)/shard_map/ppermute | solution.py:466
  144.9 66.5 %collective-permute-start.7 = (f32[8,120,256]{2,1,0:T(8,128)}, f32[8,120,256]{2,1,0:T(8,128)S(1)}, u32[]{:S(2)}, u32[]{:S(2)}) collective-permute-start(f32[8,120,256]{2,1,0:T(8,128)} %get-tuple-element.65), channel_id=1, source_target_pairs={{4,0},{8,4},{12,8},{16,12},{20,16},{24,20},{28,24},{32,28},{36,32}... | collective-permute-start | bytes 2949128 | tf_op jit(solution)/shard_map/ppermute | solution.py:466
  150.6 63.8 %collective-permute-start.14 = (f32[8,120,256]{2,1,0:T(8,128)}, f32[8,120,256]{2,1,0:T(8,128)}, u32[]{:S(2)}, u32[]{:S(2)}) collective-permute-start(f32[8,120,256]{2,1,0:T(8,128)} %get-tuple-element.76), channel_id=1, source_target_pairs={{0,4},{4,8},{8,12},{12,16},{16,20},{20,24},{24,28},{28,32},{32,36}... | collective-permute-start | bytes 2949128 | tf_op jit(solution)/shard_map/ppermute | solution.py:466
  163.5 17.7 %collective-permute-start.28 = (f32[8,32,128]{2,1,0:T(8,128)S(1)}, f32[8,32,128]{2,1,0:T(8,128)S(1)}, u32[]{:S(2)}, u32[]{:S(2)}) collective-permute-start(f32[8,32,128]{2,1,0:T(8,128)S(1)} %get-tuple-element.95), channel_id=1, source_target_pairs={{0,1},{1,2},{2,3},{4,5},{5,6},{6,7},{8,9},{9,10},{10,11},{12,13},{... | collective-permute-start | bytes 393224 | tf_op jit(solution)/shard_map/ppermute | solution.py:466
  177.4 6.9 %collective-permute-start.20 = (f32[8,32,128]{2,1,0:T(8,128)S(1)}, f32[8,32,128]{2,1,0:T(8,128)S(1)}, u32[]{:S(2)}, u32[]{:S(2)}) collective-permute-start(f32[8,32,128]{2,1,0:T(8,128)S(1)} %get-tuple-element.84), channel_id=1, source_target_pairs={{0,1},{1,2},{2,3},{4,5},{5,6},{6,7},{8,9},{9,10},{10,11},{12,13},{... | collective-permute-start | bytes 393224 | tf_op jit(solution)/shard_map/ppermute | solution.py:466
  181.3 6.9 %collective-permute-start.21 = (f32[8,32,128]{2,1,0:T(8,128)S(1)}, f32[8,32,128]{2,1,0:T(8,128)S(1)}, u32[]{:S(2)}, u32[]{:S(2)}) collective-permute-start(f32[8,32,128]{2,1,0:T(8,128)S(1)} %get-tuple-element.85), channel_id=1, source_target_pairs={{1,0},{2,1},{3,2},{5,4},{6,5},{7,6},{9,8},{10,9},{11,10},{13,12},{... | collective-permute-start | bytes 393224 | tf_op jit(solution)/shard_map/ppermute | solution.py:466
  184.2 13.7 %collective-permute-start.29 = (f32[8,32,128]{2,1,0:T(8,128)S(1)}, f32[8,32,128]{2,1,0:T(8,128)S(1)}, u32[]{:S(2)}, u32[]{:S(2)}) collective-permute-start(f32[8,32,128]{2,1,0:T(8,128)S(1)} %get-tuple-element.96), channel_id=1, source_target_pairs={{1,0},{2,1},{3,2},{5,4},{6,5},{7,6},{9,8},{10,9},{11,10},{13,12},{... | collective-permute-start | bytes 393224 | tf_op jit(solution)/shard_map/ppermute | solution.py:466
  188.1 39.2 %collective-permute-start.15 = (f32[8,120,256]{2,1,0:T(8,128)}, f32[8,120,256]{2,1,0:T(8,128)S(1)}, u32[]{:S(2)}, u32[]{:S(2)}) collective-permute-start(f32[8,120,256]{2,1,0:T(8,128)} %get-tuple-element.77), channel_id=1, source_target_pairs={{4,0},{8,4},{12,8},{16,12},{20,16},{24,20},{28,24},{32,28},{36,32}... | collective-permute-start | bytes 2949128 | tf_op jit(solution)/shard_map/ppermute | solution.py:466
  197.9 35.7 %collective-permute-start.22 = (f32[8,120,256]{2,1,0:T(8,128)}, f32[8,120,256]{2,1,0:T(8,128)S(1)}, u32[]{:S(2)}, u32[]{:S(2)}) collective-permute-start(f32[8,120,256]{2,1,0:T(8,128)} %get-tuple-element.87), channel_id=1, source_target_pairs={{0,4},{4,8},{8,12},{12,16},{16,20},{20,24},{24,28},{28,32},{32,36}... | collective-permute-start | bytes 2949128 | tf_op jit(solution)/shard_map/ppermute | solution.py:466
  199.8 34.8 %collective-permute-start.23 = (f32[8,120,256]{2,1,0:T(8,128)}, f32[8,120,256]{2,1,0:T(8,128)}, u32[]{:S(2)}, u32[]{:S(2)}) collective-permute-start(f32[8,120,256]{2,1,0:T(8,128)} %get-tuple-element.88), channel_id=1, source_target_pairs={{4,0},{8,4},{12,8},{16,12},{20,16},{24,20},{28,24},{32,28},{36,32}... | collective-permute-start | bytes 2949128 | tf_op jit(solution)/shard_map/ppermute | solution.py:466
  212.5 29.6 %collective-permute-start.30 = (f32[8,120,256]{2,1,0:T(8,128)}, f32[8,120,256]{2,1,0:T(8,128)S(1)}, u32[]{:S(2)}, u32[]{:S(2)}) collective-permute-start(f32[8,120,256]{2,1,0:T(8,128)} %get-tuple-element.98), channel_id=1, source_target_pairs={{0,4},{4,8},{8,12},{12,16},{16,20},{20,24},{24,28},{28,32},{32,36}... | collective-permute-start | bytes 2949128 | tf_op jit(solution)/shard_map/ppermute | solution.py:466
  214.4 27.7 %collective-permute-start.31 = (f32[8,120,256]{2,1,0:T(8,128)}, f32[8,120,256]{2,1,0:T(8,128)S(1)}, u32[]{:S(2)}, u32[]{:S(2)}) collective-permute-start(f32[8,120,256]{2,1,0:T(8,128)} %get-tuple-element.99), channel_id=1, source_target_pairs={{4,0},{8,4},{12,8},{16,12},{20,16},{24,20},{28,24},{32,28},{36,32}... | collective-permute-start | bytes 2949128 | tf_op jit(solution)/shard_map/ppermute | solution.py:466
  259.8 1.3 collective-permute-start.32
  261.1 4.0 %collective-permute-start.33 = (f32[2,32,32]{2,1,0:T(8,128)S(1)}, f32[2,32,32]{2,1,0:T(8,128)S(1)}, u32[]{:S(2)}, u32[]{:S(2)}) collective-permute-start(f32[2,32,32]{2,1,0:T(8,128)S(1)} %merge.7.mine), channel_id=1, source_target_pairs={{0,8},{4,12},{8,0},{12,4},{16,24},{20,28},{24,16},{28,20},{32,40},... | collective-permute-start | bytes 24584 | tf_op jit(solution)/shard_map/ppermute | solution.py:389
  265.1 5.5 %collective-permute-start.34 = (f32[2,32,32]{2,1,0:T(8,128)S(1)}, f32[2,32,32]{2,1,0:T(8,128)S(1)}, u32[]{:S(2)}, u32[]{:S(2)}) collective-permute-start(f32[2,32,32]{2,1,0:T(8,128)S(1)} %merge.8.mine), channel_id=1, source_target_pairs={{0,16},{4,20},{8,24},{12,28},{16,0},{20,4},{24,8},{28,12},{32,48},... | collective-permute-start | bytes 24584 | tf_op jit(solution)/shard_map/ppermute | solution.py:389
  270.7 4.0 %collective-permute-start.35 = (f32[2,32,32]{2,1,0:T(8,128)S(1)}, f32[2,32,32]{2,1,0:T(8,128)S(1)}, u32[]{:S(2)}, u32[]{:S(2)}) collective-permute-start(f32[2,32,32]{2,1,0:T(8,128)S(1)} %merge.9.mine), channel_id=1, source_target_pairs={{0,32},{4,36},{8,40},{12,44},{16,48},{20,52},{24,56},{28,60},{32,0... | collective-permute-start | bytes 24584 | tf_op jit(solution)/shard_map/ppermute | solution.py:389
  274.7 5.5 %collective-permute-start.36 = (f32[2,32,32]{2,1,0:T(8,128)S(1)}, f32[2,32,32]{2,1,0:T(8,128)S(1)}, u32[]{:S(2)}, u32[]{:S(2)}) collective-permute-start(f32[2,32,32]{2,1,0:T(8,128)S(1)} %merge.10.mine), channel_id=1, source_target_pairs={{0,64},{4,68},{8,72},{12,76},{16,80},{20,84},{24,88},{28,92},{32,9... | collective-permute-start | bytes 24584 | tf_op jit(solution)/shard_map/ppermute | solution.py:389
  280.2 4.0 %collective-permute-start.37 = (f32[2,32,32]{2,1,0:T(8,128)S(1)}, f32[2,32,32]{2,1,0:T(8,128)S(1)}, u32[]{:S(2)}, u32[]{:S(2)}) collective-permute-start(f32[2,32,32]{2,1,0:T(8,128)S(1)} %merge.11.mine), channel_id=1, source_target_pairs={{0,1},{1,0},{2,3},{3,2},{4,5},{5,4},{6,7},{7,6},{8,9},{9,8},{10,11... | collective-permute-start | bytes 24584 | tf_op jit(solution)/shard_map/ppermute | solution.py:389
  284.2 5.5 %collective-permute-start.38 = (f32[2,32,32]{2,1,0:T(8,128)S(1)}, f32[2,32,32]{2,1,0:T(8,128)S(1)}, u32[]{:S(2)}, u32[]{:S(2)}) collective-permute-start(f32[2,32,32]{2,1,0:T(8,128)S(1)} %merge.12.mine), channel_id=1, source_target_pairs={{0,2},{1,3},{2,0},{3,1},{4,6},{5,7},{6,4},{7,5},{8,10},{9,11},{10,... | collective-permute-start | bytes 24584 | tf_op jit(solution)/shard_map/ppermute | solution.py:389
  (36 other events, 202.7 us)
where the time goes:
time: 308 us; the launch traced here: 306 us
  Pallas kernels  137 us (44%)
  starting transfers between devices  112 us (36%)
  waiting for transfers between devices  29.4 us (10%)
  local copies, waits for them, and re-layouts  25.7 us (8%)
    ppermute x16, starting transfers between devices, both_ways(): lax.ppermute(to_previous, axis, backward)  61.6 us
    ppermute x16, starting transfers between devices, both_ways(): lax.ppermute(to_next, axis, forward)  46.9 us
    pallas_call x4, Pallas kernels, middle_stage(): pl.pallas_call(middle_kernel, out_shape=(whole, packed, packed), in_specs...  37.8 us
    ppermute x7, waiting for transfers between devices, sum_over(): lax.ppermute(value, axis, [(i, i ^ bit) for i in range(count)])  26.4 us
    unnamed x90, local copies, waits for them, and re-layouts  25.7 us
    pallas_call x4, Pallas kernels, sketch_stage(): pl.pallas_call(sketch_kernel, grid=(count,), out_shape=jax.ShapeDtypeStru...  24.1 us
    pallas_call x4, Pallas kernels, first_stage(): pl.pallas_call(first_kernel, grid=(count,), out_shape=(jax.ShapeDtypeStru...  18.8 us
    pallas_call x4, Pallas kernels, last_column_stage(): pl.pallas_call(last_column_kernel, out_shape=(whole, edge, edge), in_spec...  18.2 us
  transfers between devices with their start and end apart: 39, of which 9 were waited for; matrix products, arithmetic and copies ran while one was open for 0% of the time, Pallas kernels for 33%

commit v1 on v0

v1 whole, which is shorter than its diff:
```python
import numpy as np
import jax
import jax.numpy as jnp
from jax import lax
from jax.experimental import pallas as pl
from jax.experimental.pallas import tpu as pltpu
from jax.sharding import PartitionSpec as P

BANDS = 8
HALF = 15
TAPS = 31
ROWS = 32
COLS = 256
CHUNKS = (8, 12, 12)
PER = 4

F32 = jnp.float32
BF16 = jnp.bfloat16
HI = lax.Precision.HIGHEST
VMEM = pl.BlockSpec(memory_space=pltpu.VMEM)
SMEM = pl.BlockSpec(memory_space=pltpu.SMEM)
SIDE = jax.ShapeDtypeStruct((2,), jnp.int32)


def taps_np():
    offsets = np.arange(TAPS) - HALF
    sigma = 1.0 + 0.5 * np.arange(BANDS)
    raw = np.exp(-offsets[None, :] ** 2 / (2.0 * sigma[:, None] ** 2))
    return raw / raw.sum(axis=1, keepdims=True)


def table_np(pos_in, pos_out):
    taps = taps_np()
    offset = np.asarray(pos_in)[:, None] - np.asarray(pos_out)[None, :]
    inside = np.abs(offset) <= HALF
    return np.where(inside[None], taps[:, np.clip(offset + HALF, 0, TAPS - 1)], 0.0)


def split_np(values):
    high = values.astype(BF16)
    low = (values - high.astype(np.float64)).astype(BF16)
    return high, low


def row_constants():
    out = np.arange(ROWS)
    main = table_np(np.arange(ROWS), out)
    above = table_np(np.arange(-HALF, 0), out)
    below = table_np(np.arange(ROWS, ROWS + HALF), out)
    by_out = np.zeros((BANDS, ROWS, 512))
    by_in = np.zeros((BANDS, ROWS, 512))
    pick = np.zeros((BANDS, 512))
    for c in range(BANDS):
        parts = ((c * ROWS, ROWS, main), (256 + c * HALF, HALF, above), (376 + c * HALF, HALF, below))
        for start, size, table in parts:
            by_out[:, :, start:start + size] = table.transpose(0, 2, 1)
            by_in[:, :, start:start + size] = table[c].T[None]
            pick[c, start:start + size] = 1.0
    spread = np.repeat(np.eye(BANDS), ROWS, axis=0)
    same = np.tile(np.eye(ROWS), (BANDS, BANDS))
    return [v.astype(np.float32) for v in (by_out.reshape(256, 512), by_in.reshape(256, 512), pick, spread, same)]


def col_constants():
    out = np.arange(COLS)
    main = table_np(np.arange(COLS), out)
    left = table_np(np.arange(-16, 0), out)
    right = table_np(np.arange(COLS, COLS + 16), out)
    main_h, main_l = split_np(main)
    halo_h, halo_l = split_np(np.concatenate([left, right], axis=1))
    halo = np.zeros((BANDS, 256, COLS), BF16)
    halo[:, 0:32] = halo_h
    halo[:, 32:64] = halo_l
    halo[:, 128:160] = halo_h
    return np.concatenate([main_h, main_h, main_l, halo], axis=1)


def split(values):
    high = values.astype(BF16)
    return high, (values - high.astype(F32)).astype(BF16)


def dot(a, b, precision=None):
    return lax.dot_general(a, b, (((1,), (0,)), ((), ())), precision=precision, preferred_element_type=F32)


def dot_nt(a, b):
    return lax.dot_general(a, b, (((1,), (1,)), ((), ())), preferred_element_type=F32)


def stacked(values):
    high, low = split(values)
    return jnp.concatenate([high, high, low], axis=0)


def hand_on(side, after):
    after[0] = side[0]
    after[1] = side[1]


def params(mib=24):
    return pltpu.CompilerParams(vmem_limit_bytes=mib * 2**20)


def cost(flops, moved):
    return pl.CostEstimate(flops=int(flops), bytes_accessed=int(moved), transcendentals=0)


def prepare_kernel(side, factor, mix, by_out, by_in, pick, spread, same, first_m, last_m, mix_m, back_m):
    lower = side[0] == 0
    def expand(small, right):
        return dot(dot(spread[...], small, HI), right, HI)

    def store(out, whole):
        for part in range(whole.shape[1] // 256):
            high, low = split(whole[:, part * 256:part * 256 + 256])
            out[:, part * 768:part * 768 + 256] = high
            out[:, part * 768 + 256:part * 768 + 512] = low
            out[:, part * 768 + 512:part * 768 + 768] = high

    f = factor[...]
    a = mix[...]

    def ordered(table):
        whole = table[...]
        above, below, rest = whole[:, 256:376], whole[:, 376:496], whole[:, 496:512]
        swapped = jnp.concatenate([whole[:, 0:256], below, above, rest], axis=1)
        return jnp.where(lower, whole, swapped)

    store(first_m, expand(f, pick[...]) * ordered(by_out))
    store(last_m, expand(f.T, pick[...]) * ordered(by_in))
    store(mix_m, expand(a, pick[:, :256]) * same[...])
    store(back_m, expand(a.T, pick[:, :256]) * same[...])


def prepare(side, factor, mix):
    wide = jax.ShapeDtypeStruct((256, 1536), BF16)
    narrow = jax.ShapeDtypeStruct((256, 768), BF16)
    return pl.pallas_call(
        prepare_kernel, out_shape=(wide, wide, narrow, narrow),
        in_specs=[SMEM] + [VMEM] * 7, out_specs=(VMEM,) * 4, compiler_params=params(),
        name="prepare",
    )(side, factor, mix, *[jnp.asarray(v) for v in row_constants()])


def signed(ref_value):
    return 2.0 * ref_value.astype(F32) - 1.0


def store_edges(tile, top, bottom, p):
    for b in range(BANDS):
        top[p, b * HALF:(b + 1) * HALF, :] = tile[b, 0:HALF, :]
        bottom[p, b * HALF:(b + 1) * HALF, :] = tile[b, ROWS - HALF:ROWS, :]


def store_by_side(tile, lower, inner, outer, p):
    @pl.when(lower)
    def _():
        store_edges(tile, outer, inner, p)

    @pl.when(jnp.logical_not(lower))
    def _():
        store_edges(tile, inner, outer, p)


def edge_kernel(side, signs, scale, inner, outer):
    for p in range(signs.shape[0]):
        store_by_side(scale[...] * signed(signs[p]), side[0] == 0, inner, outer, p)


def edges(side, signs, scale):
    count = signs.shape[0]
    shape = jax.ShapeDtypeStruct((count, BANDS * HALF, COLS), F32)
    return pl.pallas_call(
        edge_kernel, grid=(count // PER,), out_shape=(shape, shape),
        in_specs=[
            SMEM,
            pl.BlockSpec((PER, BANDS, ROWS, COLS), lambda i: (i, 0, 0, 0)),
            pl.BlockSpec((BANDS, ROWS, COLS), lambda i: (0, 0, 0)),
        ],
        out_specs=[pl.BlockSpec((PER, BANDS * HALF, COLS), lambda i: (i, 0, 0))] * 2,
        compiler_params=params(), cost_estimate=cost(1e6, count * 2**19), name="edges",
    )(side, signs, scale)


def store_packed(tile, lower, near, far, p):
    lane = lax.broadcasted_iota(jnp.int32, (ROWS, 128), 1) // 16
    low = tile[0, :, :128]
    high = pltpu.roll(tile[0, :, 128:], 16, 1)
    for b in range(1, BANDS):
        low = jnp.where(lane == b, pltpu.roll(tile[b, :, :128], 16 * b, 1), low)
        mine = tile[b, :, 128:]
        if b < BANDS - 1:
            mine = pltpu.roll(mine, 16 * b + 16, 1)
        high = jnp.where(lane == b, mine, high)
    near[p] = jnp.where(lower, high, low)
    far[p] = jnp.where(lower, low, high)


def halo_rows(outer, inner, p):
    return jnp.concatenate([outer[p], inner[p], jnp.zeros((16, COLS), F32)], axis=0)


def first_kernel(side, signs, scale, inner, outer, matrix, out, near, far, after):
    hand_on(side, after)

    @pl.loop(0, out.shape[0], step=PER)
    def _(start):
        for p in range(PER):
            scaled = (scale[...] * signed(signs[start + p])).reshape(256, COLS)
            whole = jnp.concatenate([stacked(scaled), stacked(halo_rows(outer, inner, start + p))], axis=0)
            tile = dot(matrix[...], whole).reshape(BANDS, ROWS, COLS)
            out[start + p] = tile
            store_packed(tile, side[1] == 0, near, far, start + p)


def first_stage(side, signs, scale, inner, outer, matrix):
    count = signs.shape[0]
    packed = jax.ShapeDtypeStruct((count, ROWS, 128), F32)
    return pl.pallas_call(
        first_kernel,
        out_shape=(jax.ShapeDtypeStruct((count, BANDS, ROWS, COLS), F32), packed, packed, SIDE),
        in_specs=[SMEM] + [VMEM] * 5, out_specs=(VMEM, VMEM, VMEM, SMEM),
        compiler_params=params(), cost_estimate=cost(count * 2 * 256 * 1536 * 256, count * 2**20),
        name="first_stage",
    )(side, signs, scale, inner, outer, matrix)


def column_blur(lower, tiles, near, far, table, out):
    count = tiles.shape[0]
    flat = count * ROWS
    first = near[...].reshape(flat, 128)
    other = far[...].reshape(flat, 128)
    left = jnp.where(lower, other, first)
    right = jnp.where(lower, first, other)
    lane = lax.broadcasted_iota(jnp.int32, (flat, 128), 1)

    @pl.loop(0, BANDS, step=4)
    def _(start):
        for b in [start + j for j in range(4)]:
            uh, ul = split(tiles[:, b].reshape(flat, COLS))
            sides = jnp.where(lane < 16, pltpu.roll(left, 128 - 16 * b, 1), pltpu.roll(right, (144 - 16 * b) % 128, 1))
            sides = jnp.where(lane < 32, sides, pltpu.roll(sides, 32, 1))
            eh, el = split(sides)
            blurred = dot(jnp.concatenate([uh, ul, uh, eh, el], axis=1), table[b])
            out[:, b] = blurred.reshape(count, ROWS, COLS)


def middle_kernel(side, tiles, near, far, table, mix, back, weights, out, out_near, out_far, after, blurred):
    hand_on(side, after)
    lower = side[1] == 0
    column_blur(lower, tiles, near, far, table, blurred)
    weight = weights[...].reshape(256, COLS)

    group = 6 if tiles.shape[0] % 6 == 0 else 8

    @pl.loop(0, tiles.shape[0], step=group)
    def _(start):
        for p in range(group):
            weighted = weight * dot(mix[...], stacked(blurred[start + p].reshape(256, COLS)))
            tile = dot(back[...], stacked(weighted)).reshape(BANDS, ROWS, COLS)
            out[start + p] = tile
            store_packed(tile, lower, out_near, out_far, start + p)


def middle_stage(side, tiles, near, far, table, mix, back, weights):
    count = tiles.shape[0]
    whole = jax.ShapeDtypeStruct((count, BANDS, ROWS, COLS), F32)
    packed = jax.ShapeDtypeStruct((count, ROWS, 128), F32)
    return pl.pallas_call(
        middle_kernel, out_shape=(whole, packed, packed, SIDE),
        in_specs=[SMEM] + [VMEM] * 7, out_specs=(VMEM, VMEM, VMEM, SMEM),
        scratch_shapes=[pltpu.VMEM((count, BANDS, ROWS, COLS), F32)],
        compiler_params=params(), cost_estimate=cost(count * 10 * 2 * 256**3, count * 2**20),
        name="middle_stage",
    )(side, tiles, near, far, table, mix, back, weights)


def last_column_kernel(side, tiles, near, far, table, out, inner, outer, after):
    hand_on(side, after)
    column_blur(side[1] == 0, tiles, near, far, table, out)

    @pl.when(side[0] == 0)
    def _():
        @pl.loop(0, tiles.shape[0], step=PER)
        def _(start):
            for p in range(PER):
                store_edges(out[start + p], outer, inner, start + p)

    @pl.when(side[0] != 0)
    def _():
        @pl.loop(0, tiles.shape[0], step=PER)
        def _(start):
            for p in range(PER):
                store_edges(out[start + p], inner, outer, start + p)


def last_column_stage(side, tiles, near, far, table):
    count = tiles.shape[0]
    whole = jax.ShapeDtypeStruct((count, BANDS, ROWS, COLS), F32)
    edge = jax.ShapeDtypeStruct((count, BANDS * HALF, COLS), F32)
    return pl.pallas_call(
        last_column_kernel, out_shape=(whole, edge, edge, SIDE),
        in_specs=[SMEM] + [VMEM] * 4, out_specs=(VMEM, VMEM, VMEM, SMEM),
        compiler_params=params(), cost_estimate=cost(count * 4 * 2 * 256**3, count * 2**20),
        name="last_column_stage",
    )(side, tiles, near, far, table)


def sketch_kernel(side, tiles, inner, outer, matrix, signs, scale, out, after):
    hand_on(side, after)

    @pl.loop(0, out.shape[0], step=PER)
    def _(start):
        for p in range(PER):
            spot = start + p
            whole = jnp.concatenate(
                [stacked(tiles[spot].reshape(256, COLS)), stacked(halo_rows(outer, inner, spot))], axis=0
            )
            mixed = dot(matrix[...], whole).reshape(BANDS, ROWS, COLS)
            out[spot] = scale[...] * mixed + signed(signs[spot])


def sketch_stage(side, tiles, inner, outer, matrix, signs, scale):
    count = tiles.shape[0]
    return pl.pallas_call(
        sketch_kernel, out_shape=(jax.ShapeDtypeStruct((count, BANDS, ROWS, COLS), F32), SIDE),
        in_specs=[SMEM] + [VMEM] * 6, out_specs=(VMEM, SMEM),
        compiler_params=params(), cost_estimate=cost(count * 2 * 256 * 1536 * 256, count * 2**20),
        name="sketch_stage",
    )(side, tiles, inner, outer, matrix, signs, scale)


def gather_group(refs, g):
    return jnp.concatenate([r[:, g].reshape(-1, COLS) for r in refs], axis=0)


def same_place(shape):
    return lax.broadcasted_iota(jnp.int32, shape, 0) % 8 == lax.broadcasted_iota(jnp.int32, shape, 1) % 8


def spread_ones(shape, long_dim):
    long = lax.broadcasted_iota(jnp.int32, shape, long_dim) // 8
    short = lax.broadcasted_iota(jnp.int32, shape, 1 - long_dim)
    return (long == short).astype(F32)


def gram_kernel(*refs):
    chunks, out, even, cross = refs[:-3], refs[-3], refs[-2], refs[-1]
    even[...] = jnp.zeros_like(even)
    cross[...] = jnp.zeros_like(cross)

    @pl.loop(0, chunks[0].shape[1], step=8)
    def _(g):
        values = jnp.concatenate([gather_group(chunks, g + j) for j in range(8)], axis=1)
        high, low = split(values)
        even[...] += dot_nt(high, high) + dot_nt(low, low)
        cross[...] += dot_nt(high, low)

    order = even.shape[0]
    keep = same_place((order, order))

    def collapse(table):
        kept = jnp.where(keep, table, 0.0)
        return dot(dot(spread_ones((order // 8, order), 1), kept, HI), spread_ones((order, order // 8), 0), HI)

    mixed = collapse(cross[...])
    total = collapse(even[...]) + (mixed + mixed.T)
    out[0] = jnp.concatenate([total[8 * j:8 * j + 8] for j in range(4)], axis=1)
    out[1] = jnp.zeros(out.shape[1:], F32)


def gram_stage(chunks):
    probes = sum(c.shape[0] for c in chunks)
    return pl.pallas_call(
        gram_kernel, out_shape=jax.ShapeDtypeStruct((2, 8, 128), F32),
        in_specs=[VMEM] * len(chunks), out_specs=VMEM,
        scratch_shapes=[pltpu.VMEM((256, 256), F32)] * 2,
        compiler_params=params(), cost_estimate=cost(32 * 4 * 2 * 256**3, 2**23), name="gram_stage",
    )(*chunks)


def group_blocks(chunks):
    return [pl.BlockSpec((c.shape[0], PER, 8, COLS), lambda i: (0, i, 0, 0)) for c in chunks]


def two_sum(a, b):
    total = a + b
    part = total - a
    return total, (a - (total - part)) + (b - part)


def quick_sum(a, b):
    total = a + b
    return total, b - (total - a)


def halves(a):
    wide = a * 4097.0
    high = wide - (wide - a)
    return high, a - high


def two_product(a, b):
    product = a * b
    ah, al = halves(a)
    bh, bl = halves(b)
    return product, ((ah * bh - product) + ah * bl + al * bh) + al * bl


def pair_add(a, b):
    total, error = two_sum(a[0], b[0])
    return quick_sum(total, error + (a[1] + b[1]))


def pair_mul(a, b):
    product, error = two_product(a[0], b[0])
    return quick_sum(product, error + (a[0] * b[1] + a[1] * b[0]))


def pair_neg(a):
    return -a[0], -a[1]


def merge_kernel(mine, other, out):
    total = pair_add((mine[0], mine[1]), (other[0], other[1]))
    out[0] = total[0]
    out[1] = total[1]


def merge(mine, other):
    return pl.pallas_call(
        merge_kernel, out_shape=jax.ShapeDtypeStruct(mine.shape, F32),
        in_specs=[VMEM] * 2, out_specs=VMEM, compiler_params=params(), name="merge",
    )(mine, other)


def sum_over(value, axis):
    count = lax.axis_size(axis)
    bit = 1
    while bit < count:
        value = merge(value, lax.ppermute(value, axis, [(i, i ^ bit) for i in range(count)]))
        bit *= 2
    return value


def factor_kernel(gram, factor, inverse, work, *, norm):
    order = factor.shape[0]
    work[...] = jnp.zeros_like(work)
    row = lax.broadcasted_iota(jnp.int32, (order, 128), 0)
    lane = lax.broadcasted_iota(jnp.int32, (order, 128), 1)
    work[0] = (lane == row + order).astype(F32)
    for j in range(4):
        work[:, 8 * j:8 * j + 8, 0:order] = gram[:, :, j * order:(j + 1) * order]
    now = (work[0], work[1])
    for k in range(order - 1):
        pivot_row = tuple(v[k:k + 1, :] for v in now)
        pivot = tuple(jnp.broadcast_to(v[:, k:k + 1], (1, 128)) for v in pivot_row)
        first = pivot_row[0] / pivot[0]
        rest = pair_add(pivot_row, pair_neg(pair_mul((first, jnp.zeros_like(first)), pivot)))
        ratio = quick_sum(first, rest[0] / pivot[0])
        column = tuple(
            jnp.where(row > k, jnp.broadcast_to(v[:, k:k + 1], (order, 128)), 0.0) for v in now
        )
        now = pair_add(now, pair_neg(pair_mul(column, ratio)))
    diagonal = jnp.sum(jnp.where(lane == row, now[0], 0.0), axis=1, keepdims=True)
    scaled = now[0] / jnp.sqrt(diagonal)
    factor[...] = jnp.where(lane >= row, scaled, 0.0)[:, 0:order] * (1.0 / norm)
    inverse[...] = scaled[:, order:2 * order] * norm


def factor_stage(gram, order, norm):
    square = jax.ShapeDtypeStruct((order, order), F32)
    return pl.pallas_call(
        lambda *refs: factor_kernel(*refs, norm=norm), out_shape=(square, square),
        in_specs=[VMEM], out_specs=(VMEM, VMEM), scratch_shapes=[pltpu.VMEM((2, order, 128), F32)],
        compiler_params=params(), name="factor_stage",
    )(gram)


def basis_kernel(inverse, *refs):
    chunks, out, matrix = refs[:-2], refs[-2], refs[-1]
    order = matrix.shape[0]

    @pl.when(pl.program_id(0) == 0)
    def _():
        wide = dot(dot(spread_ones((order, order // 8), 0), inverse[...], HI), spread_ones((order // 8, order), 1), HI)
        high, low = split(jnp.where(same_place((order, order)), wide, 0.0))
        matrix[:, 0:order] = high
        matrix[:, order:2 * order] = low
        matrix[:, 2 * order:3 * order] = high

    start = pl.program_id(0) * out.shape[1]
    for g in range(out.shape[1]):
        values = dot(matrix[...], stacked(gather_group(chunks, start + g)))
        out[:, g] = values.reshape(-1, 8, COLS)


def basis_stage(inverse, chunks):
    probes = inverse.shape[0]
    groups = chunks[0].shape[1]
    return pl.pallas_call(
        basis_kernel, grid=(groups // 8,),
        out_shape=jax.ShapeDtypeStruct((probes, groups, 8, COLS), F32),
        in_specs=[VMEM] * (1 + len(chunks)),
        out_specs=pl.BlockSpec((probes, 8, 8, COLS), lambda i: (0, i, 0, 0)),
        scratch_shapes=[pltpu.VMEM((256, 768), BF16)],
        compiler_params=params(), cost_estimate=cost(32 * 3 * 2 * 256**3, 2**24), name="basis_stage",
    )(inverse, *chunks)


def swap(inner, outer, axis):
    count = lax.axis_size(axis)
    pairs = [(i, i ^ 1) for i in range(count)]
    others = [p for i in range(1, count - 1, 2) for p in ((i, i + 1), (i + 1, i))]
    return lax.ppermute(inner, axis, pairs), lax.ppermute(outer, axis, others)


def shards(probe_signs, prior_scale, prior_factor, band_mix, inverse_noise_variance):
    probes = probe_signs.shape[0]
    side = jnp.stack([lax.axis_index("row") % 2, lax.axis_index("col") % 2]).astype(jnp.int32)
    table = jnp.asarray(col_constants())
    starts = [sum(CHUNKS[:k]) for k in range(len(CHUNKS))]
    signs = [probe_signs[start:start + count] for start, count in zip(starts, CHUNKS)]
    rows = [swap(*edges(side, part, prior_scale), "row") for part in signs]
    first_m, last_m, mix_m, back_m = prepare(side, prior_factor, band_mix)
    last = len(CHUNKS) - 1
    state = {}

    def first(k, side):
        *state[k], side = first_stage(side, signs[k], prior_scale, *rows[k], first_m)
        state[k][1:] = swap(*state[k][1:], "col")
        return side

    def middle(k, side):
        *state[k], side = middle_stage(side, *state[k], table, mix_m, back_m, inverse_noise_variance)
        state[k][1:] = swap(*state[k][1:], "col")
        return side

    def last_column(k, side):
        *state[k], side = last_column_stage(side, *state[k], table)
        state[k][1:] = swap(*state[k][1:], "row")
        return side

    def finish(k, side):
        state[k], side = sketch_stage(side, *state[k], last_m, signs[k], prior_scale)
        return side

    side = first(0, side)
    side = middle(0, side)
    for k in range(1, last + 1):
        side = first(k, side)
        side = last_column(k - 1, side)
        side = middle(k, side)
    for k in range(last - 1):
        side = finish(k, side)
    side = last_column(last, side)
    for k in range(max(last - 1, 0), last + 1):
        side = finish(k, side)
    sketch = [state[k] for k in range(last + 1)]
    grouped = [s.reshape(s.shape[0], BANDS * ROWS // 8, 8, COLS) for s in sketch]
    gram = sum_over(sum_over(gram_stage(grouped), "row"), "col")
    total = BANDS * ROWS * COLS * lax.axis_size("row") * lax.axis_size("col")
    r_factor, inverse = factor_stage(gram, probes, float(np.sqrt(np.float32(total))))
    basis = basis_stage(inverse, grouped)
    return basis.reshape(probes, BANDS, ROWS, COLS), r_factor


def solution(mesh):
    in_specs = (P(None, None, "row", "col"), P(None, "row", "col"), P(), P(), P(None, "row", "col"))
    out_specs = (P(None, None, "row", "col"), P())
    return jax.shard_map(shards, mesh=mesh, in_specs=in_specs, out_specs=out_specs, check_vma=False)
```

time: 308 us -> 186 us (0.60)
  starting transfers between devices: 112 us -> 47.5 us
  Pallas kernels: 137 us -> 76.5 us
  waiting for transfers between devices: 29.4 us -> 54.5 us
  local copies, waits for them, and re-layouts: 25.7 us -> 5.51 us
    ppermute x32 -> x24, starting transfers between devices: 108 us -> 44.8 us  [swap(): return (lax.ppermute(inner, axis, pairs), lax.ppermute(outer, axis, others))]
    pallas_call x22 -> x17, Pallas kernels: 130 us -> 68.5 us  [the longest x3 18.5 us: middle_stage(): pl.pallas_call(middle_kernel, out_shape=(whole, packed, packed, SIDE), in...]
    ppermute x32 -> x24, waiting for transfers between devices: 3.08 us -> 29.2 us  [swap(): return (lax.ppermute(inner, axis, pairs), lax.ppermute(outer, axis, others))]
    unnamed x90 -> x34, local copies, waits for them, and re-layouts: 25.7 us -> 0.1 us
    slice x0 -> x2, local copies, waits for them, and re-layouts: none -> 5.41 us  [shards(): probe_signs[start:start + count]]
  transfers between devices with their start and end apart: 39 -> 31, of which waited for: 9 -> 12; matrix products, arithmetic and copies ran while one was open for 0% -> 2% of each run, Pallas kernels for 33% -> 30%
where the time goes in v1:
time: 186 us; the launch traced here: 185 us
  Pallas kernels  76.5 us (41%)
  waiting for transfers between devices  54.5 us (29%)
  starting transfers between devices  47.5 us (26%)
  local copies, waits for them, and re-layouts  5.51 us (3%)
    ppermute x24, starting transfers between devices, swap(): return (lax.ppermute(inner, axis, pairs), lax.ppermute(outer, axis, others))  44.8 us
    ppermute x24, waiting for transfers between devices, swap(): return (lax.ppermute(inner, axis, pairs), lax.ppermute(outer, axis, others))  29.2 us
    ppermute x7, waiting for transfers between devices, sum_over(): lax.ppermute(value, axis, [(i, i ^ bit) for i in range(count)])  25.3 us
    pallas_call x3, Pallas kernels, middle_stage(): pl.pallas_call(middle_kernel, out_shape=(whole, packed, packed, SIDE), in...  18.5 us
    pallas_call x3, Pallas kernels, first_stage(): pl.pallas_call(first_kernel, out_shape=(jax.ShapeDtypeStruct((count, BAND...  13 us
    pallas_call x3, Pallas kernels, last_column_stage(): pl.pallas_call(last_column_kernel, out_shape=(whole, edge, edge, SIDE), i...  10.9 us
    pallas_call x3, Pallas kernels, sketch_stage(): pl.pallas_call(sketch_kernel, out_shape=(jax.ShapeDtypeStruct((count, BAN...  10.1 us
    pallas_call x1, Pallas kernels, basis_stage(): pl.pallas_call(basis_kernel, grid=(groups // 8,), out_shape=jax.ShapeDtyp...  6.62 us
  transfers between devices with their start and end apart: 31, of which 12 were waited for; matrix products, arithmetic and copies ran while one was open for 2% of the time, Pallas kernels for 30%

profile of v1, /device:TPU:56, one launch (start us, length us, event | category | flops | bytes accessed | tf_op | source)
XLA Modules:
  0.0 185.4 jit_solution(4900941996995783379)
XLA Ops:
  0.7 1.8 slice.9.signs
  2.5 1.2 edges.3
  3.8 4.9 %collective-permute-start.1 = (f32[8,120,256]{2,1,0:T(8,128)S(1)}, f32[8,120,256]{2,1,0:T(8,128)S(1)}, u32[]{:S(2)}, u32[]{:S(2)}) collective-permute-start(f32[8,120,256]{2,1,0:T(8,128)S(1)} %get-tuple-element.56), channel_id=1, source_target_pairs={{4,8},{8,4},{12,16},{16,12},{20,24},{24,20},{28,32},{32,28},{36,40... | collective-permute-start | bytes 2949128 | tf_op jit(solution)/shard_map/ppermute | solution.py:516
  8.7 3.6 %fusion = (s32[12,8,32,256]{3,2,1,0:T(8,128)S(1)}, s32[12,8,32,256]{3,2,1,0:T(8,128)S(1)}) fusion(s32[32,8,32,256]{3,2,1,0:T(8,128)} %param.11), kind=kLoop, calls=%fused_computation.1 | loop fusion | bytes 12582912 | tf_op jit(solution)/shard_map/slice | solution.py:524
  12.4 1.5 edges.4
  14.1 3.0 %collective-permute-start.5 = (f32[12,120,256]{2,1,0:T(8,128)S(1)}, f32[12,120,256]{2,1,0:T(8,128)S(1)}, u32[]{:S(2)}, u32[]{:S(2)}) collective-permute-start(f32[12,120,256]{2,1,0:T(8,128)S(1)} %get-tuple-element.66), channel_id=1, source_target_pairs={{4,8},{8,4},{12,16},{16,12},{20,24},{24,20},{28,32},{32,28},{36,40... | collective-permute-start | bytes 4423688 | tf_op jit(solution)/shard_map/ppermute | solution.py:516
  17.0 1.5 edges.5
  18.7 4.8 %collective-permute-start.11 = (f32[12,120,256]{2,1,0:T(8,128)S(1)}, f32[12,120,256]{2,1,0:T(8,128)S(1)}, u32[]{:S(2)}, u32[]{:S(2)}) collective-permute-start(f32[12,120,256]{2,1,0:T(8,128)S(1)} %get-tuple-element.77), channel_id=1, source_target_pairs={{4,8},{8,4},{12,16},{16,12},{20,24},{24,20},{28,32},{32,28},{36,40... | collective-permute-start | bytes 4423688 | tf_op jit(solution)/shard_map/ppermute | solution.py:516
  23.6 3.2 %prepare.1 = (bf16[256,1536]{1,0:T(8,128)(2,1)S(1)}, bf16[256,1536]{1,0:T(8,128)(2,1)S(1)}, bf16[256,768]{1,0:T(8,128)(2,1)S(1)}, bf16[256,768]{1,0:T(8,128)(2,1)S(1)}) custom-call(s32[2]{0:T(128)S(1)} %pad_add_fusion.side, f32[8,8]{1,0:T(8,128)S(1)} %copy-done.7, f32[8,8]{1,0:T(8,128)S(1)} %copy-done.8, f32[256,512]{1,0:T(8,128)S(1)} %copy-done.3, ...), custom_call_target="tpu_custom_call" | custom-call | tf_op jit(solution)/shard_map/prepare/pallas_call | solution.py:139
  26.9 3.5 %first_stage.3 = (f32[8,8,32,256]{3,2,1,0:T(8,128)S(1)}, f32[8,32,128]{2,1,0:T(8,128)S(1)}, f32[8,32,128]{2,1,0:T(8,128)S(1)}, s32[2]{0:T(128)S(1)}) custom-call(s32[2]{0:T(128)S(1)} %pad_add_fusion.side, s32[8,8,32,256]{3,2,1,0:T(8,128)S(1)} %slice.9.signs, f32[8,32,256]{2,1,0:T(8,128)S(1)} %copy-done.1, f32[8,120,256]{2,1,0:T(8,128)S(1)} %collective-permute-done.inner, ...), custom_call_target="tpu_custom_call" | custom-call | flops 1610612736 | bytes 8388608 | tf_op jit(solution)/shard_map/first_stage/pallas_call | solution.py:220
  30.6 4.9 %collective-permute-done.2.near = f32[8,32,128]{2,1,0:T(8,128)S(1)} collective-permute-done((f32[8,32,128]{2,1,0:T(8,128)S(1)}, f32[8,32,128]{2,1,0:T(8,128)S(1)}, u32[]{:S(2)}, u32[]{:S(2)}) %collective-permute-start.2) | collective-permute-done | bytes 131104 | tf_op jit(solution)/shard_map/ppermute | solution.py:516
  35.4 3.8 %collective-permute-start.3 = (f32[8,32,128]{2,1,0:T(8,128)S(1)}, f32[8,32,128]{2,1,0:T(8,128)S(1)}, u32[]{:S(2)}, u32[]{:S(2)}) collective-permute-start(f32[8,32,128]{2,1,0:T(8,128)S(1)} %get-tuple-element.61), channel_id=1, source_target_pairs={{1,2},{2,1},{5,6},{6,5},{9,10},{10,9},{13,14},{14,13},{17,18},{18,... | collective-permute-start | bytes 393224 | tf_op jit(solution)/shard_map/ppermute | solution.py:516
  39.3 3.0 %collective-permute-done.3.far = f32[8,32,128]{2,1,0:T(8,128)S(1)} collective-permute-done((f32[8,32,128]{2,1,0:T(8,128)S(1)}, f32[8,32,128]{2,1,0:T(8,128)S(1)}, u32[]{:S(2)}, u32[]{:S(2)}) %collective-permute-start.3) | collective-permute-done | bytes 131104 | tf_op jit(solution)/shard_map/ppermute | solution.py:516
  42.3 4.5 %middle_stage.3 = (f32[8,8,32,256]{3,2,1,0:T(8,128)S(1)}, f32[8,32,128]{2,1,0:T(8,128)S(1)}, f32[8,32,128]{2,1,0:T(8,128)S(1)}, s32[2]{0:T(128)S(1)}) custom-call(s32[2]{0:T(128)S(1)} %get-tuple-element.58.side, f32[8,8,32,256]{3,2,1,0:T(8,128)S(1)} %get-tuple-element.59.tiles, f32[8,32,128]{2,1,0:T(8,128)S(1)} %collective-permute-done.2.near, ...), custom_call_target="tpu_custom_call" | custom-call | flops 2684354560 | bytes 8388608 | tf_op jit(solution)/shard_map/middle_stage/pallas_call | solution.py:270
  46.9 3.8 %collective-permute-start.7 = (f32[8,32,128]{2,1,0:T(8,128)S(1)}, f32[8,32,128]{2,1,0:T(8,128)S(1)}, u32[]{:S(2)}, u32[]{:S(2)}) collective-permute-start(f32[8,32,128]{2,1,0:T(8,128)S(1)} %get-tuple-element.70), channel_id=1, source_target_pairs={{1,2},{2,1},{5,6},{6,5},{9,10},{10,9},{13,14},{14,13},{17,18},{18,... | collective-permute-start | bytes 393224 | tf_op jit(solution)/shard_map/ppermute | solution.py:516
  50.8 4.8 %first_stage.4 = (f32[12,8,32,256]{3,2,1,0:T(8,128)S(1)}, f32[12,32,128]{2,1,0:T(8,128)S(1)}, f32[12,32,128]{2,1,0:T(8,128)S(1)}, s32[2]{0:T(128)S(1)}) custom-call(s32[2]{0:T(128)S(1)} %get-tuple-element.64.side, s32[12,8,32,256]{3,2,1,0:T(8,128)S(1)} %get-tuple-element.109.signs, f32[8,32,256]{2,1,0:T(8,128)S(1)} %copy-done.1, ...), custom_call_target="tpu_custom_call" | custom-call | flops 2415919104 | bytes 12582912 | tf_op jit(solution)/shard_map/first_stage/pallas_call | solution.py:220
  55.7 2.8 %collective-permute-start.9 = (f32[12,32,128]{2,1,0:T(8,128)S(1)}, f32[12,32,128]{2,1,0:T(8,128)S(1)}, u32[]{:S(2)}, u32[]{:S(2)}) collective-permute-start(f32[12,32,128]{2,1,0:T(8,128)S(1)} %get-tuple-element.74), channel_id=1, source_target_pairs={{1,2},{2,1},{5,6},{6,5},{9,10},{10,9},{13,14},{14,13},{17,18},{18,... | collective-permute-start | bytes 589832 | tf_op jit(solution)/shard_map/ppermute | solution.py:516
  58.5 2.9 %last_column_stage.3 = (f32[8,8,32,256]{3,2,1,0:T(8,128)S(1)}, f32[8,120,256]{2,1,0:T(8,128)S(1)}, f32[8,120,256]{2,1,0:T(8,128)S(1)}, s32[2]{0:T(128)S(1)}) custom-call(s32[2]{0:T(128)S(1)} %get-tuple-element.67.side, f32[8,8,32,256]{3,2,1,0:T(8,128)S(1)} %get-tuple-element.68.tiles, f32[8,32,128]{2,1,0:T(8,128)S(1)} %collective-permute-done.6.near, ...), custom_call_target="tpu_custom_call" | custom-call | flops 1073741824 | bytes 8388608 | tf_op jit(solution)/shard_map/last_column_stage/pallas_call | solution.py:302
  61.6 4.3 %collective-permute-start.17 = (f32[8,120,256]{2,1,0:T(8,128)S(1)}, f32[8,120,256]{2,1,0:T(8,128)S(1)}, u32[]{:S(2)}, u32[]{:S(2)}) collective-permute-start(f32[8,120,256]{2,1,0:T(8,128)S(1)} %get-tuple-element.89), channel_id=1, source_target_pairs={{4,8},{8,4},{12,16},{16,12},{20,24},{24,20},{28,32},{32,28},{36,40... | collective-permute-start | bytes 2949128 | tf_op jit(solution)/shard_map/ppermute | solution.py:516
  65.9 7.0 %middle_stage.4 = (f32[12,8,32,256]{3,2,1,0:T(8,128)S(1)}, f32[12,32,128]{2,1,0:T(8,128)S(1)}, f32[12,32,128]{2,1,0:T(8,128)S(1)}, s32[2]{0:T(128)S(1)}) custom-call(s32[2]{0:T(128)S(1)} %get-tuple-element.71.side, f32[12,8,32,256]{3,2,1,0:T(8,128)S(1)} %get-tuple-element.72.tiles, f32[12,32,128]{2,1,0:T(8,128)S(1)} %collective-permute-done.8.near, ...), custom_call_target="tpu_custom_call" | custom-call | flops 4026531840 | bytes 12582912 | tf_op jit(solution)/shard_map/middle_stage/pallas_call | solution.py:270
  73.0 3.2 %collective-permute-start.13 = (f32[12,32,128]{2,1,0:T(8,128)S(1)}, f32[12,32,128]{2,1,0:T(8,128)S(1)}, u32[]{:S(2)}, u32[]{:S(2)}) collective-permute-start(f32[12,32,128]{2,1,0:T(8,128)S(1)} %get-tuple-element.81), channel_id=1, source_target_pairs={{1,2},{2,1},{5,6},{6,5},{9,10},{10,9},{13,14},{14,13},{17,18},{18,... | collective-permute-start | bytes 589832 | tf_op jit(solution)/shard_map/ppermute | solution.py:516
  76.3 4.8 %first_stage.5 = (f32[12,8,32,256]{3,2,1,0:T(8,128)S(1)}, f32[12,32,128]{2,1,0:T(8,128)S(1)}, f32[12,32,128]{2,1,0:T(8,128)S(1)}, s32[2]{0:T(128)S(1)}) custom-call(s32[2]{0:T(128)S(1)} %get-tuple-element.75.side, s32[12,8,32,256]{3,2,1,0:T(8,128)S(1)} %get-tuple-element.108.signs, f32[8,32,256]{2,1,0:T(8,128)S(1)} %copy-done.1, ...), custom_call_target="tpu_custom_call" | custom-call | flops 2415919104 | bytes 12582912 | tf_op jit(solution)/shard_map/first_stage/pallas_call | solution.py:220
  81.2 2.6 %collective-permute-start.15 = (f32[12,32,128]{2,1,0:T(8,128)S(1)}, f32[12,32,128]{2,1,0:T(8,128)S(1)}, u32[]{:S(2)}, u32[]{:S(2)}) collective-permute-start(f32[12,32,128]{2,1,0:T(8,128)S(1)} %get-tuple-element.85), channel_id=1, source_target_pairs={{1,2},{2,1},{5,6},{6,5},{9,10},{10,9},{13,14},{14,13},{17,18},{18,... | collective-permute-start | bytes 589832 | tf_op jit(solution)/shard_map/ppermute | solution.py:516
  83.8 4.2 %last_column_stage.4 = (f32[12,8,32,256]{3,2,1,0:T(8,128)S(1)}, f32[12,120,256]{2,1,0:T(8,128)}, f32[12,120,256]{2,1,0:T(8,128)S(1)}, s32[2]{0:T(128)S(1)}) custom-call(s32[2]{0:T(128)S(1)} %get-tuple-element.78.side, f32[12,8,32,256]{3,2,1,0:T(8,128)S(1)} %get-tuple-element.79.tiles, f32[12,32,128]{2,1,0:T(8,128)S(1)} %collective-permute-done.12.near, ...), custom_call_target="tpu_custom_call" | custom-call | flops 1610612736 | bytes 12582912 | tf_op jit(solution)/shard_map/last_column_stage/pallas_call | solution.py:302
  88.0 0.7 collective-permute-done.15.far
  88.7 6.9 %middle_stage.5 = (f32[12,8,32,256]{3,2,1,0:T(8,128)S(1)}, f32[12,32,128]{2,1,0:T(8,128)S(1)}, f32[12,32,128]{2,1,0:T(8,128)S(1)}, s32[2]{0:T(128)S(1)}) custom-call(s32[2]{0:T(128)S(1)} %get-tuple-element.82.side, f32[12,8,32,256]{3,2,1,0:T(8,128)S(1)} %get-tuple-element.83.tiles, f32[12,32,128]{2,1,0:T(8,128)S(1)} %collective-permute-done.14.near, ...), custom_call_target="tpu_custom_call" | custom-call | flops 4026531840 | bytes 12582912 | tf_op jit(solution)/shard_map/middle_stage/pallas_call | solution.py:270
  95.8 2.6 %collective-permute-start.19 = (f32[12,32,128]{2,1,0:T(8,128)S(1)}, f32[12,32,128]{2,1,0:T(8,128)S(1)}, u32[]{:S(2)}, u32[]{:S(2)}) collective-permute-start(f32[12,32,128]{2,1,0:T(8,128)S(1)} %get-tuple-element.95), channel_id=1, source_target_pairs={{1,2},{2,1},{5,6},{6,5},{9,10},{10,9},{13,14},{14,13},{17,18},{18,... | collective-permute-start | bytes 589832 | tf_op jit(solution)/shard_map/ppermute | solution.py:516
  98.5 4.3 %collective-permute-start.21 = (f32[12,120,256]{2,1,0:T(8,128)S(1)}, f32[12,120,256]{2,1,0:T(8,128)S(1)}, u32[]{:S(2)}, u32[]{:S(2)}) collective-permute-start(f32[12,120,256]{2,1,0:T(8,128)S(1)} %get-tuple-element.99), channel_id=1, source_target_pairs={{4,8},{8,4},{12,16},{16,12},{20,24},{24,20},{28,32},{32,28},{36,40... | collective-permute-start | bytes 4423688 | tf_op jit(solution)/shard_map/ppermute | solution.py:516
  102.9 2.7 %sketch_stage.3 = (f32[8,8,32,256]{3,2,1,0:T(8,128)S(1)}, s32[2]{0:T(128)S(1)}) custom-call(s32[2]{0:T(128)S(1)} %get-tuple-element.86.side, f32[8,8,32,256]{3,2,1,0:T(8,128)S(1)} %get-tuple-element.87.tiles, f32[8,120,256]{2,1,0:T(8,128)S(1)} %collective-permute-done.16.inner, f32[8,120,256]{2,1,0:T(8,128)S(1)} %collective-permute-done.17.outer, ...), custom_call_target="tpu_custom_call" | custom-call | flops 1610612736 | bytes 8388608 | tf_op jit(solution)/shard_map/sketch_stage/pallas_call | solution.py:326
  105.6 3.8 %last_column_stage.5 = (f32[12,8,32,256]{3,2,1,0:T(8,128)S(1)}, f32[12,120,256]{2,1,0:T(8,128)S(1)}, f32[12,120,256]{2,1,0:T(8,128)S(1)}, s32[2]{0:T(128)S(1)}) custom-call(s32[2]{0:T(128)S(1)} %get-tuple-element.92.side, f32[12,8,32,256]{3,2,1,0:T(8,128)S(1)} %get-tuple-element.93.tiles, f32[12,32,128]{2,1,0:T(8,128)S(1)} %collective-permute-done.18.near, ...), custom_call_target="tpu_custom_call" | custom-call | flops 1610612736 | bytes 12582912 | tf_op jit(solution)/shard_map/last_column_stage/pallas_call | solution.py:302
  109.5 3.3 %collective-permute-start.23 = (f32[12,120,256]{2,1,0:T(8,128)S(1)}, f32[12,120,256]{2,1,0:T(8,128)S(1)}, u32[]{:S(2)}, u32[]{:S(2)}) collective-permute-start(f32[12,120,256]{2,1,0:T(8,128)S(1)} %get-tuple-element.104), channel_id=1, source_target_pairs={{4,8},{8,4},{12,16},{16,12},{20,24},{24,20},{28,32},{32,28},{36,40... | collective-permute-start | bytes 4423688 | tf_op jit(solution)/shard_map/ppermute | solution.py:516
  112.8 8.5 %collective-permute-done.21.outer = f32[12,120,256]{2,1,0:T(8,128)S(1)} collective-permute-done((f32[12,120,256]{2,1,0:T(8,128)S(1)}, f32[12,120,256]{2,1,0:T(8,128)S(1)}, u32[]{:S(2)}, u32[]{:S(2)}) %collective-permute-start.21) | collective-permute-done | bytes 1474592 | tf_op jit(solution)/shard_map/ppermute | solution.py:516
  121.3 3.7 %sketch_stage.4 = (f32[12,8,32,256]{3,2,1,0:T(8,128)S(1)}, s32[2]{0:T(128)S(1)}) custom-call(s32[2]{0:T(128)S(1)} %get-tuple-element.96.side, f32[12,8,32,256]{3,2,1,0:T(8,128)S(1)} %get-tuple-element.97.tiles, f32[12,120,256]{2,1,0:T(8,128)S(1)} %collective-permute-done.20.inner, f32[12,120,256]{2,1,0:T(8,128)S(1)} %collective-permute-done.21.outer, ...), custom_call_target="tpu_custom_call" | custom-call | flops 2415919104 | bytes 12582912 | tf_op jit(solution)/shard_map/sketch_stage/pallas_call | solution.py:326
  125.0 12.1 %collective-permute-done.23.outer = f32[12,120,256]{2,1,0:T(8,128)S(1)} collective-permute-done((f32[12,120,256]{2,1,0:T(8,128)S(1)}, f32[12,120,256]{2,1,0:T(8,128)S(1)}, u32[]{:S(2)}, u32[]{:S(2)}) %collective-permute-start.23) | collective-permute-done | bytes 1474592 | tf_op jit(solution)/shard_map/ppermute | solution.py:516
  137.1 3.7 %sketch_stage.5 = (f32[12,8,32,256]{3,2,1,0:T(8,128)S(1)}, s32[2]{0:T(128)}) custom-call(s32[2]{0:T(128)S(1)} %get-tuple-element.101.side, f32[12,8,32,256]{3,2,1,0:T(8,128)S(1)} %get-tuple-element.102.tiles, f32[12,120,256]{2,1,0:T(8,128)S(1)} %collective-permute-done.22.inner, f32[12,120,256]{2,1,0:T(8,128)S(1)} %collective-permute-done.23.outer, ...), custom_call_target="tpu_custom_call" | custom-call | flops 2415919104 | bytes 12582912 | tf_op jit(solution)/shard_map/sketch_stage/pallas_call | solution.py:326
  140.9 5.2 %gram_stage.1.mine = f32[2,8,128]{2,1,0:T(8,128)S(1)} custom-call(f32[8,32,8,256]{3,2,1,0:T(8,128)S(1)} %bitcast.10, f32[12,32,8,256]{3,2,1,0:T(8,128)S(1)} %bitcast.6, f32[12,32,8,256]{3,2,1,0:T(8,128)S(1)} %bitcast.8), custom_call_target="tpu_custom_call" | custom-call | flops 4294967296 | bytes 8388608 | tf_op jit(solution)/shard_map/gram_stage/pallas_call | solution.py:375
  146.1 1.2 collective-permute-done.24.other
  147.3 3.6 %collective-permute-done.25.other = f32[2,8,128]{2,1,0:T(8,128)S(1)} collective-permute-done((f32[2,8,128]{2,1,0:T(8,128)S(1)}, f32[2,8,128]{2,1,0:T(8,128)S(1)}, u32[]{:S(2)}, u32[]{:S(2)}) %collective-permute-start.25) | collective-permute-done | bytes 8224 | tf_op jit(solution)/shard_map/ppermute | solution.py:442
  151.1 5.1 %collective-permute-done.26.other = f32[2,8,128]{2,1,0:T(8,128)S(1)} collective-permute-done((f32[2,8,128]{2,1,0:T(8,128)S(1)}, f32[2,8,128]{2,1,0:T(8,128)S(1)}, u32[]{:S(2)}, u32[]{:S(2)}) %collective-permute-start.26) | collective-permute-done | bytes 8224 | tf_op jit(solution)/shard_map/ppermute | solution.py:442
  156.2 0.6 collective-permute-start.27
  156.8 3.2 %collective-permute-done.27.other = f32[2,8,128]{2,1,0:T(8,128)S(1)} collective-permute-done((f32[2,8,128]{2,1,0:T(8,128)S(1)}, f32[2,8,128]{2,1,0:T(8,128)S(1)}, u32[]{:S(2)}, u32[]{:S(2)}) %collective-permute-start.27) | collective-permute-done | bytes 8224 | tf_op jit(solution)/shard_map/ppermute | solution.py:442
  160.0 1.0 collective-permute-start.28
  161.0 4.2 %collective-permute-done.28.other = f32[2,8,128]{2,1,0:T(8,128)S(1)} collective-permute-done((f32[2,8,128]{2,1,0:T(8,128)S(1)}, f32[2,8,128]{2,1,0:T(8,128)S(1)}, u32[]{:S(2)}, u32[]{:S(2)}) %collective-permute-start.28) | collective-permute-done | bytes 8224 | tf_op jit(solution)/shard_map/ppermute | solution.py:442
  165.3 3.6 %collective-permute-done.29.other = f32[2,8,128]{2,1,0:T(8,128)S(1)} collective-permute-done((f32[2,8,128]{2,1,0:T(8,128)S(1)}, f32[2,8,128]{2,1,0:T(8,128)S(1)}, u32[]{:S(2)}, u32[]{:S(2)}) %collective-permute-start.29) | collective-permute-done | bytes 8224 | tf_op jit(solution)/shard_map/ppermute | solution.py:442
  168.9 0.8 collective-permute-start.30
  169.8 4.4 %collective-permute-done.30.other = f32[2,8,128]{2,1,0:T(8,128)S(1)} collective-permute-done((f32[2,8,128]{2,1,0:T(8,128)S(1)}, f32[2,8,128]{2,1,0:T(8,128)S(1)}, u32[]{:S(2)}, u32[]{:S(2)}) %collective-permute-start.30) | collective-permute-done | bytes 8224 | tf_op jit(solution)/shard_map/ppermute | solution.py:442
  174.2 4.6 %factor_stage.1 = (f32[32,32]{1,0:T(8,128)}, f32[32,32]{1,0:T(8,128)S(1)}) custom-call(f32[2,8,128]{2,1,0:T(8,128)S(1)} %merge.13.refs_0_), custom_call_target="tpu_custom_call" | custom-call | tf_op jit(solution)/shard_map/factor_stage/pallas_call | solution.py:474
  178.8 6.6 %basis_stage.1 = f32[32,32,8,256]{3,2,1,0:T(8,128)} custom-call(f32[32,32]{1,0:T(8,128)S(1)} %get-tuple-element.106.inverse, f32[8,32,8,256]{3,2,1,0:T(8,128)S(1)} %bitcast.11, f32[12,32,8,256]{3,2,1,0:T(8,128)S(1)} %bitcast.7, f32[12,32,8,256]{3,2,1,0:T(8,128)S(1)} %bitcast.9), custom_call_target="tpu_custom_call" | custom-call | flops 3221225472 | bytes 16777216 | tf_op jit(solution)/shard_map/basis_stage/pallas_call | solution.py:502
  (77 shorter events, 1.8 us)
Async XLA Ops:
  0.6 1.9 %copy-start.1 = (f32[8,32,256]{2,1,0:T(8,128)S(1)}, f32[8,32,256]{2,1,0:T(8,128)}, u32[]{:S(2)}) copy-start(f32[8,32,256]{2,1,0:T(8,128)} %scale.17) | copy-start | bytes 786436
  3.7 14.9 %collective-permute-start = (f32[8,120,256]{2,1,0:T(8,128)S(1)}, f32[8,120,256]{2,1,0:T(8,128)S(1)}, u32[]{:S(2)}, u32[]{:S(2)}) collective-permute-start(f32[8,120,256]{2,1,0:T(8,128)S(1)} %get-tuple-element.55), channel_id=1, source_target_pairs={{0,4},{4,0},{8,12},{12,8},{16,20},{20,16},{24,28},{28,24},{32,36},... | collective-permute-start | bytes 2949128 | tf_op jit(solution)/shard_map/ppermute | solution.py:516
  3.8 23.0 %collective-permute-start.1 = (f32[8,120,256]{2,1,0:T(8,128)S(1)}, f32[8,120,256]{2,1,0:T(8,128)S(1)}, u32[]{:S(2)}, u32[]{:S(2)}) collective-permute-start(f32[8,120,256]{2,1,0:T(8,128)S(1)} %get-tuple-element.56), channel_id=1, source_target_pairs={{4,8},{8,4},{12,16},{16,12},{20,24},{24,20},{28,32},{32,28},{36,40... | collective-permute-start | bytes 2949128 | tf_op jit(solution)/shard_map/ppermute | solution.py:516
  13.9 9.6 %copy-start.2 = (f32[256,512]{1,0:T(8,128)S(1)}, f32[256,512]{1,0:T(8,128)}, u32[]{:S(2)}) copy-start(f32[256,512]{1,0:T(8,128)} %constant.40.clone.by_in) | copy-start | bytes 1572868
  13.9 9.6 %copy-start.3 = (f32[256,512]{1,0:T(8,128)S(1)}, f32[256,512]{1,0:T(8,128)}, u32[]{:S(2)}) copy-start(f32[256,512]{1,0:T(8,128)} %constant.39.clone.by_out) | copy-start | bytes 1572868
  13.9 9.6 %copy-start.4 = (f32[256,256]{1,0:T(8,128)S(1)}, f32[256,256]{1,0:T(8,128)}, u32[]{:S(2)}) copy-start(f32[256,256]{1,0:T(8,128)} %constant.43.clone.same) | copy-start | bytes 786436
  13.9 9.6 %copy-start.5 = (f32[256,8]{1,0:T(8,128)S(1)}, f32[256,8]{1,0:T(8,128)}, u32[]{:S(2)}) copy-start(f32[256,8]{1,0:T(8,128)} %constant.42.clone.spread) | copy-start | bytes 24580
  13.9 9.6 %copy-start.6 = (f32[8,512]{1,0:T(8,128)S(1)}, f32[8,512]{1,0:T(8,128)}, u32[]{:S(2)}) copy-start(f32[8,512]{1,0:T(8,128)} %constant.41.clone.pick) | copy-start | bytes 49156
  14.0 9.6 %copy-start.7 = (f32[8,8]{1,0:T(8,128)S(1)}, f32[8,8]{1,0:T(8,128)}, u32[]{:S(2)}) copy-start(f32[8,8]{1,0:T(8,128)} %factor.1) | copy-start | bytes 772
  14.0 9.6 %copy-start.8 = (f32[8,8]{1,0:T(8,128)S(1)}, f32[8,8]{1,0:T(8,128)}, u32[]{:S(2)}) copy-start(f32[8,8]{1,0:T(8,128)} %mix.1) | copy-start | bytes 772
  14.0 32.9 %collective-permute-start.4 = (f32[12,120,256]{2,1,0:T(8,128)S(1)}, f32[12,120,256]{2,1,0:T(8,128)S(1)}, u32[]{:S(2)}, u32[]{:S(2)}) collective-permute-start(f32[12,120,256]{2,1,0:T(8,128)S(1)} %get-tuple-element.65), channel_id=1, source_target_pairs={{0,4},{4,0},{8,12},{12,8},{16,20},{20,16},{24,28},{28,24},{32,36},... | collective-permute-start | bytes 4423688 | tf_op jit(solution)/shard_map/ppermute | solution.py:516
  14.1 36.7 %collective-permute-start.5 = (f32[12,120,256]{2,1,0:T(8,128)S(1)}, f32[12,120,256]{2,1,0:T(8,128)S(1)}, u32[]{:S(2)}, u32[]{:S(2)}) collective-permute-start(f32[12,120,256]{2,1,0:T(8,128)S(1)} %get-tuple-element.66), channel_id=1, source_target_pairs={{4,8},{8,4},{12,16},{16,12},{20,24},{24,20},{28,32},{32,28},{36,40... | collective-permute-start | bytes 4423688 | tf_op jit(solution)/shard_map/ppermute | solution.py:516
  18.6 54.5 %collective-permute-start.10 = (f32[12,120,256]{2,1,0:T(8,128)S(1)}, f32[12,120,256]{2,1,0:T(8,128)S(1)}, u32[]{:S(2)}, u32[]{:S(2)}) collective-permute-start(f32[12,120,256]{2,1,0:T(8,128)S(1)} %get-tuple-element.76), channel_id=1, source_target_pairs={{0,4},{4,0},{8,12},{12,8},{16,20},{20,16},{24,28},{28,24},{32,36},... | collective-permute-start | bytes 4423688 | tf_op jit(solution)/shard_map/ppermute | solution.py:516
  18.7 57.6 %collective-permute-start.11 = (f32[12,120,256]{2,1,0:T(8,128)S(1)}, f32[12,120,256]{2,1,0:T(8,128)S(1)}, u32[]{:S(2)}, u32[]{:S(2)}) collective-permute-start(f32[12,120,256]{2,1,0:T(8,128)S(1)} %get-tuple-element.77), channel_id=1, source_target_pairs={{4,8},{8,4},{12,16},{16,12},{20,24},{24,20},{28,32},{32,28},{36,40... | collective-permute-start | bytes 4423688 | tf_op jit(solution)/shard_map/ppermute | solution.py:516
  26.8 15.5 %copy-start.11 = (bf16[256,768]{1,0:T(8,128)(2,1)}, bf16[256,768]{1,0:T(8,128)(2,1)S(1)}, u32[]{:S(2)}) copy-start(bf16[256,768]{1,0:T(8,128)(2,1)S(1)} %get-tuple-element.62.mix) | copy-start | bytes 1179652
  26.8 15.5 %copy-start.13 = (bf16[256,768]{1,0:T(8,128)(2,1)}, bf16[256,768]{1,0:T(8,128)(2,1)S(1)}, u32[]{:S(2)}) copy-start(bf16[256,768]{1,0:T(8,128)(2,1)S(1)} %get-tuple-element.63.back) | copy-start | bytes 1179652
  26.8 24.0 %copy-start.9 = (bf16[256,1536]{1,0:T(8,128)(2,1)}, bf16[256,1536]{1,0:T(8,128)(2,1)S(1)}, u32[]{:S(2)}) copy-start(bf16[256,1536]{1,0:T(8,128)(2,1)S(1)} %get-tuple-element.57.matrix) | copy-start | bytes 2359300
  26.9 15.4 %copy-start = (bf16[8,1024,256]{2,1,0:T(8,128)(2,1)S(1)}, bf16[8,1024,256]{2,1,0:T(8,128)(2,1)}, u32[]{:S(2)}) copy-start(bf16[8,1024,256]{2,1,0:T(8,128)(2,1)} %constant.38.clone.table) | copy-start | bytes 12582916
  26.9 15.4 %copy-start.16 = (f32[8,32,256]{2,1,0:T(8,128)S(1)}, f32[8,32,256]{2,1,0:T(8,128)}, u32[]{:S(2)}) copy-start(f32[8,32,256]{2,1,0:T(8,128)} %weights.5) | copy-start | bytes 786436
  30.4 5.0 %collective-permute-start.2 = (f32[8,32,128]{2,1,0:T(8,128)S(1)}, f32[8,32,128]{2,1,0:T(8,128)S(1)}, u32[]{:S(2)}, u32[]{:S(2)}) collective-permute-start(f32[8,32,128]{2,1,0:T(8,128)S(1)} %get-tuple-element.60), channel_id=1, source_target_pairs={{0,1},{1,0},{2,3},{3,2},{4,5},{5,4},{6,7},{7,6},{8,9},{9,8},{10,11... | collective-permute-start | bytes 393224 | tf_op jit(solution)/shard_map/ppermute | solution.py:516
  35.4 6.8 %collective-permute-start.3 = (f32[8,32,128]{2,1,0:T(8,128)S(1)}, f32[8,32,128]{2,1,0:T(8,128)S(1)}, u32[]{:S(2)}, u32[]{:S(2)}) collective-permute-start(f32[8,32,128]{2,1,0:T(8,128)S(1)} %get-tuple-element.61), channel_id=1, source_target_pairs={{1,2},{2,1},{5,6},{6,5},{9,10},{10,9},{13,14},{14,13},{17,18},{18,... | collective-permute-start | bytes 393224 | tf_op jit(solution)/shard_map/ppermute | solution.py:516
  46.8 8.8 %collective-permute-start.6 = (f32[8,32,128]{2,1,0:T(8,128)S(1)}, f32[8,32,128]{2,1,0:T(8,128)S(1)}, u32[]{:S(2)}, u32[]{:S(2)}) collective-permute-start(f32[8,32,128]{2,1,0:T(8,128)S(1)} %get-tuple-element.69), channel_id=1, source_target_pairs={{0,1},{1,0},{2,3},{3,2},{4,5},{5,4},{6,7},{7,6},{8,9},{9,8},{10,11... | collective-permute-start | bytes 393224 | tf_op jit(solution)/shard_map/ppermute | solution.py:516
  46.9 11.6 %collective-permute-start.7 = (f32[8,32,128]{2,1,0:T(8,128)S(1)}, f32[8,32,128]{2,1,0:T(8,128)S(1)}, u32[]{:S(2)}, u32[]{:S(2)}) collective-permute-start(f32[8,32,128]{2,1,0:T(8,128)S(1)} %get-tuple-element.70), channel_id=1, source_target_pairs={{1,2},{2,1},{5,6},{6,5},{9,10},{10,9},{13,14},{14,13},{17,18},{18,... | collective-permute-start | bytes 393224 | tf_op jit(solution)/shard_map/ppermute | solution.py:516
  55.6 6.0 %collective-permute-start.8 = (f32[12,32,128]{2,1,0:T(8,128)S(1)}, f32[12,32,128]{2,1,0:T(8,128)S(1)}, u32[]{:S(2)}, u32[]{:S(2)}) collective-permute-start(f32[12,32,128]{2,1,0:T(8,128)S(1)} %get-tuple-element.73), channel_id=1, source_target_pairs={{0,1},{1,0},{2,3},{3,2},{4,5},{5,4},{6,7},{7,6},{8,9},{9,8},{10,11... | collective-permute-start | bytes 589832 | tf_op jit(solution)/shard_map/ppermute | solution.py:516
  55.7 10.2 %collective-permute-start.9 = (f32[12,32,128]{2,1,0:T(8,128)S(1)}, f32[12,32,128]{2,1,0:T(8,128)S(1)}, u32[]{:S(2)}, u32[]{:S(2)}) collective-permute-start(f32[12,32,128]{2,1,0:T(8,128)S(1)} %get-tuple-element.74), channel_id=1, source_target_pairs={{1,2},{2,1},{5,6},{6,5},{9,10},{10,9},{13,14},{14,13},{17,18},{18,... | collective-permute-start | bytes 589832 | tf_op jit(solution)/shard_map/ppermute | solution.py:516
  58.5 7.4 %copy-start.12 = (bf16[256,768]{1,0:T(8,128)(2,1)S(1)}, bf16[256,768]{1,0:T(8,128)(2,1)}, u32[]{:S(2)}) copy-start(bf16[256,768]{1,0:T(8,128)(2,1)} %copy-done.11) | copy-start | bytes 1179652
  58.5 7.4 %copy-start.14 = (bf16[256,768]{1,0:T(8,128)(2,1)S(1)}, bf16[256,768]{1,0:T(8,128)(2,1)}, u32[]{:S(2)}) copy-start(bf16[256,768]{1,0:T(8,128)(2,1)} %copy-done.13) | copy-start | bytes 1179652
  61.5 37.0 %collective-permute-start.16 = (f32[8,120,256]{2,1,0:T(8,128)S(1)}, f32[8,120,256]{2,1,0:T(8,128)S(1)}, u32[]{:S(2)}, u32[]{:S(2)}) collective-permute-start(f32[8,120,256]{2,1,0:T(8,128)S(1)} %get-tuple-element.88), channel_id=1, source_target_pairs={{0,4},{4,0},{8,12},{12,8},{16,20},{20,16},{24,28},{28,24},{32,36},... | collective-permute-start | bytes 2949128 | tf_op jit(solution)/shard_map/ppermute | solution.py:516
  61.6 41.3 %collective-permute-start.17 = (f32[8,120,256]{2,1,0:T(8,128)S(1)}, f32[8,120,256]{2,1,0:T(8,128)S(1)}, u32[]{:S(2)}, u32[]{:S(2)}) collective-permute-start(f32[8,120,256]{2,1,0:T(8,128)S(1)} %get-tuple-element.89), channel_id=1, source_target_pairs={{4,8},{8,4},{12,16},{16,12},{20,24},{24,20},{28,32},{32,28},{36,40... | collective-permute-start | bytes 2949128 | tf_op jit(solution)/shard_map/ppermute | solution.py:516
  65.9 10.4 %copy-start.10 = (bf16[256,1536]{1,0:T(8,128)(2,1)S(1)}, bf16[256,1536]{1,0:T(8,128)(2,1)}, u32[]{:S(2)}) copy-start(bf16[256,1536]{1,0:T(8,128)(2,1)} %copy-done.9) | copy-start | bytes 2359300
  72.9 8.2 %collective-permute-start.12 = (f32[12,32,128]{2,1,0:T(8,128)S(1)}, f32[12,32,128]{2,1,0:T(8,128)S(1)}, u32[]{:S(2)}, u32[]{:S(2)}) collective-permute-start(f32[12,32,128]{2,1,0:T(8,128)S(1)} %get-tuple-element.80), channel_id=1, source_target_pairs={{0,1},{1,0},{2,3},{3,2},{4,5},{5,4},{6,7},{7,6},{8,9},{9,8},{10,11... | collective-permute-start | bytes 589832 | tf_op jit(solution)/shard_map/ppermute | solution.py:516
  73.0 10.8 %collective-permute-start.13 = (f32[12,32,128]{2,1,0:T(8,128)S(1)}, f32[12,32,128]{2,1,0:T(8,128)S(1)}, u32[]{:S(2)}, u32[]{:S(2)}) collective-permute-start(f32[12,32,128]{2,1,0:T(8,128)S(1)} %get-tuple-element.81), channel_id=1, source_target_pairs={{1,2},{2,1},{5,6},{6,5},{9,10},{10,9},{13,14},{14,13},{17,18},{18,... | collective-permute-start | bytes 589832 | tf_op jit(solution)/shard_map/ppermute | solution.py:516
  81.1 7.0 %collective-permute-start.14 = (f32[12,32,128]{2,1,0:T(8,128)S(1)}, f32[12,32,128]{2,1,0:T(8,128)S(1)}, u32[]{:S(2)}, u32[]{:S(2)}) collective-permute-start(f32[12,32,128]{2,1,0:T(8,128)S(1)} %get-tuple-element.84), channel_id=1, source_target_pairs={{0,1},{1,0},{2,3},{3,2},{4,5},{5,4},{6,7},{7,6},{8,9},{9,8},{10,11... | collective-permute-start | bytes 589832 | tf_op jit(solution)/shard_map/ppermute | solution.py:516
  81.2 7.6 %collective-permute-start.15 = (f32[12,32,128]{2,1,0:T(8,128)S(1)}, f32[12,32,128]{2,1,0:T(8,128)S(1)}, u32[]{:S(2)}, u32[]{:S(2)}) collective-permute-start(f32[12,32,128]{2,1,0:T(8,128)S(1)} %get-tuple-element.85), channel_id=1, source_target_pairs={{1,2},{2,1},{5,6},{6,5},{9,10},{10,9},{13,14},{14,13},{17,18},{18,... | collective-permute-start | bytes 589832 | tf_op jit(solution)/shard_map/ppermute | solution.py:516
  83.8 4.9 %copy-start.15 = (bf16[256,768]{1,0:T(8,128)(2,1)S(1)}, bf16[256,768]{1,0:T(8,128)(2,1)}, u32[]{:S(2)}) copy-start(bf16[256,768]{1,0:T(8,128)(2,1)} %copy-done.13) | copy-start | bytes 1179652
  95.7 9.9 %collective-permute-start.18 = (f32[12,32,128]{2,1,0:T(8,128)S(1)}, f32[12,32,128]{2,1,0:T(8,128)S(1)}, u32[]{:S(2)}, u32[]{:S(2)}) collective-permute-start(f32[12,32,128]{2,1,0:T(8,128)S(1)} %get-tuple-element.94), channel_id=1, source_target_pairs={{0,1},{1,0},{2,3},{3,2},{4,5},{5,4},{6,7},{7,6},{8,9},{9,8},{10,11... | collective-permute-start | bytes 589832 | tf_op jit(solution)/shard_map/ppermute | solution.py:516
  95.8 9.8 %collective-permute-start.19 = (f32[12,32,128]{2,1,0:T(8,128)S(1)}, f32[12,32,128]{2,1,0:T(8,128)S(1)}, u32[]{:S(2)}, u32[]{:S(2)}) collective-permute-start(f32[12,32,128]{2,1,0:T(8,128)S(1)} %get-tuple-element.95), channel_id=1, source_target_pairs={{1,2},{2,1},{5,6},{6,5},{9,10},{10,9},{13,14},{14,13},{17,18},{18,... | collective-permute-start | bytes 589832 | tf_op jit(solution)/shard_map/ppermute | solution.py:516
  98.4 14.4 %collective-permute-start.20 = (f32[12,120,256]{2,1,0:T(8,128)}, f32[12,120,256]{2,1,0:T(8,128)S(1)}, u32[]{:S(2)}, u32[]{:S(2)}) collective-permute-start(f32[12,120,256]{2,1,0:T(8,128)} %get-tuple-element.98), channel_id=1, source_target_pairs={{0,4},{4,0},{8,12},{12,8},{16,20},{20,16},{24,28},{28,24},{32,36},... | collective-permute-start | bytes 4423688 | tf_op jit(solution)/shard_map/ppermute | solution.py:516
  98.5 22.8 %collective-permute-start.21 = (f32[12,120,256]{2,1,0:T(8,128)S(1)}, f32[12,120,256]{2,1,0:T(8,128)S(1)}, u32[]{:S(2)}, u32[]{:S(2)}) collective-permute-start(f32[12,120,256]{2,1,0:T(8,128)S(1)} %get-tuple-element.99), channel_id=1, source_target_pairs={{4,8},{8,4},{12,16},{16,12},{20,24},{24,20},{28,32},{32,28},{36,40... | collective-permute-start | bytes 4423688 | tf_op jit(solution)/shard_map/ppermute | solution.py:516
  109.4 15.6 %collective-permute-start.22 = (f32[12,120,256]{2,1,0:T(8,128)S(1)}, f32[12,120,256]{2,1,0:T(8,128)S(1)}, u32[]{:S(2)}, u32[]{:S(2)}) collective-permute-start(f32[12,120,256]{2,1,0:T(8,128)S(1)} %get-tuple-element.103), channel_id=1, source_target_pairs={{0,4},{4,0},{8,12},{12,8},{16,20},{20,16},{24,28},{28,24},{32,36},... | collective-permute-start | bytes 4423688 | tf_op jit(solution)/shard_map/ppermute | solution.py:516
  109.5 27.6 %collective-permute-start.23 = (f32[12,120,256]{2,1,0:T(8,128)S(1)}, f32[12,120,256]{2,1,0:T(8,128)S(1)}, u32[]{:S(2)}, u32[]{:S(2)}) collective-permute-start(f32[12,120,256]{2,1,0:T(8,128)S(1)} %get-tuple-element.104), channel_id=1, source_target_pairs={{4,8},{8,4},{12,16},{16,12},{20,24},{24,20},{28,32},{32,28},{36,40... | collective-permute-start | bytes 4423688 | tf_op jit(solution)/shard_map/ppermute | solution.py:516
  146.0 1.2 collective-permute-start.24
  147.3 3.7 %collective-permute-start.25 = (f32[2,8,128]{2,1,0:T(8,128)S(1)}, f32[2,8,128]{2,1,0:T(8,128)S(1)}, u32[]{:S(2)}, u32[]{:S(2)}) collective-permute-start(f32[2,8,128]{2,1,0:T(8,128)S(1)} %merge.7.mine), channel_id=1, source_target_pairs={{0,8},{4,12},{8,0},{12,4},{16,24},{20,28},{24,16},{28,20},{32,40},... | collective-permute-start | bytes 24584 | tf_op jit(solution)/shard_map/ppermute | solution.py:442
  151.0 5.2 %collective-permute-start.26 = (f32[2,8,128]{2,1,0:T(8,128)S(1)}, f32[2,8,128]{2,1,0:T(8,128)S(1)}, u32[]{:S(2)}, u32[]{:S(2)}) collective-permute-start(f32[2,8,128]{2,1,0:T(8,128)S(1)} %merge.8.mine), channel_id=1, source_target_pairs={{0,16},{4,20},{8,24},{12,28},{16,0},{20,4},{24,8},{28,12},{32,48},... | collective-permute-start | bytes 24584 | tf_op jit(solution)/shard_map/ppermute | solution.py:442
  156.2 3.7 %collective-permute-start.27 = (f32[2,8,128]{2,1,0:T(8,128)S(1)}, f32[2,8,128]{2,1,0:T(8,128)S(1)}, u32[]{:S(2)}, u32[]{:S(2)}) collective-permute-start(f32[2,8,128]{2,1,0:T(8,128)S(1)} %merge.9.mine), channel_id=1, source_target_pairs={{0,32},{4,36},{8,40},{12,44},{16,48},{20,52},{24,56},{28,60},{32,0... | collective-permute-start | bytes 24584 | tf_op jit(solution)/shard_map/ppermute | solution.py:442
  160.0 5.2 %collective-permute-start.28 = (f32[2,8,128]{2,1,0:T(8,128)S(1)}, f32[2,8,128]{2,1,0:T(8,128)S(1)}, u32[]{:S(2)}, u32[]{:S(2)}) collective-permute-start(f32[2,8,128]{2,1,0:T(8,128)S(1)} %merge.10.mine), channel_id=1, source_target_pairs={{0,64},{4,68},{8,72},{12,76},{16,80},{20,84},{24,88},{28,92},{32,9... | collective-permute-start | bytes 24584 | tf_op jit(solution)/shard_map/ppermute | solution.py:442
  165.2 3.7 %collective-permute-start.29 = (f32[2,8,128]{2,1,0:T(8,128)S(1)}, f32[2,8,128]{2,1,0:T(8,128)S(1)}, u32[]{:S(2)}, u32[]{:S(2)}) collective-permute-start(f32[2,8,128]{2,1,0:T(8,128)S(1)} %merge.11.mine), channel_id=1, source_target_pairs={{0,1},{1,0},{2,3},{3,2},{4,5},{5,4},{6,7},{7,6},{8,9},{9,8},{10,11... | collective-permute-start | bytes 24584 | tf_op jit(solution)/shard_map/ppermute | solution.py:442
  168.9 5.2 %collective-permute-start.30 = (f32[2,8,128]{2,1,0:T(8,128)S(1)}, f32[2,8,128]{2,1,0:T(8,128)S(1)}, u32[]{:S(2)}, u32[]{:S(2)}) collective-permute-start(f32[2,8,128]{2,1,0:T(8,128)S(1)} %merge.12.mine), channel_id=1, source_target_pairs={{0,2},{1,3},{2,0},{3,1},{4,6},{5,7},{6,4},{7,5},{8,10},{9,11},{10,... | collective-permute-start | bytes 24584 | tf_op jit(solution)/shard_map/ppermute | solution.py:442

commit v2 on v1

--- a/solution.py
+++ b/solution.py
@@ -246,7 +246,7 @@
             out[:, b] = blurred.reshape(count, ROWS, COLS)
 
 
-def middle_kernel(side, tiles, near, far, table, mix, back, weights, out, out_near, out_far, after, blurred):
+def middle_kernel(side, tiles, near, far, table, mix, back, weights, ahead, out, out_near, out_far, after, blurred):
     hand_on(side, after)
     lower = side[1] == 0
     column_blur(lower, tiles, near, far, table, blurred)
@@ -263,17 +263,18 @@
             store_packed(tile, lower, out_near, out_far, start + p)
 
 
-def middle_stage(side, tiles, near, far, table, mix, back, weights):
+def middle_stage(side, tiles, near, far, table, mix, back, weights, ahead):
+    ahead = side if ahead is None else ahead
     count = tiles.shape[0]
     whole = jax.ShapeDtypeStruct((count, BANDS, ROWS, COLS), F32)
     packed = jax.ShapeDtypeStruct((count, ROWS, 128), F32)
     return pl.pallas_call(
         middle_kernel, out_shape=(whole, packed, packed, SIDE),
-        in_specs=[SMEM] + [VMEM] * 7, out_specs=(VMEM, VMEM, VMEM, SMEM),
+        in_specs=[SMEM] + [VMEM] * 7 + [pl.BlockSpec(memory_space=pl.ANY)], out_specs=(VMEM, VMEM, VMEM, SMEM),
         scratch_shapes=[pltpu.VMEM((count, BANDS, ROWS, COLS), F32)],
         compiler_params=params(), cost_estimate=cost(count * 10 * 2 * 256**3, count * 2**20),
         name="middle_stage",
-    )(side, tiles, near, far, table, mix, back, weights)
+    )(side, tiles, near, far, table, mix, back, weights, ahead)
 
 
 def last_column_kernel(side, tiles, near, far, table, out, inner, outer, after):
@@ -345,8 +346,15 @@
     return (long == short).astype(F32)
 
 
-def gram_kernel(*refs):
-    chunks, out, even, cross = refs[:-3], refs[-3], refs[-2], refs[-1]
+def collapse(table):
+    kept = jnp.where(same_place(table.shape), table, 0.0)
+    rows, cols = table.shape
+    return dot(dot(spread_ones((rows // 8, rows), 1), kept, HI), spread_ones((cols, cols // 8), 0), HI)
+
+
+def early_gram_kernel(side, *refs):
+    chunks, out, after, even, cross = refs[:-4], refs[-4], refs[-3], refs[-2], refs[-1]
+    hand_on(side, after)
     even[...] = jnp.zeros_like(even)
     cross[...] = jnp.zeros_like(cross)
 
@@ -357,27 +365,55 @@
         even[...] += dot_nt(high, high) + dot_nt(low, low)
         cross[...] += dot_nt(high, low)
 
-    order = even.shape[0]
-    keep = same_place((order, order))
-
-    def collapse(table):
-        kept = jnp.where(keep, table, 0.0)
-        return dot(dot(spread_ones((order // 8, order), 1), kept, HI), spread_ones((order, order // 8), 0), HI)
-
     mixed = collapse(cross[...])
-    total = collapse(even[...]) + (mixed + mixed.T)
-    out[0] = jnp.concatenate([total[8 * j:8 * j + 8] for j in range(4)], axis=1)
+    out[...] = collapse(even[...]) + (mixed + mixed.T)
+
+
+def early_gram_stage(side, chunks):
+    probes = sum(c.shape[0] for c in chunks)
+    return pl.pallas_call(
+        early_gram_kernel, out_shape=(jax.ShapeDtypeStruct((probes, probes), F32), SIDE),
+        in_specs=[SMEM] + [VMEM] * len(chunks), out_specs=(VMEM, SMEM),
+        scratch_shapes=[pltpu.VMEM((8 * probes, 8 * probes), F32)] * 2,
+        compiler_params=params(), cost_estimate=cost(32 * 2 * 2 * 256**3, 2**23), name="early_gram_stage",
+    )(side, *chunks)
+
+
+def gram_kernel(early, *refs):
+    chunks, out, total = refs[:-2], refs[-2], refs[-1]
+    total[...] = jnp.zeros_like(total)
+    done = early.shape[0]
+
+    @pl.loop(0, chunks[0].shape[1], step=8)
+    def _(g):
+        values = jnp.concatenate([gather_group(chunks, g + j) for j in range(8)], axis=1)
+        high, low = split(values)
+        new_high, new_low = high[8 * done:], low[8 * done:]
+        total[...] += dot_nt(jnp.concatenate([new_high, new_low], axis=0), high)
+        total[...] += dot_nt(jnp.concatenate([new_low, new_high], axis=0), low)
+
+    rows = total.shape[0] // 2
+    late = collapse(total[0:rows] + total[rows:])
+    corner = 0.5 * (late[:, done:] + late[:, done:].T)
+    gram = jnp.concatenate(
+        [
+            jnp.concatenate([early[...], late[:, :done].T], axis=1),
+            jnp.concatenate([late[:, :done], corner], axis=1),
+        ],
+        axis=0,
+    )
+    out[0] = jnp.concatenate([gram[8 * j:8 * j + 8] for j in range(4)], axis=1)
     out[1] = jnp.zeros(out.shape[1:], F32)
 
 
-def gram_stage(chunks):
+def gram_stage(early, chunks):
     probes = sum(c.shape[0] for c in chunks)
     return pl.pallas_call(
         gram_kernel, out_shape=jax.ShapeDtypeStruct((2, 8, 128), F32),
-        in_specs=[VMEM] * len(chunks), out_specs=VMEM,
-        scratch_shapes=[pltpu.VMEM((256, 256), F32)] * 2,
-        compiler_params=params(), cost_estimate=cost(32 * 4 * 2 * 256**3, 2**23), name="gram_stage",
-    )(*chunks)
+        in_specs=[VMEM] * (1 + len(chunks)), out_specs=VMEM,
+        scratch_shapes=[pltpu.VMEM((16 * chunks[-1].shape[0], 8 * probes), F32)],
+        compiler_params=params(), cost_estimate=cost(32 * 2 * 2 * 256**3, 2**23), name="gram_stage",
+    )(early, *chunks)
 
 
 def group_blocks(chunks):
@@ -532,8 +568,8 @@
         state[k][1:] = swap(*state[k][1:], "col")
         return side
 
-    def middle(k, side):
-        *state[k], side = middle_stage(side, *state[k], table, mix_m, back_m, inverse_noise_variance)
+    def middle(k, side, ahead=None):
+        *state[k], side = middle_stage(side, *state[k], table, mix_m, back_m, inverse_noise_variance, ahead)
         state[k][1:] = swap(*state[k][1:], "col")
         return side
 
@@ -546,20 +582,26 @@
         state[k], side = sketch_stage(side, *state[k], last_m, signs[k], prior_scale)
         return side
 
+    def group(k):
+        return state[k].reshape(CHUNKS[k], BANDS * ROWS // 8, 8, COLS)
+
     side = first(0, side)
     side = middle(0, side)
-    for k in range(1, last + 1):
+    side = first(1, side)
+    side = last_column(0, side)
+    for k in range(2, last + 1):
+        side = middle(k - 1, side, state[k - 2][1])
         side = first(k, side)
         side = last_column(k - 1, side)
-        side = middle(k, side)
+    side = middle(last, side, state[last - 1][1])
     for k in range(last - 1):
         side = finish(k, side)
     side = last_column(last, side)
-    for k in range(max(last - 1, 0), last + 1):
-        side = finish(k, side)
-    sketch = [state[k] for k in range(last + 1)]
-    grouped = [s.reshape(s.shape[0], BANDS * ROWS // 8, 8, COLS) for s in sketch]
-    gram = sum_over(sum_over(gram_stage(grouped), "row"), "col")
+    side = finish(last - 1, side)
+    early, side = early_gram_stage(side, [group(k) for k in range(last)])
+    side = finish(last, side)
+    grouped = [group(k) for k in range(last + 1)]
+    gram = sum_over(sum_over(gram_stage(early, grouped), "row"), "col")
     total = BANDS * ROWS * COLS * lax.axis_size("row") * lax.axis_size("col")
     r_factor, inverse = factor_stage(gram, probes, float(np.sqrt(np.float32(total))))
     basis = basis_stage(inverse, grouped)

time: 186 us -> 179 us (0.962)
  waiting for transfers between devices: 54.5 us -> 49 us
    ppermute x24, waiting for transfers between devices: 29.2 us -> 23.2 us  [swap(): return (lax.ppermute(inner, axis, pairs), lax.ppermute(outer, axis, others))]
    pallas_call x0 -> x1, Pallas kernels: none -> 3.98 us  [early_gram_stage(): pl.pallas_call(early_gram_kernel, out_shape=(jax.ShapeDtypeStruct((probes...]
  transfers between devices with their start and end apart: 31 -> 31, of which waited for: 12 -> 16; matrix products, arithmetic and copies ran while one was open for 2% -> 2% of each run, Pallas kernels for 30% -> 30%
where the time goes in v2:
time: 179 us
  Pallas kernels  77.2 us (43%)
  waiting for transfers between devices  49 us (27%)
  starting transfers between devices  45.7 us (26%)
  local copies, waits for them, and re-layouts  5.46 us (3%)
    ppermute x24, starting transfers between devices, swap(): return (lax.ppermute(inner, axis, pairs), lax.ppermute(outer, axis, others))  43.5 us
    ppermute x7, waiting for transfers between devices, sum_over(): lax.ppermute(value, axis, [(i, i ^ bit) for i in range(count)])  25.8 us
    ppermute x24, waiting for transfers between devices, swap(): return (lax.ppermute(inner, axis, pairs), lax.ppermute(outer, axis, others))  23.2 us
    pallas_call x3, Pallas kernels, middle_stage(): pl.pallas_call(middle_kernel, out_shape=(whole, packed, packed, SIDE), in...  17.9 us
    pallas_call x3, Pallas kernels, first_stage(): pl.pallas_call(first_kernel, out_shape=(jax.ShapeDtypeStruct((count, BAND...  12.6 us
    pallas_call x3, Pallas kernels, sketch_stage(): pl.pallas_call(sketch_kernel, out_shape=(jax.ShapeDtypeStruct((count, BAN...  10.1 us
    pallas_call x3, Pallas kernels, last_column_stage(): pl.pallas_call(last_column_kernel, out_shape=(whole, edge, edge, SIDE), i...  10.1 us
    pallas_call x1, Pallas kernels, basis_stage(): pl.pallas_call(basis_kernel, grid=(groups // 8,), out_shape=jax.ShapeDtyp...  6.52 us
  transfers between devices with their start and end apart: 31, of which 16 were waited for; matrix products, arithmetic and copies ran while one was open for 2% of the time, Pallas kernels for 30%

profile of v2, /device:TPU:56, one launch (start us, length us, event | category | flops | bytes accessed | tf_op | source)
XLA Modules:
  0.0 178.9 jit_solution(13161595253780242932)
XLA Ops:
  0.7 1.8 slice.9.signs
  2.5 1.2 edges.3
  3.8 4.9 %collective-permute-start.1 = (f32[8,120,256]{2,1,0:T(8,128)S(1)}, f32[8,120,256]{2,1,0:T(8,128)S(1)}, u32[]{:S(2)}, u32[]{:S(2)}) collective-permute-start(f32[8,120,256]{2,1,0:T(8,128)S(1)} %get-tuple-element.58), channel_id=1, source_target_pairs={{4,8},{8,4},{12,16},{16,12},{20,24},{24,20},{28,32},{32,28},{36,40... | collective-permute-start | bytes 2949128 | tf_op jit(solution)/shard_map/ppermute | solution.py:552
  8.7 3.6 %fusion = (s32[12,8,32,256]{3,2,1,0:T(8,128)S(1)}, s32[12,8,32,256]{3,2,1,0:T(8,128)S(1)}) fusion(s32[32,8,32,256]{3,2,1,0:T(8,128)} %param.11), kind=kLoop, calls=%fused_computation.1 | loop fusion | bytes 12582912 | tf_op jit(solution)/shard_map/slice | solution.py:560
  12.4 1.5 edges.4
  14.0 2.8 %collective-permute-start.5 = (f32[12,120,256]{2,1,0:T(8,128)S(1)}, f32[12,120,256]{2,1,0:T(8,128)S(1)}, u32[]{:S(2)}, u32[]{:S(2)}) collective-permute-start(f32[12,120,256]{2,1,0:T(8,128)S(1)} %get-tuple-element.68), channel_id=1, source_target_pairs={{4,8},{8,4},{12,16},{16,12},{20,24},{24,20},{28,32},{32,28},{36,40... | collective-permute-start | bytes 4423688 | tf_op jit(solution)/shard_map/ppermute | solution.py:552
  16.9 3.2 %prepare.1 = (bf16[256,1536]{1,0:T(8,128)(2,1)S(1)}, bf16[256,1536]{1,0:T(8,128)(2,1)S(1)}, bf16[256,768]{1,0:T(8,128)(2,1)S(1)}, bf16[256,768]{1,0:T(8,128)(2,1)S(1)}) custom-call(s32[2]{0:T(128)S(1)} %pad_add_fusion.side, f32[8,8]{1,0:T(8,128)S(1)} %copy-done.7, f32[8,8]{1,0:T(8,128)S(1)} %copy-done.8, f32[256,512]{1,0:T(8,128)S(1)} %copy-done.3, ...), custom_call_target="tpu_custom_call" | custom-call | tf_op jit(solution)/shard_map/prepare/pallas_call | solution.py:139
  20.2 1.1 collective-permute-done.1.outer
  21.3 3.4 %first_stage.3 = (f32[8,8,32,256]{3,2,1,0:T(8,128)S(1)}, f32[8,32,128]{2,1,0:T(8,128)S(1)}, f32[8,32,128]{2,1,0:T(8,128)S(1)}, s32[2]{0:T(128)S(1)}) custom-call(s32[2]{0:T(128)S(1)} %pad_add_fusion.side, s32[8,8,32,256]{3,2,1,0:T(8,128)S(1)} %slice.9.signs, f32[8,32,256]{2,1,0:T(8,128)S(1)} %copy-done.1, f32[8,120,256]{2,1,0:T(8,128)S(1)} %collective-permute-done.inner, ...), custom_call_target="tpu_custom_call" | custom-call | flops 1610612736 | bytes 8388608 | tf_op jit(solution)/shard_map/first_stage/pallas_call | solution.py:220
  25.0 5.3 %collective-permute-start.3 = (f32[8,32,128]{2,1,0:T(8,128)S(1)}, f32[8,32,128]{2,1,0:T(8,128)S(1)}, u32[]{:S(2)}, u32[]{:S(2)}) collective-permute-start(f32[8,32,128]{2,1,0:T(8,128)S(1)} %get-tuple-element.63), channel_id=1, source_target_pairs={{1,2},{2,1},{5,6},{6,5},{9,10},{10,9},{13,14},{14,13},{17,18},{18,... | collective-permute-start | bytes 393224 | tf_op jit(solution)/shard_map/ppermute | solution.py:552
  30.3 1.5 edges.5
  31.9 4.3 %collective-permute-start.12 = (f32[12,120,256]{2,1,0:T(8,128)S(1)}, f32[12,120,256]{2,1,0:T(8,128)S(1)}, u32[]{:S(2)}, u32[]{:S(2)}) collective-permute-start(f32[12,120,256]{2,1,0:T(8,128)S(1)} %get-tuple-element.80), channel_id=1, source_target_pairs={{4,8},{8,4},{12,16},{16,12},{20,24},{24,20},{28,32},{32,28},{36,40... | collective-permute-start | bytes 4423688 | tf_op jit(solution)/shard_map/ppermute | solution.py:552
  36.3 4.4 %middle_stage.3 = (f32[8,8,32,256]{3,2,1,0:T(8,128)S(1)}, f32[8,32,128]{2,1,0:T(8,128)S(1)}, f32[8,32,128]{2,1,0:T(8,128)S(1)}, s32[2]{0:T(128)S(1)}) custom-call(s32[2]{0:T(128)S(1)} %get-tuple-element.60.side.ahead, f32[8,8,32,256]{3,2,1,0:T(8,128)S(1)} %get-tuple-element.61.tiles, f32[8,32,128]{2,1,0:T(8,128)S(1)} %collective-permute-done.2.near, ...), custom_call_target="tpu_custom_call" | custom-call | flops 2684354560 | bytes 8388608 | tf_op jit(solution)/shard_map/middle_stage/pallas_call | solution.py:271
  40.8 3.0 %collective-permute-start.7 = (f32[8,32,128]{2,1,0:T(8,128)S(1)}, f32[8,32,128]{2,1,0:T(8,128)S(1)}, u32[]{:S(2)}, u32[]{:S(2)}) collective-permute-start(f32[8,32,128]{2,1,0:T(8,128)S(1)} %get-tuple-element.72), channel_id=1, source_target_pairs={{1,2},{2,1},{5,6},{6,5},{9,10},{10,9},{13,14},{14,13},{17,18},{18,... | collective-permute-start | bytes 393224 | tf_op jit(solution)/shard_map/ppermute | solution.py:552
  43.9 4.6 %first_stage.4 = (f32[12,8,32,256]{3,2,1,0:T(8,128)S(1)}, f32[12,32,128]{2,1,0:T(8,128)S(1)}, f32[12,32,128]{2,1,0:T(8,128)S(1)}, s32[2]{0:T(128)S(1)}) custom-call(s32[2]{0:T(128)S(1)} %get-tuple-element.66.side, s32[12,8,32,256]{3,2,1,0:T(8,128)S(1)} %get-tuple-element.113.signs, f32[8,32,256]{2,1,0:T(8,128)S(1)} %copy-done.1, ...), custom_call_target="tpu_custom_call" | custom-call | flops 2415919104 | bytes 12582912 | tf_op jit(solution)/shard_map/first_stage/pallas_call | solution.py:220
  48.5 2.9 %last_column_stage.3 = (f32[8,8,32,256]{3,2,1,0:T(8,128)S(1)}, f32[8,120,256]{2,1,0:T(8,128)S(1)}, f32[8,120,256]{2,1,0:T(8,128)S(1)}, s32[2]{0:T(128)S(1)}) custom-call(s32[2]{0:T(128)S(1)} %get-tuple-element.69.side, f32[8,8,32,256]{3,2,1,0:T(8,128)S(1)} %get-tuple-element.70.tiles, f32[8,32,128]{2,1,0:T(8,128)S(1)} %collective-permute-done.6.near, ...), custom_call_target="tpu_custom_call" | custom-call | flops 1073741824 | bytes 8388608 | tf_op jit(solution)/shard_map/last_column_stage/pallas_call | solution.py:303
  51.8 2.8 %collective-permute-start.9 = (f32[12,32,128]{2,1,0:T(8,128)S(1)}, f32[12,32,128]{2,1,0:T(8,128)S(1)}, u32[]{:S(2)}, u32[]{:S(2)}) collective-permute-start(f32[12,32,128]{2,1,0:T(8,128)S(1)} %get-tuple-element.76), channel_id=1, source_target_pairs={{1,2},{2,1},{5,6},{6,5},{9,10},{10,9},{13,14},{14,13},{17,18},{18,... | collective-permute-start | bytes 589832 | tf_op jit(solution)/shard_map/ppermute | solution.py:552
  54.7 4.4 %collective-permute-done.8.near = f32[12,32,128]{2,1,0:T(8,128)S(1)} collective-permute-done((f32[12,32,128]{2,1,0:T(8,128)S(1)}, f32[12,32,128]{2,1,0:T(8,128)S(1)}, u32[]{:S(2)}, u32[]{:S(2)}) %collective-permute-start.8) | collective-permute-done | bytes 196640 | tf_op jit(solution)/shard_map/ppermute | solution.py:552
  59.1 1.9 %collective-permute-done.9.far = f32[12,32,128]{2,1,0:T(8,128)S(1)} collective-permute-done((f32[12,32,128]{2,1,0:T(8,128)S(1)}, f32[12,32,128]{2,1,0:T(8,128)S(1)}, u32[]{:S(2)}, u32[]{:S(2)}) %collective-permute-start.9) | collective-permute-done | bytes 196640 | tf_op jit(solution)/shard_map/ppermute | solution.py:552
  61.0 6.7 %middle_stage.4 = (f32[12,8,32,256]{3,2,1,0:T(8,128)S(1)}, f32[12,32,128]{2,1,0:T(8,128)S(1)}, f32[12,32,128]{2,1,0:T(8,128)S(1)}, s32[2]{0:T(128)S(1)}) custom-call(s32[2]{0:T(128)S(1)} %get-tuple-element.73.side, f32[12,8,32,256]{3,2,1,0:T(8,128)S(1)} %get-tuple-element.74.tiles, f32[12,32,128]{2,1,0:T(8,128)S(1)} %collective-permute-done.8.near, ...), custom_call_target="tpu_custom_call" | custom-call | flops 4026531840 | bytes 12582912 | tf_op jit(solution)/shard_map/middle_stage/pallas_call | solution.py:271
  67.8 2.8 %collective-permute-start.14 = (f32[12,32,128]{2,1,0:T(8,128)S(1)}, f32[12,32,128]{2,1,0:T(8,128)S(1)}, u32[]{:S(2)}, u32[]{:S(2)}) collective-permute-start(f32[12,32,128]{2,1,0:T(8,128)S(1)} %get-tuple-element.84), channel_id=1, source_target_pairs={{1,2},{2,1},{5,6},{6,5},{9,10},{10,9},{13,14},{14,13},{17,18},{18,... | collective-permute-start | bytes 589832 | tf_op jit(solution)/shard_map/ppermute | solution.py:552
  70.6 4.6 %first_stage.5 = (f32[12,8,32,256]{3,2,1,0:T(8,128)S(1)}, f32[12,32,128]{2,1,0:T(8,128)S(1)}, f32[12,32,128]{2,1,0:T(8,128)S(1)}, s32[2]{0:T(128)S(1)}) custom-call(s32[2]{0:T(128)S(1)} %get-tuple-element.78.side, s32[12,8,32,256]{3,2,1,0:T(8,128)S(1)} %get-tuple-element.112.signs, f32[8,32,256]{2,1,0:T(8,128)S(1)} %copy-done.1, ...), custom_call_target="tpu_custom_call" | custom-call | flops 2415919104 | bytes 12582912 | tf_op jit(solution)/shard_map/first_stage/pallas_call | solution.py:220
  76.2 3.6 %last_column_stage.4 = (f32[12,8,32,256]{3,2,1,0:T(8,128)S(1)}, f32[12,120,256]{2,1,0:T(8,128)S(1)}, f32[12,120,256]{2,1,0:T(8,128)S(1)}, s32[2]{0:T(128)S(1)}) custom-call(s32[2]{0:T(128)S(1)} %get-tuple-element.81.side, f32[12,8,32,256]{3,2,1,0:T(8,128)S(1)} %get-tuple-element.82.tiles, f32[12,32,128]{2,1,0:T(8,128)S(1)} %collective-permute-done.13.near, ...), custom_call_target="tpu_custom_call" | custom-call | flops 1610612736 | bytes 12582912 | tf_op jit(solution)/shard_map/last_column_stage/pallas_call | solution.py:303
  79.8 2.7 %collective-permute-start.18 = (f32[8,120,256]{2,1,0:T(8,128)S(1)}, f32[8,120,256]{2,1,0:T(8,128)S(1)}, u32[]{:S(2)}, u32[]{:S(2)}) collective-permute-start(f32[8,120,256]{2,1,0:T(8,128)S(1)} %get-tuple-element.92), channel_id=1, source_target_pairs={{4,8},{8,4},{12,16},{16,12},{20,24},{24,20},{28,32},{32,28},{36,40... | collective-permute-start | bytes 2949128 | tf_op jit(solution)/shard_map/ppermute | solution.py:552
  82.7 2.8 %collective-permute-start.16 = (f32[12,32,128]{2,1,0:T(8,128)S(1)}, f32[12,32,128]{2,1,0:T(8,128)S(1)}, u32[]{:S(2)}, u32[]{:S(2)}) collective-permute-start(f32[12,32,128]{2,1,0:T(8,128)S(1)} %get-tuple-element.88), channel_id=1, source_target_pairs={{1,2},{2,1},{5,6},{6,5},{9,10},{10,9},{13,14},{14,13},{17,18},{18,... | collective-permute-start | bytes 589832 | tf_op jit(solution)/shard_map/ppermute | solution.py:552
  85.5 4.5 %collective-permute-start.21 = (f32[12,120,256]{2,1,0:T(8,128)S(1)}, f32[12,120,256]{2,1,0:T(8,128)S(1)}, u32[]{:S(2)}, u32[]{:S(2)}) collective-permute-start(f32[12,120,256]{2,1,0:T(8,128)S(1)} %get-tuple-element.100), channel_id=1, source_target_pairs={{4,8},{8,4},{12,16},{16,12},{20,24},{24,20},{28,32},{32,28},{36,40... | collective-permute-start | bytes 4423688 | tf_op jit(solution)/shard_map/ppermute | solution.py:552
  90.1 1.0 collective-permute-done.16.far
  91.0 6.7 %middle_stage.5 = (f32[12,8,32,256]{3,2,1,0:T(8,128)S(1)}, f32[12,32,128]{2,1,0:T(8,128)S(1)}, f32[12,32,128]{2,1,0:T(8,128)S(1)}, s32[2]{0:T(128)S(1)}) custom-call(s32[2]{0:T(128)S(1)} %get-tuple-element.85.side, f32[12,8,32,256]{3,2,1,0:T(8,128)S(1)} %get-tuple-element.86.tiles, f32[12,32,128]{2,1,0:T(8,128)S(1)} %collective-permute-done.15.near, ...), custom_call_target="tpu_custom_call" | custom-call | flops 4026531840 | bytes 12582912 | tf_op jit(solution)/shard_map/middle_stage/pallas_call | solution.py:271
  97.9 2.7 %collective-permute-start.20 = (f32[12,32,128]{2,1,0:T(8,128)S(1)}, f32[12,32,128]{2,1,0:T(8,128)S(1)}, u32[]{:S(2)}, u32[]{:S(2)}) collective-permute-start(f32[12,32,128]{2,1,0:T(8,128)S(1)} %get-tuple-element.97), channel_id=1, source_target_pairs={{1,2},{2,1},{5,6},{6,5},{9,10},{10,9},{13,14},{14,13},{17,18},{18,... | collective-permute-start | bytes 589832 | tf_op jit(solution)/shard_map/ppermute | solution.py:552
  100.6 2.6 %sketch_stage.3 = (f32[8,8,32,256]{3,2,1,0:T(8,128)S(1)}, s32[2]{0:T(128)S(1)}) custom-call(s32[2]{0:T(128)S(1)} %get-tuple-element.90.side, f32[8,8,32,256]{3,2,1,0:T(8,128)S(1)} %get-tuple-element.91.tiles, f32[8,120,256]{2,1,0:T(8,128)S(1)} %collective-permute-done.10.ahead.inner, f32[8,120,256]{2,1,0:T(8,128)S(1)} %collective-permute-done.18.outer, ...), custom_call_target="tpu_custom_call" | custom-call | flops 1610612736 | bytes 8388608 | tf_op jit(solution)/shard_map/sketch_stage/pallas_call | solution.py:327
  103.5 1.9 %collective-permute-done.20.far = f32[12,32,128]{2,1,0:T(8,128)S(1)} collective-permute-done((f32[12,32,128]{2,1,0:T(8,128)S(1)}, f32[12,32,128]{2,1,0:T(8,128)S(1)}, u32[]{:S(2)}, u32[]{:S(2)}) %collective-permute-start.20) | collective-permute-done | bytes 196640 | tf_op jit(solution)/shard_map/ppermute | solution.py:552
  105.4 3.6 %last_column_stage.5 = (f32[12,8,32,256]{3,2,1,0:T(8,128)S(1)}, f32[12,120,256]{2,1,0:T(8,128)S(1)}, f32[12,120,256]{2,1,0:T(8,128)S(1)}, s32[2]{0:T(128)S(1)}) custom-call(s32[2]{0:T(128)S(1)} %get-tuple-element.94.side, f32[12,8,32,256]{3,2,1,0:T(8,128)S(1)} %get-tuple-element.95.tiles, f32[12,32,128]{2,1,0:T(8,128)S(1)} %collective-permute-done.19.near, ...), custom_call_target="tpu_custom_call" | custom-call | flops 1610612736 | bytes 12582912 | tf_op jit(solution)/shard_map/last_column_stage/pallas_call | solution.py:303
  109.1 3.4 %collective-permute-start.23 = (f32[12,120,256]{2,1,0:T(8,128)S(1)}, f32[12,120,256]{2,1,0:T(8,128)S(1)}, u32[]{:S(2)}, u32[]{:S(2)}) collective-permute-start(f32[12,120,256]{2,1,0:T(8,128)S(1)} %get-tuple-element.108), channel_id=1, source_target_pairs={{4,8},{8,4},{12,16},{16,12},{20,24},{24,20},{28,32},{32,28},{36,40... | collective-permute-start | bytes 4423688 | tf_op jit(solution)/shard_map/ppermute | solution.py:552
  113.2 3.7 %sketch_stage.4 = (f32[12,8,32,256]{3,2,1,0:T(8,128)S(1)}, s32[2]{0:T(128)S(1)}) custom-call(s32[2]{0:T(128)S(1)} %get-tuple-element.98.side, f32[12,8,32,256]{3,2,1,0:T(8,128)S(1)} %get-tuple-element.99.tiles, f32[12,120,256]{2,1,0:T(8,128)S(1)} %collective-permute-done.17.ahead.inner, f32[12,120,256]{2,1,0:T(8,128)S(1)} %collective-permute-done.21.outer, ...), custom_call_target="tpu_custom_call" | custom-call | flops 2415919104 | bytes 12582912 | tf_op jit(solution)/shard_map/sketch_stage/pallas_call | solution.py:327
  116.9 4.0 %early_gram_stage.1 = (f32[20,20]{1,0:T(8,128)S(1)}, s32[2]{0:T(128)S(1)}) custom-call(s32[2]{0:T(128)S(1)} %get-tuple-element.101.side, f32[8,32,8,256]{3,2,1,0:T(8,128)S(1)} %bitcast.11, f32[12,32,8,256]{3,2,1,0:T(8,128)S(1)} %bitcast.6), custom_call_target="tpu_custom_call" | custom-call | flops 2147483648 | bytes 8388608 | tf_op jit(solution)/shard_map/early_gram_stage/pallas_call | solution.py:374
  120.9 11.0 %collective-permute-done.23.outer = f32[12,120,256]{2,1,0:T(8,128)S(1)} collective-permute-done((f32[12,120,256]{2,1,0:T(8,128)S(1)}, f32[12,120,256]{2,1,0:T(8,128)S(1)}, u32[]{:S(2)}, u32[]{:S(2)}) %collective-permute-start.23) | collective-permute-done | bytes 1474592 | tf_op jit(solution)/shard_map/ppermute | solution.py:552
  131.9 3.7 %sketch_stage.5 = (f32[12,8,32,256]{3,2,1,0:T(8,128)S(1)}, s32[2]{0:T(128)}) custom-call(s32[2]{0:T(128)S(1)} %get-tuple-element.105.side, f32[12,8,32,256]{3,2,1,0:T(8,128)S(1)} %get-tuple-element.106.tiles, f32[12,120,256]{2,1,0:T(8,128)S(1)} %collective-permute-done.22.inner, f32[12,120,256]{2,1,0:T(8,128)S(1)} %collective-permute-done.23.outer, ...), custom_call_target="tpu_custom_call" | custom-call | flops 2415919104 | bytes 12582912 | tf_op jit(solution)/shard_map/sketch_stage/pallas_call | solution.py:327
  135.6 3.9 %gram_stage.1.mine = f32[2,8,128]{2,1,0:T(8,128)S(1)} custom-call(f32[20,20]{1,0:T(8,128)S(1)} %get-tuple-element.104.early, f32[8,32,8,256]{3,2,1,0:T(8,128)S(1)} %bitcast.12, f32[12,32,8,256]{3,2,1,0:T(8,128)S(1)} %bitcast.7, f32[12,32,8,256]{3,2,1,0:T(8,128)S(1)} %bitcast.9), custom_call_target="tpu_custom_call" | custom-call | flops 2147483648 | bytes 8388608 | tf_op jit(solution)/shard_map/gram_stage/pallas_call | solution.py:411
  139.6 1.2 collective-permute-done.24.other
  140.9 3.6 %collective-permute-done.25.other = f32[2,8,128]{2,1,0:T(8,128)S(1)} collective-permute-done((f32[2,8,128]{2,1,0:T(8,128)S(1)}, f32[2,8,128]{2,1,0:T(8,128)S(1)}, u32[]{:S(2)}, u32[]{:S(2)}) %collective-permute-start.25) | collective-permute-done | bytes 8224 | tf_op jit(solution)/shard_map/ppermute | solution.py:478
  144.7 5.1 %collective-permute-done.26.other = f32[2,8,128]{2,1,0:T(8,128)S(1)} collective-permute-done((f32[2,8,128]{2,1,0:T(8,128)S(1)}, f32[2,8,128]{2,1,0:T(8,128)S(1)}, u32[]{:S(2)}, u32[]{:S(2)}) %collective-permute-start.26) | collective-permute-done | bytes 8224 | tf_op jit(solution)/shard_map/ppermute | solution.py:478
  150.3 3.2 %collective-permute-done.27.other = f32[2,8,128]{2,1,0:T(8,128)S(1)} collective-permute-done((f32[2,8,128]{2,1,0:T(8,128)S(1)}, f32[2,8,128]{2,1,0:T(8,128)S(1)}, u32[]{:S(2)}, u32[]{:S(2)}) %collective-permute-start.27) | collective-permute-done | bytes 8224 | tf_op jit(solution)/shard_map/ppermute | solution.py:478
  153.5 1.0 collective-permute-start.28
  154.5 4.2 %collective-permute-done.28.other = f32[2,8,128]{2,1,0:T(8,128)S(1)} collective-permute-done((f32[2,8,128]{2,1,0:T(8,128)S(1)}, f32[2,8,128]{2,1,0:T(8,128)S(1)}, u32[]{:S(2)}, u32[]{:S(2)}) %collective-permute-start.28) | collective-permute-done | bytes 8224 | tf_op jit(solution)/shard_map/ppermute | solution.py:478
  158.8 3.6 %collective-permute-done.29.other = f32[2,8,128]{2,1,0:T(8,128)S(1)} collective-permute-done((f32[2,8,128]{2,1,0:T(8,128)S(1)}, f32[2,8,128]{2,1,0:T(8,128)S(1)}, u32[]{:S(2)}, u32[]{:S(2)}) %collective-permute-start.29) | collective-permute-done | bytes 8224 | tf_op jit(solution)/shard_map/ppermute | solution.py:478
  162.8 4.9 %collective-permute-done.30.other = f32[2,8,128]{2,1,0:T(8,128)S(1)} collective-permute-done((f32[2,8,128]{2,1,0:T(8,128)S(1)}, f32[2,8,128]{2,1,0:T(8,128)S(1)}, u32[]{:S(2)}, u32[]{:S(2)}) %collective-permute-start.30) | collective-permute-done | bytes 8224 | tf_op jit(solution)/shard_map/ppermute | solution.py:478
  167.7 4.6 %factor_stage.1 = (f32[32,32]{1,0:T(8,128)}, f32[32,32]{1,0:T(8,128)S(1)}) custom-call(f32[2,8,128]{2,1,0:T(8,128)S(1)} %merge.13.refs_0_), custom_call_target="tpu_custom_call" | custom-call | tf_op jit(solution)/shard_map/factor_stage/pallas_call | solution.py:510
  172.4 6.5 %basis_stage.1 = f32[32,32,8,256]{3,2,1,0:T(8,128)} custom-call(f32[32,32]{1,0:T(8,128)S(1)} %get-tuple-element.110.inverse, f32[8,32,8,256]{3,2,1,0:T(8,128)S(1)} %bitcast.13, f32[12,32,8,256]{3,2,1,0:T(8,128)S(1)} %bitcast.8, f32[12,32,8,256]{3,2,1,0:T(8,128)S(1)} %bitcast.10), custom_call_target="tpu_custom_call" | custom-call | flops 3221225472 | bytes 16777216 | tf_op jit(solution)/shard_map/basis_stage/pallas_call | solution.py:538
  (76 shorter events, 4.7 us)
Async XLA Ops:
  0.6 1.9 %copy-start.1 = (f32[8,32,256]{2,1,0:T(8,128)S(1)}, f32[8,32,256]{2,1,0:T(8,128)}, u32[]{:S(2)}) copy-start(f32[8,32,256]{2,1,0:T(8,128)} %scale.17) | copy-start | bytes 786436
  3.7 16.5 %collective-permute-start = (f32[8,120,256]{2,1,0:T(8,128)S(1)}, f32[8,120,256]{2,1,0:T(8,128)S(1)}, u32[]{:S(2)}, u32[]{:S(2)}) collective-permute-start(f32[8,120,256]{2,1,0:T(8,128)S(1)} %get-tuple-element.57), channel_id=1, source_target_pairs={{0,4},{4,0},{8,12},{12,8},{16,20},{20,16},{24,28},{28,24},{32,36},... | collective-permute-start | bytes 2949128 | tf_op jit(solution)/shard_map/ppermute | solution.py:552
  3.8 17.5 %collective-permute-start.1 = (f32[8,120,256]{2,1,0:T(8,128)S(1)}, f32[8,120,256]{2,1,0:T(8,128)S(1)}, u32[]{:S(2)}, u32[]{:S(2)}) collective-permute-start(f32[8,120,256]{2,1,0:T(8,128)S(1)} %get-tuple-element.58), channel_id=1, source_target_pairs={{4,8},{8,4},{12,16},{16,12},{20,24},{24,20},{28,32},{32,28},{36,40... | collective-permute-start | bytes 2949128 | tf_op jit(solution)/shard_map/ppermute | solution.py:552
  12.3 4.5 %copy-start.2 = (f32[256,512]{1,0:T(8,128)S(1)}, f32[256,512]{1,0:T(8,128)}, u32[]{:S(2)}) copy-start(f32[256,512]{1,0:T(8,128)} %constant.40.clone.by_in) | copy-start | bytes 1572868
  12.4 4.5 %copy-start.3 = (f32[256,512]{1,0:T(8,128)S(1)}, f32[256,512]{1,0:T(8,128)}, u32[]{:S(2)}) copy-start(f32[256,512]{1,0:T(8,128)} %constant.39.clone.by_out) | copy-start | bytes 1572868
  12.4 4.5 %copy-start.4 = (f32[256,256]{1,0:T(8,128)S(1)}, f32[256,256]{1,0:T(8,128)}, u32[]{:S(2)}) copy-start(f32[256,256]{1,0:T(8,128)} %constant.43.clone.same) | copy-start | bytes 786436
  12.4 4.5 %copy-start.5 = (f32[256,8]{1,0:T(8,128)S(1)}, f32[256,8]{1,0:T(8,128)}, u32[]{:S(2)}) copy-start(f32[256,8]{1,0:T(8,128)} %constant.42.clone.spread) | copy-start | bytes 24580
  12.4 4.5 %copy-start.6 = (f32[8,512]{1,0:T(8,128)S(1)}, f32[8,512]{1,0:T(8,128)}, u32[]{:S(2)}) copy-start(f32[8,512]{1,0:T(8,128)} %constant.41.clone.pick) | copy-start | bytes 49156
  12.4 4.5 %copy-start.7 = (f32[8,8]{1,0:T(8,128)S(1)}, f32[8,8]{1,0:T(8,128)}, u32[]{:S(2)}) copy-start(f32[8,8]{1,0:T(8,128)} %factor.1) | copy-start | bytes 772
  12.4 4.5 %copy-start.8 = (f32[8,8]{1,0:T(8,128)S(1)}, f32[8,8]{1,0:T(8,128)}, u32[]{:S(2)}) copy-start(f32[8,8]{1,0:T(8,128)} %mix.1) | copy-start | bytes 772
  13.9 26.9 %collective-permute-start.4 = (f32[12,120,256]{2,1,0:T(8,128)S(1)}, f32[12,120,256]{2,1,0:T(8,128)S(1)}, u32[]{:S(2)}, u32[]{:S(2)}) collective-permute-start(f32[12,120,256]{2,1,0:T(8,128)S(1)} %get-tuple-element.67), channel_id=1, source_target_pairs={{0,4},{4,0},{8,12},{12,8},{16,20},{20,16},{24,28},{28,24},{32,36},... | collective-permute-start | bytes 4423688 | tf_op jit(solution)/shard_map/ppermute | solution.py:552
  14.0 29.8 %collective-permute-start.5 = (f32[12,120,256]{2,1,0:T(8,128)S(1)}, f32[12,120,256]{2,1,0:T(8,128)S(1)}, u32[]{:S(2)}, u32[]{:S(2)}) collective-permute-start(f32[12,120,256]{2,1,0:T(8,128)S(1)} %get-tuple-element.68), channel_id=1, source_target_pairs={{4,8},{8,4},{12,16},{16,12},{20,24},{24,20},{28,32},{32,28},{36,40... | collective-permute-start | bytes 4423688 | tf_op jit(solution)/shard_map/ppermute | solution.py:552
  20.2 16.1 %copy-start.13 = (bf16[256,768]{1,0:T(8,128)(2,1)}, bf16[256,768]{1,0:T(8,128)(2,1)S(1)}, u32[]{:S(2)}) copy-start(bf16[256,768]{1,0:T(8,128)(2,1)S(1)} %get-tuple-element.65.back) | copy-start | bytes 1179652
  20.2 23.7 %copy-start.9 = (bf16[256,1536]{1,0:T(8,128)(2,1)}, bf16[256,1536]{1,0:T(8,128)(2,1)S(1)}, u32[]{:S(2)}) copy-start(bf16[256,1536]{1,0:T(8,128)(2,1)S(1)} %get-tuple-element.59.matrix) | copy-start | bytes 2359300
  20.2 40.8 %copy-start.11 = (bf16[256,768]{1,0:T(8,128)(2,1)}, bf16[256,768]{1,0:T(8,128)(2,1)S(1)}, u32[]{:S(2)}) copy-start(bf16[256,768]{1,0:T(8,128)(2,1)S(1)} %get-tuple-element.64.mix) | copy-start | bytes 1179652
  21.3 15.0 %copy-start = (bf16[8,1024,256]{2,1,0:T(8,128)(2,1)S(1)}, bf16[8,1024,256]{2,1,0:T(8,128)(2,1)}, u32[]{:S(2)}) copy-start(bf16[8,1024,256]{2,1,0:T(8,128)(2,1)} %constant.38.clone.table) | copy-start | bytes 12582916
  24.8 11.5 %copy-start.15 = (f32[8,32,256]{2,1,0:T(8,128)S(1)}, f32[8,32,256]{2,1,0:T(8,128)}, u32[]{:S(2)}) copy-start(f32[8,32,256]{2,1,0:T(8,128)} %weights.5) | copy-start | bytes 786436
  24.8 7.1 %collective-permute-start.2 = (f32[8,32,128]{2,1,0:T(8,128)S(1)}, f32[8,32,128]{2,1,0:T(8,128)S(1)}, u32[]{:S(2)}, u32[]{:S(2)}) collective-permute-start(f32[8,32,128]{2,1,0:T(8,128)S(1)} %get-tuple-element.62), channel_id=1, source_target_pairs={{0,1},{1,0},{2,3},{3,2},{4,5},{5,4},{6,7},{7,6},{8,9},{9,8},{10,11... | collective-permute-start | bytes 393224 | tf_op jit(solution)/shard_map/ppermute | solution.py:552
  25.0 11.3 %collective-permute-start.3 = (f32[8,32,128]{2,1,0:T(8,128)S(1)}, f32[8,32,128]{2,1,0:T(8,128)S(1)}, u32[]{:S(2)}, u32[]{:S(2)}) collective-permute-start(f32[8,32,128]{2,1,0:T(8,128)S(1)} %get-tuple-element.63), channel_id=1, source_target_pairs={{1,2},{2,1},{5,6},{6,5},{9,10},{10,9},{13,14},{14,13},{17,18},{18,... | collective-permute-start | bytes 393224 | tf_op jit(solution)/shard_map/ppermute | solution.py:552
  31.8 38.8 %collective-permute-start.11 = (f32[12,120,256]{2,1,0:T(8,128)S(1)}, f32[12,120,256]{2,1,0:T(8,128)S(1)}, u32[]{:S(2)}, u32[]{:S(2)}) collective-permute-start(f32[12,120,256]{2,1,0:T(8,128)S(1)} %get-tuple-element.79), channel_id=1, source_target_pairs={{0,4},{4,0},{8,12},{12,8},{16,20},{20,16},{24,28},{28,24},{32,36},... | collective-permute-start | bytes 4423688 | tf_op jit(solution)/shard_map/ppermute | solution.py:552
  31.9 38.7 %collective-permute-start.12 = (f32[12,120,256]{2,1,0:T(8,128)S(1)}, f32[12,120,256]{2,1,0:T(8,128)S(1)}, u32[]{:S(2)}, u32[]{:S(2)}) collective-permute-start(f32[12,120,256]{2,1,0:T(8,128)S(1)} %get-tuple-element.80), channel_id=1, source_target_pairs={{4,8},{8,4},{12,16},{16,12},{20,24},{24,20},{28,32},{32,28},{36,40... | collective-permute-start | bytes 4423688 | tf_op jit(solution)/shard_map/ppermute | solution.py:552
  40.7 7.8 %collective-permute-start.6 = (f32[8,32,128]{2,1,0:T(8,128)S(1)}, f32[8,32,128]{2,1,0:T(8,128)S(1)}, u32[]{:S(2)}, u32[]{:S(2)}) collective-permute-start(f32[8,32,128]{2,1,0:T(8,128)S(1)} %get-tuple-element.71), channel_id=1, source_target_pairs={{0,1},{1,0},{2,3},{3,2},{4,5},{5,4},{6,7},{7,6},{8,9},{9,8},{10,11... | collective-permute-start | bytes 393224 | tf_op jit(solution)/shard_map/ppermute | solution.py:552
  40.8 7.7 %collective-permute-start.7 = (f32[8,32,128]{2,1,0:T(8,128)S(1)}, f32[8,32,128]{2,1,0:T(8,128)S(1)}, u32[]{:S(2)}, u32[]{:S(2)}) collective-permute-start(f32[8,32,128]{2,1,0:T(8,128)S(1)} %get-tuple-element.72), channel_id=1, source_target_pairs={{1,2},{2,1},{5,6},{6,5},{9,10},{10,9},{13,14},{14,13},{17,18},{18,... | collective-permute-start | bytes 393224 | tf_op jit(solution)/shard_map/ppermute | solution.py:552
  48.5 12.4 %copy-start.14 = (bf16[256,768]{1,0:T(8,128)(2,1)S(1)}, bf16[256,768]{1,0:T(8,128)(2,1)}, u32[]{:S(2)}) copy-start(bf16[256,768]{1,0:T(8,128)(2,1)} %copy-done.13) | copy-start | bytes 1179652
  51.5 9.5 %collective-permute-start.10 = (f32[8,120,256]{2,1,0:T(8,128)S(1)}, f32[8,120,256]{2,1,0:T(8,128)S(1)}, u32[]{:S(2)}, u32[]{:S(2)}) collective-permute-start(f32[8,120,256]{2,1,0:T(8,128)S(1)} %get-tuple-element.77), channel_id=1, source_target_pairs={{0,4},{4,0},{8,12},{12,8},{16,20},{20,16},{24,28},{28,24},{32,36},... | collective-permute-start | bytes 2949128 | tf_op jit(solution)/shard_map/ppermute | solution.py:552
  51.7 7.3 %collective-permute-start.8 = (f32[12,32,128]{2,1,0:T(8,128)S(1)}, f32[12,32,128]{2,1,0:T(8,128)S(1)}, u32[]{:S(2)}, u32[]{:S(2)}) collective-permute-start(f32[12,32,128]{2,1,0:T(8,128)S(1)} %get-tuple-element.75), channel_id=1, source_target_pairs={{0,1},{1,0},{2,3},{3,2},{4,5},{5,4},{6,7},{7,6},{8,9},{9,8},{10,11... | collective-permute-start | bytes 589832 | tf_op jit(solution)/shard_map/ppermute | solution.py:552
  51.8 9.1 %collective-permute-start.9 = (f32[12,32,128]{2,1,0:T(8,128)S(1)}, f32[12,32,128]{2,1,0:T(8,128)S(1)}, u32[]{:S(2)}, u32[]{:S(2)}) collective-permute-start(f32[12,32,128]{2,1,0:T(8,128)S(1)} %get-tuple-element.76), channel_id=1, source_target_pairs={{1,2},{2,1},{5,6},{6,5},{9,10},{10,9},{13,14},{14,13},{17,18},{18,... | collective-permute-start | bytes 589832 | tf_op jit(solution)/shard_map/ppermute | solution.py:552
  61.0 9.7 %copy-start.10 = (bf16[256,1536]{1,0:T(8,128)(2,1)S(1)}, bf16[256,1536]{1,0:T(8,128)(2,1)}, u32[]{:S(2)}) copy-start(bf16[256,1536]{1,0:T(8,128)(2,1)} %copy-done.9) | copy-start | bytes 2359300
  67.7 7.5 %collective-permute-start.13 = (f32[12,32,128]{2,1,0:T(8,128)S(1)}, f32[12,32,128]{2,1,0:T(8,128)S(1)}, u32[]{:S(2)}, u32[]{:S(2)}) collective-permute-start(f32[12,32,128]{2,1,0:T(8,128)S(1)} %get-tuple-element.83), channel_id=1, source_target_pairs={{0,1},{1,0},{2,3},{3,2},{4,5},{5,4},{6,7},{7,6},{8,9},{9,8},{10,11... | collective-permute-start | bytes 589832 | tf_op jit(solution)/shard_map/ppermute | solution.py:552
  67.8 8.3 %collective-permute-start.14 = (f32[12,32,128]{2,1,0:T(8,128)S(1)}, f32[12,32,128]{2,1,0:T(8,128)S(1)}, u32[]{:S(2)}, u32[]{:S(2)}) collective-permute-start(f32[12,32,128]{2,1,0:T(8,128)S(1)} %get-tuple-element.84), channel_id=1, source_target_pairs={{1,2},{2,1},{5,6},{6,5},{9,10},{10,9},{13,14},{14,13},{17,18},{18,... | collective-permute-start | bytes 589832 | tf_op jit(solution)/shard_map/ppermute | solution.py:552
  76.2 14.9 %copy-start.12 = (bf16[256,768]{1,0:T(8,128)(2,1)S(1)}, bf16[256,768]{1,0:T(8,128)(2,1)}, u32[]{:S(2)}) copy-start(bf16[256,768]{1,0:T(8,128)(2,1)} %copy-done.11) | copy-start | bytes 1179652
  79.7 11.3 %collective-permute-start.17 = (f32[12,120,256]{2,1,0:T(8,128)S(1)}, f32[12,120,256]{2,1,0:T(8,128)S(1)}, u32[]{:S(2)}, u32[]{:S(2)}) collective-permute-start(f32[12,120,256]{2,1,0:T(8,128)S(1)} %get-tuple-element.89), channel_id=1, source_target_pairs={{0,4},{4,0},{8,12},{12,8},{16,20},{20,16},{24,28},{28,24},{32,36},... | collective-permute-start | bytes 4423688 | tf_op jit(solution)/shard_map/ppermute | solution.py:552
  79.8 20.8 %collective-permute-start.18 = (f32[8,120,256]{2,1,0:T(8,128)S(1)}, f32[8,120,256]{2,1,0:T(8,128)S(1)}, u32[]{:S(2)}, u32[]{:S(2)}) collective-permute-start(f32[8,120,256]{2,1,0:T(8,128)S(1)} %get-tuple-element.92), channel_id=1, source_target_pairs={{4,8},{8,4},{12,16},{16,12},{20,24},{24,20},{28,32},{32,28},{36,40... | collective-permute-start | bytes 2949128 | tf_op jit(solution)/shard_map/ppermute | solution.py:552
  82.6 7.5 %collective-permute-start.15 = (f32[12,32,128]{2,1,0:T(8,128)S(1)}, f32[12,32,128]{2,1,0:T(8,128)S(1)}, u32[]{:S(2)}, u32[]{:S(2)}) collective-permute-start(f32[12,32,128]{2,1,0:T(8,128)S(1)} %get-tuple-element.87), channel_id=1, source_target_pairs={{0,1},{1,0},{2,3},{3,2},{4,5},{5,4},{6,7},{7,6},{8,9},{9,8},{10,11... | collective-permute-start | bytes 589832 | tf_op jit(solution)/shard_map/ppermute | solution.py:552
  82.7 8.4 %collective-permute-start.16 = (f32[12,32,128]{2,1,0:T(8,128)S(1)}, f32[12,32,128]{2,1,0:T(8,128)S(1)}, u32[]{:S(2)}, u32[]{:S(2)}) collective-permute-start(f32[12,32,128]{2,1,0:T(8,128)S(1)} %get-tuple-element.88), channel_id=1, source_target_pairs={{1,2},{2,1},{5,6},{6,5},{9,10},{10,9},{13,14},{14,13},{17,18},{18,... | collective-permute-start | bytes 589832 | tf_op jit(solution)/shard_map/ppermute | solution.py:552
  85.5 27.7 %collective-permute-start.21 = (f32[12,120,256]{2,1,0:T(8,128)S(1)}, f32[12,120,256]{2,1,0:T(8,128)S(1)}, u32[]{:S(2)}, u32[]{:S(2)}) collective-permute-start(f32[12,120,256]{2,1,0:T(8,128)S(1)} %get-tuple-element.100), channel_id=1, source_target_pairs={{4,8},{8,4},{12,16},{16,12},{20,24},{24,20},{28,32},{32,28},{36,40... | collective-permute-start | bytes 4423688 | tf_op jit(solution)/shard_map/ppermute | solution.py:552
  97.8 5.7 %collective-permute-start.19 = (f32[12,32,128]{2,1,0:T(8,128)S(1)}, f32[12,32,128]{2,1,0:T(8,128)S(1)}, u32[]{:S(2)}, u32[]{:S(2)}) collective-permute-start(f32[12,32,128]{2,1,0:T(8,128)S(1)} %get-tuple-element.96), channel_id=1, source_target_pairs={{0,1},{1,0},{2,3},{3,2},{4,5},{5,4},{6,7},{7,6},{8,9},{9,8},{10,11... | collective-permute-start | bytes 589832 | tf_op jit(solution)/shard_map/ppermute | solution.py:552
  97.9 7.6 %collective-permute-start.20 = (f32[12,32,128]{2,1,0:T(8,128)S(1)}, f32[12,32,128]{2,1,0:T(8,128)S(1)}, u32[]{:S(2)}, u32[]{:S(2)}) collective-permute-start(f32[12,32,128]{2,1,0:T(8,128)S(1)} %get-tuple-element.97), channel_id=1, source_target_pairs={{1,2},{2,1},{5,6},{6,5},{9,10},{10,9},{13,14},{14,13},{17,18},{18,... | collective-permute-start | bytes 589832 | tf_op jit(solution)/shard_map/ppermute | solution.py:552
  109.0 11.9 %collective-permute-start.22 = (f32[12,120,256]{2,1,0:T(8,128)S(1)}, f32[12,120,256]{2,1,0:T(8,128)S(1)}, u32[]{:S(2)}, u32[]{:S(2)}) collective-permute-start(f32[12,120,256]{2,1,0:T(8,128)S(1)} %get-tuple-element.107), channel_id=1, source_target_pairs={{0,4},{4,0},{8,12},{12,8},{16,20},{20,16},{24,28},{28,24},{32,36},... | collective-permute-start | bytes 4423688 | tf_op jit(solution)/shard_map/ppermute | solution.py:552
  109.1 22.8 %collective-permute-start.23 = (f32[12,120,256]{2,1,0:T(8,128)S(1)}, f32[12,120,256]{2,1,0:T(8,128)S(1)}, u32[]{:S(2)}, u32[]{:S(2)}) collective-permute-start(f32[12,120,256]{2,1,0:T(8,128)S(1)} %get-tuple-element.108), channel_id=1, source_target_pairs={{4,8},{8,4},{12,16},{16,12},{20,24},{24,20},{28,32},{32,28},{36,40... | collective-permute-start | bytes 4423688 | tf_op jit(solution)/shard_map/ppermute | solution.py:552
  139.6 1.2 collective-permute-start.24
  140.8 3.7 %collective-permute-start.25 = (f32[2,8,128]{2,1,0:T(8,128)S(1)}, f32[2,8,128]{2,1,0:T(8,128)S(1)}, u32[]{:S(2)}, u32[]{:S(2)}) collective-permute-start(f32[2,8,128]{2,1,0:T(8,128)S(1)} %merge.7.mine), channel_id=1, source_target_pairs={{0,8},{4,12},{8,0},{12,4},{16,24},{20,28},{24,16},{28,20},{32,40},... | collective-permute-start | bytes 24584 | tf_op jit(solution)/shard_map/ppermute | solution.py:478
  144.5 5.2 %collective-permute-start.26 = (f32[2,8,128]{2,1,0:T(8,128)S(1)}, f32[2,8,128]{2,1,0:T(8,128)S(1)}, u32[]{:S(2)}, u32[]{:S(2)}) collective-permute-start(f32[2,8,128]{2,1,0:T(8,128)S(1)} %merge.8.mine), channel_id=1, source_target_pairs={{0,16},{4,20},{8,24},{12,28},{16,0},{20,4},{24,8},{28,12},{32,48},... | collective-permute-start | bytes 24584 | tf_op jit(solution)/shard_map/ppermute | solution.py:478
  149.8 3.7 %collective-permute-start.27 = (f32[2,8,128]{2,1,0:T(8,128)S(1)}, f32[2,8,128]{2,1,0:T(8,128)S(1)}, u32[]{:S(2)}, u32[]{:S(2)}) collective-permute-start(f32[2,8,128]{2,1,0:T(8,128)S(1)} %merge.9.mine), channel_id=1, source_target_pairs={{0,32},{4,36},{8,40},{12,44},{16,48},{20,52},{24,56},{28,60},{32,0... | collective-permute-start | bytes 24584 | tf_op jit(solution)/shard_map/ppermute | solution.py:478
  153.5 5.2 %collective-permute-start.28 = (f32[2,8,128]{2,1,0:T(8,128)S(1)}, f32[2,8,128]{2,1,0:T(8,128)S(1)}, u32[]{:S(2)}, u32[]{:S(2)}) collective-permute-start(f32[2,8,128]{2,1,0:T(8,128)S(1)} %merge.10.mine), channel_id=1, source_target_pairs={{0,64},{4,68},{8,72},{12,76},{16,80},{20,84},{24,88},{28,92},{32,9... | collective-permute-start | bytes 24584 | tf_op jit(solution)/shard_map/ppermute | solution.py:478
  158.8 3.7 %collective-permute-start.29 = (f32[2,8,128]{2,1,0:T(8,128)S(1)}, f32[2,8,128]{2,1,0:T(8,128)S(1)}, u32[]{:S(2)}, u32[]{:S(2)}) collective-permute-start(f32[2,8,128]{2,1,0:T(8,128)S(1)} %merge.11.mine), channel_id=1, source_target_pairs={{0,1},{1,0},{2,3},{3,2},{4,5},{5,4},{6,7},{7,6},{8,9},{9,8},{10,11... | collective-permute-start | bytes 24584 | tf_op jit(solution)/shard_map/ppermute | solution.py:478
  162.5 5.2 %collective-permute-start.30 = (f32[2,8,128]{2,1,0:T(8,128)S(1)}, f32[2,8,128]{2,1,0:T(8,128)S(1)}, u32[]{:S(2)}, u32[]{:S(2)}) collective-permute-start(f32[2,8,128]{2,1,0:T(8,128)S(1)} %merge.12.mine), channel_id=1, source_target_pairs={{0,2},{1,3},{2,0},{3,1},{4,6},{5,7},{6,4},{7,5},{8,10},{9,11},{10,... | collective-permute-start | bytes 24584 | tf_op jit(solution)/shard_map/ppermute | solution.py:478

commit v3 on v2

--- a/solution.py
+++ b/solution.py
@@ -98,7 +98,7 @@
     after[1] = side[1]
 
 
-def params(mib=24):
+def params(mib=20):
     return pltpu.CompilerParams(vmem_limit_bytes=mib * 2**20)
 
 
@@ -332,6 +332,25 @@
     )(side, tiles, inner, outer, matrix, signs, scale)
 
 
+def sketch_main_kernel(side, tiles, matrix, out, after):
+    hand_on(side, after)
+
+    @pl.loop(0, out.shape[0], step=PER)
+    def _(start):
+        for p in range(PER):
+            out[start + p] = dot(matrix[:, 0:768], stacked(tiles[start + p].reshape(256, COLS)))
+
+
+def sketch_main_stage(side, tiles, matrix):
+    count = tiles.shape[0]
+    return pl.pallas_call(
+        sketch_main_kernel, out_shape=(jax.ShapeDtypeStruct((count, 256, COLS), F32), SIDE),
+        in_specs=[SMEM, VMEM, VMEM], out_specs=(VMEM, SMEM),
+        compiler_params=params(), cost_estimate=cost(count * 256 * 1536 * 256, count * 2**19),
+        name="sketch_main_stage",
+    )(side, tiles, matrix)
+
+
 def gather_group(refs, g):
     return jnp.concatenate([r[:, g].reshape(-1, COLS) for r in refs], axis=0)
 
@@ -379,14 +398,24 @@
     )(side, *chunks)
 
 
-def gram_kernel(early, *refs):
-    chunks, out, total = refs[:-2], refs[-2], refs[-1]
+def gram_kernel(early, main, inner, outer, matrix, signs, scale, *refs):
+    chunks, out, sketch, total = refs[:-3], refs[-3], refs[-2], refs[-1]
     total[...] = jnp.zeros_like(total)
     done = early.shape[0]
 
-    @pl.loop(0, chunks[0].shape[1], step=8)
+    @pl.loop(0, main.shape[0], step=PER)
+    def _(start):
+        for p in range(PER):
+            spot = start + p
+            mixed = main[spot] + dot(matrix[:, 768:], stacked(halo_rows(outer, inner, spot)))
+            values = scale[...] * mixed.reshape(BANDS, ROWS, COLS) + signed(signs[spot])
+            sketch[spot] = values.reshape(BANDS * ROWS // 8, 8, COLS)
+
+    whole = chunks + (sketch,)
+
+    @pl.loop(0, sketch.shape[1], step=8)
     def _(g):
-        values = jnp.concatenate([gather_group(chunks, g + j) for j in range(8)], axis=1)
+        values = jnp.concatenate([gather_group(whole, g + j) for j in range(8)], axis=1)
         high, low = split(values)
         new_high, new_low = high[8 * done:], low[8 * done:]
         total[...] += dot_nt(jnp.concatenate([new_high, new_low], axis=0), high)
@@ -406,14 +435,16 @@
     out[1] = jnp.zeros(out.shape[1:], F32)
 
 
-def gram_stage(early, chunks):
-    probes = sum(c.shape[0] for c in chunks)
-    return pl.pallas_call(
-        gram_kernel, out_shape=jax.ShapeDtypeStruct((2, 8, 128), F32),
-        in_specs=[VMEM] * (1 + len(chunks)), out_specs=VMEM,
-        scratch_shapes=[pltpu.VMEM((16 * chunks[-1].shape[0], 8 * probes), F32)],
+def gram_stage(early, main, inner, outer, matrix, signs, scale, chunks):
+    count = main.shape[0]
+    probes = sum(c.shape[0] for c in chunks) + count
+    grouped = jax.ShapeDtypeStruct((count, BANDS * ROWS // 8, 8, COLS), F32)
+    return pl.pallas_call(
+        gram_kernel, out_shape=(jax.ShapeDtypeStruct((2, 8, 128), F32), grouped),
+        in_specs=[VMEM] * (7 + len(chunks)), out_specs=(VMEM, VMEM),
+        scratch_shapes=[pltpu.VMEM((16 * count, 8 * probes), F32)],
         compiler_params=params(), cost_estimate=cost(32 * 2 * 2 * 256**3, 2**23), name="gram_stage",
-    )(early, *chunks)
+    )(early, main, inner, outer, matrix, signs, scale, *chunks)
 
 
 def group_blocks(chunks):
@@ -598,10 +629,13 @@
         side = finish(k, side)
     side = last_column(last, side)
     side = finish(last - 1, side)
-    early, side = early_gram_stage(side, [group(k) for k in range(last)])
-    side = finish(last, side)
-    grouped = [group(k) for k in range(last + 1)]
-    gram = sum_over(sum_over(gram_stage(early, grouped), "row"), "col")
+    grouped = [group(k) for k in range(last)]
+    early, side = early_gram_stage(side, grouped)
+    tiles, *edge_rows = state[last]
+    main, side = sketch_main_stage(side, tiles, last_m)
+    gram, latest = gram_stage(early, main, *edge_rows, last_m, signs[last], prior_scale, grouped)
+    grouped.append(latest)
+    gram = sum_over(sum_over(gram, "row"), "col")
     total = BANDS * ROWS * COLS * lax.axis_size("row") * lax.axis_size("col")
     r_factor, inverse = factor_stage(gram, probes, float(np.sqrt(np.float32(total))))
     basis = basis_stage(inverse, grouped)

time: 179 us -> 179 us (level)
  waiting for transfers between devices: 49 us -> 46.7 us
    pallas_call x1 -> x2, Pallas kernels: 3.92 us -> 8.32 us  [the longest x1 5.97 us: gram_stage(): pl.pallas_call(gram_kernel, out_shape=(jax.ShapeDtypeStruct((2, 8, 128),...]
    pallas_call x3 -> x2, Pallas kernels: 10.1 us -> 6.37 us  [sketch_stage(): pl.pallas_call(sketch_kernel, out_shape=(jax.ShapeDtypeStruct((count, BAN...]
    ppermute x24, waiting for transfers between devices: 23.2 us -> 20.9 us  [swap(): return (lax.ppermute(inner, axis, pairs), lax.ppermute(outer, axis, others))]
  transfers between devices with their start and end apart: 31 -> 31, of which waited for: 16 -> 16; matrix products, arithmetic and copies ran while one was open for 2% -> 2% of each run, Pallas kernels for 30% -> 32%
where the time goes in v3:
time: 179 us; the launch traced here: 178 us
  Pallas kernels  78.9 us (44%)
  waiting for transfers between devices  46.7 us (26%)
  starting transfers between devices  45.7 us (26%)
  local copies, waits for them, and re-layouts  5.47 us (3%)
    ppermute x24, starting transfers between devices, swap(): return (lax.ppermute(inner, axis, pairs), lax.ppermute(outer, axis, others))  43.5 us
    ppermute x7, waiting for transfers between devices, sum_over(): lax.ppermute(value, axis, [(i, i ^ bit) for i in range(count)])  25.8 us
    ppermute x24, waiting for transfers between devices, swap(): return (lax.ppermute(inner, axis, pairs), lax.ppermute(outer, axis, others))  20.9 us
    pallas_call x3, Pallas kernels, middle_stage(): pl.pallas_call(middle_kernel, out_shape=(whole, packed, packed, SIDE), in...  18.7 us
    pallas_call x3, Pallas kernels, first_stage(): pl.pallas_call(first_kernel, out_shape=(jax.ShapeDtypeStruct((count, BAND...  12.6 us
    pallas_call x3, Pallas kernels, last_column_stage(): pl.pallas_call(last_column_kernel, out_shape=(whole, edge, edge, SIDE), i...  10.2 us
    pallas_call x1, Pallas kernels, basis_stage(): pl.pallas_call(basis_kernel, grid=(groups // 8,), out_shape=jax.ShapeDtyp...  6.62 us
    pallas_call x2, Pallas kernels, sketch_stage(): pl.pallas_call(sketch_kernel, out_shape=(jax.ShapeDtypeStruct((count, BAN...  6.37 us
  transfers between devices with their start and end apart: 31, of which 16 were waited for; matrix products, arithmetic and copies ran while one was open for 2% of the time, Pallas kernels for 32%

profile of v3, /device:TPU:56, one launch (start us, length us, event | category | flops | bytes accessed | tf_op | source)
XLA Modules:
  0.0 178.1 jit_solution(17936935826771467432)
XLA Ops:
  0.7 1.8 slice.9.signs
  2.5 1.2 edges.3
  3.8 4.9 %collective-permute-start.1 = (f32[8,120,256]{2,1,0:T(8,128)S(1)}, f32[8,120,256]{2,1,0:T(8,128)S(1)}, u32[]{:S(2)}, u32[]{:S(2)}) collective-permute-start(f32[8,120,256]{2,1,0:T(8,128)S(1)} %get-tuple-element.60), channel_id=1, source_target_pairs={{4,8},{8,4},{12,16},{16,12},{20,24},{24,20},{28,32},{32,28},{36,40... | collective-permute-start | bytes 2949128 | tf_op jit(solution)/shard_map/ppermute | solution.py:583
  8.7 3.6 %fusion = (s32[12,8,32,256]{3,2,1,0:T(8,128)S(1)}, s32[12,8,32,256]{3,2,1,0:T(8,128)S(1)}) fusion(s32[32,8,32,256]{3,2,1,0:T(8,128)} %param.11), kind=kLoop, calls=%fused_computation.1 | loop fusion | bytes 12582912 | tf_op jit(solution)/shard_map/slice | solution.py:591
  12.5 1.5 edges.4
  14.1 2.8 %collective-permute-start.5 = (f32[12,120,256]{2,1,0:T(8,128)S(1)}, f32[12,120,256]{2,1,0:T(8,128)S(1)}, u32[]{:S(2)}, u32[]{:S(2)}) collective-permute-start(f32[12,120,256]{2,1,0:T(8,128)S(1)} %get-tuple-element.70), channel_id=1, source_target_pairs={{4,8},{8,4},{12,16},{16,12},{20,24},{24,20},{28,32},{32,28},{36,40... | collective-permute-start | bytes 4423688 | tf_op jit(solution)/shard_map/ppermute | solution.py:583
  17.0 3.2 %prepare.1 = (bf16[256,1536]{1,0:T(8,128)(2,1)S(1)}, bf16[256,1536]{1,0:T(8,128)(2,1)S(1)}, bf16[256,768]{1,0:T(8,128)(2,1)S(1)}, bf16[256,768]{1,0:T(8,128)(2,1)S(1)}) custom-call(s32[2]{0:T(128)S(1)} %pad_add_fusion.side, f32[8,8]{1,0:T(8,128)S(1)} %copy-done.7, f32[8,8]{1,0:T(8,128)S(1)} %copy-done.8, f32[256,512]{1,0:T(8,128)S(1)} %copy-done.3, ...), custom_call_target="tpu_custom_call" | custom-call | tf_op jit(solution)/shard_map/prepare/pallas_call | solution.py:139
  20.2 1.1 collective-permute-done.1.outer
  21.3 3.4 %first_stage.3 = (f32[8,8,32,256]{3,2,1,0:T(8,128)S(1)}, f32[8,32,128]{2,1,0:T(8,128)S(1)}, f32[8,32,128]{2,1,0:T(8,128)S(1)}, s32[2]{0:T(128)S(1)}) custom-call(s32[2]{0:T(128)S(1)} %pad_add_fusion.side, s32[8,8,32,256]{3,2,1,0:T(8,128)S(1)} %slice.9.signs, f32[8,32,256]{2,1,0:T(8,128)S(1)} %copy-done.1, f32[8,120,256]{2,1,0:T(8,128)S(1)} %collective-permute-done.inner, ...), custom_call_target="tpu_custom_call" | custom-call | flops 1610612736 | bytes 8388608 | tf_op jit(solution)/shard_map/first_stage/pallas_call | solution.py:220
  24.9 5.3 %collective-permute-start.3 = (f32[8,32,128]{2,1,0:T(8,128)S(1)}, f32[8,32,128]{2,1,0:T(8,128)S(1)}, u32[]{:S(2)}, u32[]{:S(2)}) collective-permute-start(f32[8,32,128]{2,1,0:T(8,128)S(1)} %get-tuple-element.65), channel_id=1, source_target_pairs={{1,2},{2,1},{5,6},{6,5},{9,10},{10,9},{13,14},{14,13},{17,18},{18,... | collective-permute-start | bytes 393224 | tf_op jit(solution)/shard_map/ppermute | solution.py:583
  30.3 1.5 edges.5
  31.9 4.4 %collective-permute-start.12 = (f32[12,120,256]{2,1,0:T(8,128)S(1)}, f32[12,120,256]{2,1,0:T(8,128)S(1)}, u32[]{:S(2)}, u32[]{:S(2)}) collective-permute-start(f32[12,120,256]{2,1,0:T(8,128)S(1)} %get-tuple-element.82), channel_id=1, source_target_pairs={{4,8},{8,4},{12,16},{16,12},{20,24},{24,20},{28,32},{32,28},{36,40... | collective-permute-start | bytes 4423688 | tf_op jit(solution)/shard_map/ppermute | solution.py:583
  36.3 4.6 %middle_stage.3 = (f32[8,8,32,256]{3,2,1,0:T(8,128)S(1)}, f32[8,32,128]{2,1,0:T(8,128)S(1)}, f32[8,32,128]{2,1,0:T(8,128)S(1)}, s32[2]{0:T(128)S(1)}) custom-call(s32[2]{0:T(128)S(1)} %get-tuple-element.62.side.ahead, f32[8,8,32,256]{3,2,1,0:T(8,128)S(1)} %get-tuple-element.63.tiles, f32[8,32,128]{2,1,0:T(8,128)S(1)} %collective-permute-done.2.near, ...), custom_call_target="tpu_custom_call" | custom-call | flops 2684354560 | bytes 8388608 | tf_op jit(solution)/shard_map/middle_stage/pallas_call | solution.py:271
  40.9 3.0 %collective-permute-start.7 = (f32[8,32,128]{2,1,0:T(8,128)S(1)}, f32[8,32,128]{2,1,0:T(8,128)S(1)}, u32[]{:S(2)}, u32[]{:S(2)}) collective-permute-start(f32[8,32,128]{2,1,0:T(8,128)S(1)} %get-tuple-element.74), channel_id=1, source_target_pairs={{1,2},{2,1},{5,6},{6,5},{9,10},{10,9},{13,14},{14,13},{17,18},{18,... | collective-permute-start | bytes 393224 | tf_op jit(solution)/shard_map/ppermute | solution.py:583
  44.0 4.6 %first_stage.4 = (f32[12,8,32,256]{3,2,1,0:T(8,128)S(1)}, f32[12,32,128]{2,1,0:T(8,128)S(1)}, f32[12,32,128]{2,1,0:T(8,128)S(1)}, s32[2]{0:T(128)S(1)}) custom-call(s32[2]{0:T(128)S(1)} %get-tuple-element.68.side, s32[12,8,32,256]{3,2,1,0:T(8,128)S(1)} %get-tuple-element.117.signs, f32[8,32,256]{2,1,0:T(8,128)S(1)} %copy-done.1, ...), custom_call_target="tpu_custom_call" | custom-call | flops 2415919104 | bytes 12582912 | tf_op jit(solution)/shard_map/first_stage/pallas_call | solution.py:220
  48.6 2.9 %last_column_stage.3 = (f32[8,8,32,256]{3,2,1,0:T(8,128)S(1)}, f32[8,120,256]{2,1,0:T(8,128)S(1)}, f32[8,120,256]{2,1,0:T(8,128)S(1)}, s32[2]{0:T(128)S(1)}) custom-call(s32[2]{0:T(128)S(1)} %get-tuple-element.71.side, f32[8,8,32,256]{3,2,1,0:T(8,128)S(1)} %get-tuple-element.72.tiles, f32[8,32,128]{2,1,0:T(8,128)S(1)} %collective-permute-done.6.near, ...), custom_call_target="tpu_custom_call" | custom-call | flops 1073741824 | bytes 8388608 | tf_op jit(solution)/shard_map/last_column_stage/pallas_call | solution.py:303
  51.9 2.8 %collective-permute-start.9 = (f32[12,32,128]{2,1,0:T(8,128)S(1)}, f32[12,32,128]{2,1,0:T(8,128)S(1)}, u32[]{:S(2)}, u32[]{:S(2)}) collective-permute-start(f32[12,32,128]{2,1,0:T(8,128)S(1)} %get-tuple-element.78), channel_id=1, source_target_pairs={{1,2},{2,1},{5,6},{6,5},{9,10},{10,9},{13,14},{14,13},{17,18},{18,... | collective-permute-start | bytes 589832 | tf_op jit(solution)/shard_map/ppermute | solution.py:583
  54.8 4.4 %collective-permute-done.8.near = f32[12,32,128]{2,1,0:T(8,128)S(1)} collective-permute-done((f32[12,32,128]{2,1,0:T(8,128)S(1)}, f32[12,32,128]{2,1,0:T(8,128)S(1)}, u32[]{:S(2)}, u32[]{:S(2)}) %collective-permute-start.8) | collective-permute-done | bytes 196640 | tf_op jit(solution)/shard_map/ppermute | solution.py:583
  59.2 1.9 %collective-permute-done.9.far = f32[12,32,128]{2,1,0:T(8,128)S(1)} collective-permute-done((f32[12,32,128]{2,1,0:T(8,128)S(1)}, f32[12,32,128]{2,1,0:T(8,128)S(1)}, u32[]{:S(2)}, u32[]{:S(2)}) %collective-permute-start.9) | collective-permute-done | bytes 196640 | tf_op jit(solution)/shard_map/ppermute | solution.py:583
  61.1 7.1 %middle_stage.4 = (f32[12,8,32,256]{3,2,1,0:T(8,128)S(1)}, f32[12,32,128]{2,1,0:T(8,128)S(1)}, f32[12,32,128]{2,1,0:T(8,128)S(1)}, s32[2]{0:T(128)S(1)}) custom-call(s32[2]{0:T(128)S(1)} %get-tuple-element.75.side, f32[12,8,32,256]{3,2,1,0:T(8,128)S(1)} %get-tuple-element.76.tiles, f32[12,32,128]{2,1,0:T(8,128)S(1)} %collective-permute-done.8.near, ...), custom_call_target="tpu_custom_call" | custom-call | flops 4026531840 | bytes 12582912 | tf_op jit(solution)/shard_map/middle_stage/pallas_call | solution.py:271
  68.2 2.8 %collective-permute-start.14 = (f32[12,32,128]{2,1,0:T(8,128)S(1)}, f32[12,32,128]{2,1,0:T(8,128)S(1)}, u32[]{:S(2)}, u32[]{:S(2)}) collective-permute-start(f32[12,32,128]{2,1,0:T(8,128)S(1)} %get-tuple-element.86), channel_id=1, source_target_pairs={{1,2},{2,1},{5,6},{6,5},{9,10},{10,9},{13,14},{14,13},{17,18},{18,... | collective-permute-start | bytes 589832 | tf_op jit(solution)/shard_map/ppermute | solution.py:583
  71.0 4.6 %first_stage.5 = (f32[12,8,32,256]{3,2,1,0:T(8,128)S(1)}, f32[12,32,128]{2,1,0:T(8,128)S(1)}, f32[12,32,128]{2,1,0:T(8,128)S(1)}, s32[2]{0:T(128)S(1)}) custom-call(s32[2]{0:T(128)S(1)} %get-tuple-element.80.side, s32[12,8,32,256]{3,2,1,0:T(8,128)S(1)} %get-tuple-element.116.signs, f32[8,32,256]{2,1,0:T(8,128)S(1)} %copy-done.1, ...), custom_call_target="tpu_custom_call" | custom-call | flops 2415919104 | bytes 12582912 | tf_op jit(solution)/shard_map/first_stage/pallas_call | solution.py:220
  76.6 3.6 %last_column_stage.4 = (f32[12,8,32,256]{3,2,1,0:T(8,128)S(1)}, f32[12,120,256]{2,1,0:T(8,128)S(1)}, f32[12,120,256]{2,1,0:T(8,128)S(1)}, s32[2]{0:T(128)S(1)}) custom-call(s32[2]{0:T(128)S(1)} %get-tuple-element.83.side, f32[12,8,32,256]{3,2,1,0:T(8,128)S(1)} %get-tuple-element.84.tiles, f32[12,32,128]{2,1,0:T(8,128)S(1)} %collective-permute-done.13.near, ...), custom_call_target="tpu_custom_call" | custom-call | flops 1610612736 | bytes 12582912 | tf_op jit(solution)/shard_map/last_column_stage/pallas_call | solution.py:303
  80.3 2.7 %collective-permute-start.18 = (f32[8,120,256]{2,1,0:T(8,128)S(1)}, f32[8,120,256]{2,1,0:T(8,128)S(1)}, u32[]{:S(2)}, u32[]{:S(2)}) collective-permute-start(f32[8,120,256]{2,1,0:T(8,128)S(1)} %get-tuple-element.94), channel_id=1, source_target_pairs={{4,8},{8,4},{12,16},{16,12},{20,24},{24,20},{28,32},{32,28},{36,40... | collective-permute-start | bytes 2949128 | tf_op jit(solution)/shard_map/ppermute | solution.py:583
  83.1 2.8 %collective-permute-start.16 = (f32[12,32,128]{2,1,0:T(8,128)S(1)}, f32[12,32,128]{2,1,0:T(8,128)S(1)}, u32[]{:S(2)}, u32[]{:S(2)}) collective-permute-start(f32[12,32,128]{2,1,0:T(8,128)S(1)} %get-tuple-element.90), channel_id=1, source_target_pairs={{1,2},{2,1},{5,6},{6,5},{9,10},{10,9},{13,14},{14,13},{17,18},{18,... | collective-permute-start | bytes 589832 | tf_op jit(solution)/shard_map/ppermute | solution.py:583
  86.0 4.5 %collective-permute-start.21 = (f32[12,120,256]{2,1,0:T(8,128)S(1)}, f32[12,120,256]{2,1,0:T(8,128)S(1)}, u32[]{:S(2)}, u32[]{:S(2)}) collective-permute-start(f32[12,120,256]{2,1,0:T(8,128)S(1)} %get-tuple-element.102), channel_id=1, source_target_pairs={{4,8},{8,4},{12,16},{16,12},{20,24},{24,20},{28,32},{32,28},{36,40... | collective-permute-start | bytes 4423688 | tf_op jit(solution)/shard_map/ppermute | solution.py:583
  90.5 1.0 collective-permute-done.16.far
  91.5 7.1 %middle_stage.5 = (f32[12,8,32,256]{3,2,1,0:T(8,128)S(1)}, f32[12,32,128]{2,1,0:T(8,128)S(1)}, f32[12,32,128]{2,1,0:T(8,128)S(1)}, s32[2]{0:T(128)S(1)}) custom-call(s32[2]{0:T(128)S(1)} %get-tuple-element.87.side, f32[12,8,32,256]{3,2,1,0:T(8,128)S(1)} %get-tuple-element.88.tiles, f32[12,32,128]{2,1,0:T(8,128)S(1)} %collective-permute-done.15.near, ...), custom_call_target="tpu_custom_call" | custom-call | flops 4026531840 | bytes 12582912 | tf_op jit(solution)/shard_map/middle_stage/pallas_call | solution.py:271
  98.7 2.7 %collective-permute-start.20 = (f32[12,32,128]{2,1,0:T(8,128)S(1)}, f32[12,32,128]{2,1,0:T(8,128)S(1)}, u32[]{:S(2)}, u32[]{:S(2)}) collective-permute-start(f32[12,32,128]{2,1,0:T(8,128)S(1)} %get-tuple-element.99), channel_id=1, source_target_pairs={{1,2},{2,1},{5,6},{6,5},{9,10},{10,9},{13,14},{14,13},{17,18},{18,... | collective-permute-start | bytes 589832 | tf_op jit(solution)/shard_map/ppermute | solution.py:583
  101.4 2.7 %sketch_stage.2 = (f32[8,8,32,256]{3,2,1,0:T(8,128)S(1)}, s32[2]{0:T(128)S(1)}) custom-call(s32[2]{0:T(128)S(1)} %get-tuple-element.92.side, f32[8,8,32,256]{3,2,1,0:T(8,128)S(1)} %get-tuple-element.93.tiles, f32[8,120,256]{2,1,0:T(8,128)S(1)} %collective-permute-done.10.ahead.inner, f32[8,120,256]{2,1,0:T(8,128)S(1)} %collective-permute-done.18.outer, ...), custom_call_target="tpu_custom_call" | custom-call | flops 1610612736 | bytes 8388608 | tf_op jit(solution)/shard_map/sketch_stage/pallas_call | solution.py:327
  104.3 1.9 %collective-permute-done.20.far = f32[12,32,128]{2,1,0:T(8,128)S(1)} collective-permute-done((f32[12,32,128]{2,1,0:T(8,128)S(1)}, f32[12,32,128]{2,1,0:T(8,128)S(1)}, u32[]{:S(2)}, u32[]{:S(2)}) %collective-permute-start.20) | collective-permute-done | bytes 196640 | tf_op jit(solution)/shard_map/ppermute | solution.py:583
  106.2 3.6 %last_column_stage.5 = (f32[12,8,32,256]{3,2,1,0:T(8,128)S(1)}, f32[12,120,256]{2,1,0:T(8,128)S(1)}, f32[12,120,256]{2,1,0:T(8,128)S(1)}, s32[2]{0:T(128)S(1)}) custom-call(s32[2]{0:T(128)S(1)} %get-tuple-element.96.side, f32[12,8,32,256]{3,2,1,0:T(8,128)S(1)} %get-tuple-element.97.tiles, f32[12,32,128]{2,1,0:T(8,128)S(1)} %collective-permute-done.19.near, ...), custom_call_target="tpu_custom_call" | custom-call | flops 1610612736 | bytes 12582912 | tf_op jit(solution)/shard_map/last_column_stage/pallas_call | solution.py:303
  110.0 3.3 %collective-permute-start.23 = (f32[12,120,256]{2,1,0:T(8,128)S(1)}, f32[12,120,256]{2,1,0:T(8,128)S(1)}, u32[]{:S(2)}, u32[]{:S(2)}) collective-permute-start(f32[12,120,256]{2,1,0:T(8,128)S(1)} %get-tuple-element.111), channel_id=1, source_target_pairs={{4,8},{8,4},{12,16},{16,12},{20,24},{24,20},{28,32},{32,28},{36,40... | collective-permute-start | bytes 4423688 | tf_op jit(solution)/shard_map/ppermute | solution.py:583
  113.6 3.7 %sketch_stage.3 = (f32[12,8,32,256]{3,2,1,0:T(8,128)S(1)}, s32[2]{0:T(128)S(1)}) custom-call(s32[2]{0:T(128)S(1)} %get-tuple-element.100.side, f32[12,8,32,256]{3,2,1,0:T(8,128)S(1)} %get-tuple-element.101.tiles, f32[12,120,256]{2,1,0:T(8,128)S(1)} %collective-permute-done.17.ahead.inner, f32[12,120,256]{2,1,0:T(8,128)S(1)} %collective-permute-done.21.outer, ...), custom_call_target="tpu_custom_call" | custom-call | flops 2415919104 | bytes 12582912 | tf_op jit(solution)/shard_map/sketch_stage/pallas_call | solution.py:327
  117.4 4.0 %early_gram_stage.1 = (f32[20,20]{1,0:T(8,128)S(1)}, s32[2]{0:T(128)S(1)}) custom-call(s32[2]{0:T(128)S(1)} %get-tuple-element.103.side, f32[8,32,8,256]{3,2,1,0:T(8,128)S(1)} %bitcast.8, f32[12,32,8,256]{3,2,1,0:T(8,128)S(1)} %bitcast.5), custom_call_target="tpu_custom_call" | custom-call | flops 2147483648 | bytes 8388608 | tf_op jit(solution)/shard_map/early_gram_stage/pallas_call | solution.py:393
  121.4 2.4 %sketch_main_stage.1 = (f32[12,256,256]{2,1,0:T(8,128)S(1)}, s32[2]{0:T(128)}) custom-call(s32[2]{0:T(128)S(1)} %get-tuple-element.107.side, f32[12,8,32,256]{3,2,1,0:T(8,128)S(1)} %get-tuple-element.108.tiles, bf16[256,1536]{1,0:T(8,128)(2,1)S(1)} %get-tuple-element.95.matrix), custom_call_target="tpu_custom_call" | custom-call | flops 1207959552 | bytes 6291456 | tf_op jit(solution)/shard_map/sketch_main_stage/pallas_call | solution.py:346
  123.7 9.0 %collective-permute-done.23.outer = f32[12,120,256]{2,1,0:T(8,128)S(1)} collective-permute-done((f32[12,120,256]{2,1,0:T(8,128)S(1)}, f32[12,120,256]{2,1,0:T(8,128)S(1)}, u32[]{:S(2)}, u32[]{:S(2)}) %collective-permute-start.23) | collective-permute-done | bytes 1474592 | tf_op jit(solution)/shard_map/ppermute | solution.py:583
  132.7 6.0 %gram_stage.1 = (f32[2,8,128]{2,1,0:T(8,128)S(1)}, f32[12,32,8,256]{3,2,1,0:T(8,128)S(1)}) custom-call(f32[20,20]{1,0:T(8,128)S(1)} %get-tuple-element.106.early, f32[12,256,256]{2,1,0:T(8,128)S(1)} %get-tuple-element.109.main, f32[12,120,256]{2,1,0:T(8,128)S(1)} %collective-permute-done.22.inner, f32[12,120,256]{2,1,0:T(8,128)S(1)} %collective-permute-done.23.outer, ...), custom_call_target="tpu_custom_call" | custom-call | flops 2147483648 | bytes 8388608 | tf_op jit(solution)/shard_map/gram_stage/pallas_call | solution.py:442
  138.8 1.2 collective-permute-done.24.other
  140.1 3.6 %collective-permute-done.25.other = f32[2,8,128]{2,1,0:T(8,128)S(1)} collective-permute-done((f32[2,8,128]{2,1,0:T(8,128)S(1)}, f32[2,8,128]{2,1,0:T(8,128)S(1)}, u32[]{:S(2)}, u32[]{:S(2)}) %collective-permute-start.25) | collective-permute-done | bytes 8224 | tf_op jit(solution)/shard_map/ppermute | solution.py:509
  143.9 5.1 %collective-permute-done.26.other = f32[2,8,128]{2,1,0:T(8,128)S(1)} collective-permute-done((f32[2,8,128]{2,1,0:T(8,128)S(1)}, f32[2,8,128]{2,1,0:T(8,128)S(1)}, u32[]{:S(2)}, u32[]{:S(2)}) %collective-permute-start.26) | collective-permute-done | bytes 8224 | tf_op jit(solution)/shard_map/ppermute | solution.py:509
  149.5 3.2 %collective-permute-done.27.other = f32[2,8,128]{2,1,0:T(8,128)S(1)} collective-permute-done((f32[2,8,128]{2,1,0:T(8,128)S(1)}, f32[2,8,128]{2,1,0:T(8,128)S(1)}, u32[]{:S(2)}, u32[]{:S(2)}) %collective-permute-start.27) | collective-permute-done | bytes 8224 | tf_op jit(solution)/shard_map/ppermute | solution.py:509
  152.7 1.0 collective-permute-start.28
  153.7 4.2 %collective-permute-done.28.other = f32[2,8,128]{2,1,0:T(8,128)S(1)} collective-permute-done((f32[2,8,128]{2,1,0:T(8,128)S(1)}, f32[2,8,128]{2,1,0:T(8,128)S(1)}, u32[]{:S(2)}, u32[]{:S(2)}) %collective-permute-start.28) | collective-permute-done | bytes 8224 | tf_op jit(solution)/shard_map/ppermute | solution.py:509
  158.0 3.6 %collective-permute-done.29.other = f32[2,8,128]{2,1,0:T(8,128)S(1)} collective-permute-done((f32[2,8,128]{2,1,0:T(8,128)S(1)}, f32[2,8,128]{2,1,0:T(8,128)S(1)}, u32[]{:S(2)}, u32[]{:S(2)}) %collective-permute-start.29) | collective-permute-done | bytes 8224 | tf_op jit(solution)/shard_map/ppermute | solution.py:509
  161.9 4.9 %collective-permute-done.30.other = f32[2,8,128]{2,1,0:T(8,128)S(1)} collective-permute-done((f32[2,8,128]{2,1,0:T(8,128)S(1)}, f32[2,8,128]{2,1,0:T(8,128)S(1)}, u32[]{:S(2)}, u32[]{:S(2)}) %collective-permute-start.30) | collective-permute-done | bytes 8224 | tf_op jit(solution)/shard_map/ppermute | solution.py:509
  166.9 4.6 %factor_stage.1 = (f32[32,32]{1,0:T(8,128)}, f32[32,32]{1,0:T(8,128)S(1)}) custom-call(f32[2,8,128]{2,1,0:T(8,128)S(1)} %merge.13.refs_0_), custom_call_target="tpu_custom_call" | custom-call | tf_op jit(solution)/shard_map/factor_stage/pallas_call | solution.py:541
  171.5 6.6 %basis_stage.1 = f32[32,32,8,256]{3,2,1,0:T(8,128)} custom-call(f32[32,32]{1,0:T(8,128)S(1)} %get-tuple-element.113.inverse, f32[8,32,8,256]{3,2,1,0:T(8,128)S(1)} %bitcast.10, f32[12,32,8,256]{3,2,1,0:T(8,128)S(1)} %bitcast.7, f32[12,32,8,256]{3,2,1,0:T(8,128)S(1)} %get-tuple-element.114.refs_2_), custom_call_target="tpu_custom_call" | custom-call | flops 3221225472 | bytes 16777216 | tf_op jit(solution)/shard_map/basis_stage/pallas_call | solution.py:569
  (64 shorter events, 4.3 us)
Async XLA Ops:
  0.6 1.9 %copy-start.1 = (f32[8,32,256]{2,1,0:T(8,128)S(1)}, f32[8,32,256]{2,1,0:T(8,128)}, u32[]{:S(2)}) copy-start(f32[8,32,256]{2,1,0:T(8,128)} %scale.17) | copy-start | bytes 786436
  3.7 16.5 %collective-permute-start = (f32[8,120,256]{2,1,0:T(8,128)S(1)}, f32[8,120,256]{2,1,0:T(8,128)S(1)}, u32[]{:S(2)}, u32[]{:S(2)}) collective-permute-start(f32[8,120,256]{2,1,0:T(8,128)S(1)} %get-tuple-element.59), channel_id=1, source_target_pairs={{0,4},{4,0},{8,12},{12,8},{16,20},{20,16},{24,28},{28,24},{32,36},... | collective-permute-start | bytes 2949128 | tf_op jit(solution)/shard_map/ppermute | solution.py:583
  3.8 17.5 %collective-permute-start.1 = (f32[8,120,256]{2,1,0:T(8,128)S(1)}, f32[8,120,256]{2,1,0:T(8,128)S(1)}, u32[]{:S(2)}, u32[]{:S(2)}) collective-permute-start(f32[8,120,256]{2,1,0:T(8,128)S(1)} %get-tuple-element.60), channel_id=1, source_target_pairs={{4,8},{8,4},{12,16},{16,12},{20,24},{24,20},{28,32},{32,28},{36,40... | collective-permute-start | bytes 2949128 | tf_op jit(solution)/shard_map/ppermute | solution.py:583
  12.4 4.5 %copy-start.2 = (f32[256,512]{1,0:T(8,128)S(1)}, f32[256,512]{1,0:T(8,128)}, u32[]{:S(2)}) copy-start(f32[256,512]{1,0:T(8,128)} %constant.40.clone.by_in) | copy-start | bytes 1572868
  12.4 4.5 %copy-start.3 = (f32[256,512]{1,0:T(8,128)S(1)}, f32[256,512]{1,0:T(8,128)}, u32[]{:S(2)}) copy-start(f32[256,512]{1,0:T(8,128)} %constant.39.clone.by_out) | copy-start | bytes 1572868
  12.4 4.5 %copy-start.4 = (f32[256,256]{1,0:T(8,128)S(1)}, f32[256,256]{1,0:T(8,128)}, u32[]{:S(2)}) copy-start(f32[256,256]{1,0:T(8,128)} %constant.43.clone.same) | copy-start | bytes 786436
  12.4 4.5 %copy-start.5 = (f32[256,8]{1,0:T(8,128)S(1)}, f32[256,8]{1,0:T(8,128)}, u32[]{:S(2)}) copy-start(f32[256,8]{1,0:T(8,128)} %constant.42.clone.spread) | copy-start | bytes 24580
  12.4 4.5 %copy-start.6 = (f32[8,512]{1,0:T(8,128)S(1)}, f32[8,512]{1,0:T(8,128)}, u32[]{:S(2)}) copy-start(f32[8,512]{1,0:T(8,128)} %constant.41.clone.pick) | copy-start | bytes 49156
  12.4 4.5 %copy-start.7 = (f32[8,8]{1,0:T(8,128)S(1)}, f32[8,8]{1,0:T(8,128)}, u32[]{:S(2)}) copy-start(f32[8,8]{1,0:T(8,128)} %factor.1) | copy-start | bytes 772
  12.5 4.5 %copy-start.8 = (f32[8,8]{1,0:T(8,128)S(1)}, f32[8,8]{1,0:T(8,128)}, u32[]{:S(2)}) copy-start(f32[8,8]{1,0:T(8,128)} %mix.1) | copy-start | bytes 772
  14.0 26.9 %collective-permute-start.4 = (f32[12,120,256]{2,1,0:T(8,128)S(1)}, f32[12,120,256]{2,1,0:T(8,128)S(1)}, u32[]{:S(2)}, u32[]{:S(2)}) collective-permute-start(f32[12,120,256]{2,1,0:T(8,128)S(1)} %get-tuple-element.69), channel_id=1, source_target_pairs={{0,4},{4,0},{8,12},{12,8},{16,20},{20,16},{24,28},{28,24},{32,36},... | collective-permute-start | bytes 4423688 | tf_op jit(solution)/shard_map/ppermute | solution.py:583
  14.1 29.9 %collective-permute-start.5 = (f32[12,120,256]{2,1,0:T(8,128)S(1)}, f32[12,120,256]{2,1,0:T(8,128)S(1)}, u32[]{:S(2)}, u32[]{:S(2)}) collective-permute-start(f32[12,120,256]{2,1,0:T(8,128)S(1)} %get-tuple-element.70), channel_id=1, source_target_pairs={{4,8},{8,4},{12,16},{16,12},{20,24},{24,20},{28,32},{32,28},{36,40... | collective-permute-start | bytes 4423688 | tf_op jit(solution)/shard_map/ppermute | solution.py:583
  21.3 14.9 %copy-start = (bf16[8,1024,256]{2,1,0:T(8,128)(2,1)S(1)}, bf16[8,1024,256]{2,1,0:T(8,128)(2,1)}, u32[]{:S(2)}) copy-start(bf16[8,1024,256]{2,1,0:T(8,128)(2,1)} %constant.38.clone.table) | copy-start | bytes 12582916
  24.7 11.5 %copy-start.9 = (f32[8,32,256]{2,1,0:T(8,128)S(1)}, f32[8,32,256]{2,1,0:T(8,128)}, u32[]{:S(2)}) copy-start(f32[8,32,256]{2,1,0:T(8,128)} %weights.5) | copy-start | bytes 786436
  24.7 7.1 %collective-permute-start.2 = (f32[8,32,128]{2,1,0:T(8,128)S(1)}, f32[8,32,128]{2,1,0:T(8,128)S(1)}, u32[]{:S(2)}, u32[]{:S(2)}) collective-permute-start(f32[8,32,128]{2,1,0:T(8,128)S(1)} %get-tuple-element.64), channel_id=1, source_target_pairs={{0,1},{1,0},{2,3},{3,2},{4,5},{5,4},{6,7},{7,6},{8,9},{9,8},{10,11... | collective-permute-start | bytes 393224 | tf_op jit(solution)/shard_map/ppermute | solution.py:583
  24.9 11.3 %collective-permute-start.3 = (f32[8,32,128]{2,1,0:T(8,128)S(1)}, f32[8,32,128]{2,1,0:T(8,128)S(1)}, u32[]{:S(2)}, u32[]{:S(2)}) collective-permute-start(f32[8,32,128]{2,1,0:T(8,128)S(1)} %get-tuple-element.65), channel_id=1, source_target_pairs={{1,2},{2,1},{5,6},{6,5},{9,10},{10,9},{13,14},{14,13},{17,18},{18,... | collective-permute-start | bytes 393224 | tf_op jit(solution)/shard_map/ppermute | solution.py:583
  31.8 39.2 %collective-permute-start.11 = (f32[12,120,256]{2,1,0:T(8,128)S(1)}, f32[12,120,256]{2,1,0:T(8,128)S(1)}, u32[]{:S(2)}, u32[]{:S(2)}) collective-permute-start(f32[12,120,256]{2,1,0:T(8,128)S(1)} %get-tuple-element.81), channel_id=1, source_target_pairs={{0,4},{4,0},{8,12},{12,8},{16,20},{20,16},{24,28},{28,24},{32,36},... | collective-permute-start | bytes 4423688 | tf_op jit(solution)/shard_map/ppermute | solution.py:583
  31.9 39.1 %collective-permute-start.12 = (f32[12,120,256]{2,1,0:T(8,128)S(1)}, f32[12,120,256]{2,1,0:T(8,128)S(1)}, u32[]{:S(2)}, u32[]{:S(2)}) collective-permute-start(f32[12,120,256]{2,1,0:T(8,128)S(1)} %get-tuple-element.82), channel_id=1, source_target_pairs={{4,8},{8,4},{12,16},{16,12},{20,24},{24,20},{28,32},{32,28},{36,40... | collective-permute-start | bytes 4423688 | tf_op jit(solution)/shard_map/ppermute | solution.py:583
  40.8 7.8 %collective-permute-start.6 = (f32[8,32,128]{2,1,0:T(8,128)S(1)}, f32[8,32,128]{2,1,0:T(8,128)S(1)}, u32[]{:S(2)}, u32[]{:S(2)}) collective-permute-start(f32[8,32,128]{2,1,0:T(8,128)S(1)} %get-tuple-element.73), channel_id=1, source_target_pairs={{0,1},{1,0},{2,3},{3,2},{4,5},{5,4},{6,7},{7,6},{8,9},{9,8},{10,11... | collective-permute-start | bytes 393224 | tf_op jit(solution)/shard_map/ppermute | solution.py:583
  40.9 7.7 %collective-permute-start.7 = (f32[8,32,128]{2,1,0:T(8,128)S(1)}, f32[8,32,128]{2,1,0:T(8,128)S(1)}, u32[]{:S(2)}, u32[]{:S(2)}) collective-permute-start(f32[8,32,128]{2,1,0:T(8,128)S(1)} %get-tuple-element.74), channel_id=1, source_target_pairs={{1,2},{2,1},{5,6},{6,5},{9,10},{10,9},{13,14},{14,13},{17,18},{18,... | collective-permute-start | bytes 393224 | tf_op jit(solution)/shard_map/ppermute | solution.py:583
  51.6 9.5 %collective-permute-start.10 = (f32[8,120,256]{2,1,0:T(8,128)S(1)}, f32[8,120,256]{2,1,0:T(8,128)S(1)}, u32[]{:S(2)}, u32[]{:S(2)}) collective-permute-start(f32[8,120,256]{2,1,0:T(8,128)S(1)} %get-tuple-element.79), channel_id=1, source_target_pairs={{0,4},{4,0},{8,12},{12,8},{16,20},{20,16},{24,28},{28,24},{32,36},... | collective-permute-start | bytes 2949128 | tf_op jit(solution)/shard_map/ppermute | solution.py:583
  51.8 7.3 %collective-permute-start.8 = (f32[12,32,128]{2,1,0:T(8,128)S(1)}, f32[12,32,128]{2,1,0:T(8,128)S(1)}, u32[]{:S(2)}, u32[]{:S(2)}) collective-permute-start(f32[12,32,128]{2,1,0:T(8,128)S(1)} %get-tuple-element.77), channel_id=1, source_target_pairs={{0,1},{1,0},{2,3},{3,2},{4,5},{5,4},{6,7},{7,6},{8,9},{9,8},{10,11... | collective-permute-start | bytes 589832 | tf_op jit(solution)/shard_map/ppermute | solution.py:583
  51.9 9.1 %collective-permute-start.9 = (f32[12,32,128]{2,1,0:T(8,128)S(1)}, f32[12,32,128]{2,1,0:T(8,128)S(1)}, u32[]{:S(2)}, u32[]{:S(2)}) collective-permute-start(f32[12,32,128]{2,1,0:T(8,128)S(1)} %get-tuple-element.78), channel_id=1, source_target_pairs={{1,2},{2,1},{5,6},{6,5},{9,10},{10,9},{13,14},{14,13},{17,18},{18,... | collective-permute-start | bytes 589832 | tf_op jit(solution)/shard_map/ppermute | solution.py:583
  68.1 7.5 %collective-permute-start.13 = (f32[12,32,128]{2,1,0:T(8,128)S(1)}, f32[12,32,128]{2,1,0:T(8,128)S(1)}, u32[]{:S(2)}, u32[]{:S(2)}) collective-permute-start(f32[12,32,128]{2,1,0:T(8,128)S(1)} %get-tuple-element.85), channel_id=1, source_target_pairs={{0,1},{1,0},{2,3},{3,2},{4,5},{5,4},{6,7},{7,6},{8,9},{9,8},{10,11... | collective-permute-start | bytes 589832 | tf_op jit(solution)/shard_map/ppermute | solution.py:583
  68.2 8.3 %collective-permute-start.14 = (f32[12,32,128]{2,1,0:T(8,128)S(1)}, f32[12,32,128]{2,1,0:T(8,128)S(1)}, u32[]{:S(2)}, u32[]{:S(2)}) collective-permute-start(f32[12,32,128]{2,1,0:T(8,128)S(1)} %get-tuple-element.86), channel_id=1, source_target_pairs={{1,2},{2,1},{5,6},{6,5},{9,10},{10,9},{13,14},{14,13},{17,18},{18,... | collective-permute-start | bytes 589832 | tf_op jit(solution)/shard_map/ppermute | solution.py:583
  80.2 11.3 %collective-permute-start.17 = (f32[12,120,256]{2,1,0:T(8,128)S(1)}, f32[12,120,256]{2,1,0:T(8,128)S(1)}, u32[]{:S(2)}, u32[]{:S(2)}) collective-permute-start(f32[12,120,256]{2,1,0:T(8,128)S(1)} %get-tuple-element.91), channel_id=1, source_target_pairs={{0,4},{4,0},{8,12},{12,8},{16,20},{20,16},{24,28},{28,24},{32,36},... | collective-permute-start | bytes 4423688 | tf_op jit(solution)/shard_map/ppermute | solution.py:583
  80.3 21.1 %collective-permute-start.18 = (f32[8,120,256]{2,1,0:T(8,128)S(1)}, f32[8,120,256]{2,1,0:T(8,128)S(1)}, u32[]{:S(2)}, u32[]{:S(2)}) collective-permute-start(f32[8,120,256]{2,1,0:T(8,128)S(1)} %get-tuple-element.94), channel_id=1, source_target_pairs={{4,8},{8,4},{12,16},{16,12},{20,24},{24,20},{28,32},{32,28},{36,40... | collective-permute-start | bytes 2949128 | tf_op jit(solution)/shard_map/ppermute | solution.py:583
  83.1 7.5 %collective-permute-start.15 = (f32[12,32,128]{2,1,0:T(8,128)S(1)}, f32[12,32,128]{2,1,0:T(8,128)S(1)}, u32[]{:S(2)}, u32[]{:S(2)}) collective-permute-start(f32[12,32,128]{2,1,0:T(8,128)S(1)} %get-tuple-element.89), channel_id=1, source_target_pairs={{0,1},{1,0},{2,3},{3,2},{4,5},{5,4},{6,7},{7,6},{8,9},{9,8},{10,11... | collective-permute-start | bytes 589832 | tf_op jit(solution)/shard_map/ppermute | solution.py:583
  83.1 8.4 %collective-permute-start.16 = (f32[12,32,128]{2,1,0:T(8,128)S(1)}, f32[12,32,128]{2,1,0:T(8,128)S(1)}, u32[]{:S(2)}, u32[]{:S(2)}) collective-permute-start(f32[12,32,128]{2,1,0:T(8,128)S(1)} %get-tuple-element.90), channel_id=1, source_target_pairs={{1,2},{2,1},{5,6},{6,5},{9,10},{10,9},{13,14},{14,13},{17,18},{18,... | collective-permute-start | bytes 589832 | tf_op jit(solution)/shard_map/ppermute | solution.py:583
  86.0 27.7 %collective-permute-start.21 = (f32[12,120,256]{2,1,0:T(8,128)S(1)}, f32[12,120,256]{2,1,0:T(8,128)S(1)}, u32[]{:S(2)}, u32[]{:S(2)}) collective-permute-start(f32[12,120,256]{2,1,0:T(8,128)S(1)} %get-tuple-element.102), channel_id=1, source_target_pairs={{4,8},{8,4},{12,16},{16,12},{20,24},{24,20},{28,32},{32,28},{36,40... | collective-permute-start | bytes 4423688 | tf_op jit(solution)/shard_map/ppermute | solution.py:583
  98.6 5.7 %collective-permute-start.19 = (f32[12,32,128]{2,1,0:T(8,128)S(1)}, f32[12,32,128]{2,1,0:T(8,128)S(1)}, u32[]{:S(2)}, u32[]{:S(2)}) collective-permute-start(f32[12,32,128]{2,1,0:T(8,128)S(1)} %get-tuple-element.98), channel_id=1, source_target_pairs={{0,1},{1,0},{2,3},{3,2},{4,5},{5,4},{6,7},{7,6},{8,9},{9,8},{10,11... | collective-permute-start | bytes 589832 | tf_op jit(solution)/shard_map/ppermute | solution.py:583
  98.7 7.6 %collective-permute-start.20 = (f32[12,32,128]{2,1,0:T(8,128)S(1)}, f32[12,32,128]{2,1,0:T(8,128)S(1)}, u32[]{:S(2)}, u32[]{:S(2)}) collective-permute-start(f32[12,32,128]{2,1,0:T(8,128)S(1)} %get-tuple-element.99), channel_id=1, source_target_pairs={{1,2},{2,1},{5,6},{6,5},{9,10},{10,9},{13,14},{14,13},{17,18},{18,... | collective-permute-start | bytes 589832 | tf_op jit(solution)/shard_map/ppermute | solution.py:583
  109.9 13.9 %collective-permute-start.22 = (f32[12,120,256]{2,1,0:T(8,128)S(1)}, f32[12,120,256]{2,1,0:T(8,128)S(1)}, u32[]{:S(2)}, u32[]{:S(2)}) collective-permute-start(f32[12,120,256]{2,1,0:T(8,128)S(1)} %get-tuple-element.110), channel_id=1, source_target_pairs={{0,4},{4,0},{8,12},{12,8},{16,20},{20,16},{24,28},{28,24},{32,36},... | collective-permute-start | bytes 4423688 | tf_op jit(solution)/shard_map/ppermute | solution.py:583
  110.0 22.8 %collective-permute-start.23 = (f32[12,120,256]{2,1,0:T(8,128)S(1)}, f32[12,120,256]{2,1,0:T(8,128)S(1)}, u32[]{:S(2)}, u32[]{:S(2)}) collective-permute-start(f32[12,120,256]{2,1,0:T(8,128)S(1)} %get-tuple-element.111), channel_id=1, source_target_pairs={{4,8},{8,4},{12,16},{16,12},{20,24},{24,20},{28,32},{32,28},{36,40... | collective-permute-start | bytes 4423688 | tf_op jit(solution)/shard_map/ppermute | solution.py:583
  138.7 1.2 collective-permute-start.24
  140.0 3.7 %collective-permute-start.25 = (f32[2,8,128]{2,1,0:T(8,128)S(1)}, f32[2,8,128]{2,1,0:T(8,128)S(1)}, u32[]{:S(2)}, u32[]{:S(2)}) collective-permute-start(f32[2,8,128]{2,1,0:T(8,128)S(1)} %merge.7.mine), channel_id=1, source_target_pairs={{0,8},{4,12},{8,0},{12,4},{16,24},{20,28},{24,16},{28,20},{32,40},... | collective-permute-start | bytes 24584 | tf_op jit(solution)/shard_map/ppermute | solution.py:509
  143.7 5.2 %collective-permute-start.26 = (f32[2,8,128]{2,1,0:T(8,128)S(1)}, f32[2,8,128]{2,1,0:T(8,128)S(1)}, u32[]{:S(2)}, u32[]{:S(2)}) collective-permute-start(f32[2,8,128]{2,1,0:T(8,128)S(1)} %merge.8.mine), channel_id=1, source_target_pairs={{0,16},{4,20},{8,24},{12,28},{16,0},{20,4},{24,8},{28,12},{32,48},... | collective-permute-start | bytes 24584 | tf_op jit(solution)/shard_map/ppermute | solution.py:509
  148.9 3.7 %collective-permute-start.27 = (f32[2,8,128]{2,1,0:T(8,128)S(1)}, f32[2,8,128]{2,1,0:T(8,128)S(1)}, u32[]{:S(2)}, u32[]{:S(2)}) collective-permute-start(f32[2,8,128]{2,1,0:T(8,128)S(1)} %merge.9.mine), channel_id=1, source_target_pairs={{0,32},{4,36},{8,40},{12,44},{16,48},{20,52},{24,56},{28,60},{32,0... | collective-permute-start | bytes 24584 | tf_op jit(solution)/shard_map/ppermute | solution.py:509
  152.7 5.2 %collective-permute-start.28 = (f32[2,8,128]{2,1,0:T(8,128)S(1)}, f32[2,8,128]{2,1,0:T(8,128)S(1)}, u32[]{:S(2)}, u32[]{:S(2)}) collective-permute-start(f32[2,8,128]{2,1,0:T(8,128)S(1)} %merge.10.mine), channel_id=1, source_target_pairs={{0,64},{4,68},{8,72},{12,76},{16,80},{20,84},{24,88},{28,92},{32,9... | collective-permute-start | bytes 24584 | tf_op jit(solution)/shard_map/ppermute | solution.py:509
  157.9 3.7 %collective-permute-start.29 = (f32[2,8,128]{2,1,0:T(8,128)S(1)}, f32[2,8,128]{2,1,0:T(8,128)S(1)}, u32[]{:S(2)}, u32[]{:S(2)}) collective-permute-start(f32[2,8,128]{2,1,0:T(8,128)S(1)} %merge.11.mine), channel_id=1, source_target_pairs={{0,1},{1,0},{2,3},{3,2},{4,5},{5,4},{6,7},{7,6},{8,9},{9,8},{10,11... | collective-permute-start | bytes 24584 | tf_op jit(solution)/shard_map/ppermute | solution.py:509
  161.6 5.2 %collective-permute-start.30 = (f32[2,8,128]{2,1,0:T(8,128)S(1)}, f32[2,8,128]{2,1,0:T(8,128)S(1)}, u32[]{:S(2)}, u32[]{:S(2)}) collective-permute-start(f32[2,8,128]{2,1,0:T(8,128)S(1)} %merge.12.mine), channel_id=1, source_target_pairs={{0,2},{1,3},{2,0},{3,1},{4,6},{5,7},{6,4},{7,5},{8,10},{9,11},{10,... | collective-permute-start | bytes 24584 | tf_op jit(solution)/shard_map/ppermute | solution.py:509

commit v4 on v3

--- a/solution.py
+++ b/solution.py
@@ -520,18 +520,24 @@
     for j in range(4):
         work[:, 8 * j:8 * j + 8, 0:order] = gram[:, :, j * order:(j + 1) * order]
     now = (work[0], work[1])
+    finished, base, place = [], 0, row
     for k in range(order - 1):
-        pivot_row = tuple(v[k:k + 1, :] for v in now)
+        if k - base == 8:
+            finished.append(now[0][:8])
+            now = tuple(v[8:] for v in now)
+            base, place = k, place[8:]
+        pivot_row = tuple(v[k - base:k - base + 1, :] for v in now)
         pivot = tuple(jnp.broadcast_to(v[:, k:k + 1], (1, 128)) for v in pivot_row)
         first = pivot_row[0] / pivot[0]
         rest = pair_add(pivot_row, pair_neg(pair_mul((first, jnp.zeros_like(first)), pivot)))
         ratio = quick_sum(first, rest[0] / pivot[0])
         column = tuple(
-            jnp.where(row > k, jnp.broadcast_to(v[:, k:k + 1], (order, 128)), 0.0) for v in now
+            jnp.where(place > k, jnp.broadcast_to(v[:, k:k + 1], (order - base, 128)), 0.0) for v in now
         )
         now = pair_add(now, pair_neg(pair_mul(column, ratio)))
-    diagonal = jnp.sum(jnp.where(lane == row, now[0], 0.0), axis=1, keepdims=True)
-    scaled = now[0] / jnp.sqrt(diagonal)
+    reduced = jnp.concatenate(finished + [now[0]], axis=0)
+    diagonal = jnp.sum(jnp.where(lane == row, reduced, 0.0), axis=1, keepdims=True)
+    scaled = reduced / jnp.sqrt(diagonal)
     factor[...] = jnp.where(lane >= row, scaled, 0.0)[:, 0:order] * (1.0 / norm)
     inverse[...] = scaled[:, order:2 * order] * norm
 

time: 179 us -> 179 us (level)
  no operation moved by 1% of the time
where the time goes in v4:
time: 179 us; the launch traced here: 178 us
  Pallas kernels  78.9 us (44%)
  waiting for transfers between devices  46.7 us (26%)
  starting transfers between devices  45.7 us (26%)
  local copies, waits for them, and re-layouts  5.47 us (3%)
    ppermute x24, starting transfers between devices, swap(): return (lax.ppermute(inner, axis, pairs), lax.ppermute(outer, axis, others))  43.5 us
    ppermute x7, waiting for transfers between devices, sum_over(): lax.ppermute(value, axis, [(i, i ^ bit) for i in range(count)])  25.8 us
    ppermute x24, waiting for transfers between devices, swap(): return (lax.ppermute(inner, axis, pairs), lax.ppermute(outer, axis, others))  20.9 us
    pallas_call x3, Pallas kernels, middle_stage(): pl.pallas_call(middle_kernel, out_shape=(whole, packed, packed, SIDE), in...  18.7 us
    pallas_call x3, Pallas kernels, first_stage(): pl.pallas_call(first_kernel, out_shape=(jax.ShapeDtypeStruct((count, BAND...  12.6 us
    pallas_call x3, Pallas kernels, last_column_stage(): pl.pallas_call(last_column_kernel, out_shape=(whole, edge, edge, SIDE), i...  10.2 us
    pallas_call x1, Pallas kernels, basis_stage(): pl.pallas_call(basis_kernel, grid=(groups // 8,), out_shape=jax.ShapeDtyp...  6.62 us
    pallas_call x2, Pallas kernels, sketch_stage(): pl.pallas_call(sketch_kernel, out_shape=(jax.ShapeDtypeStruct((count, BAN...  6.37 us
  transfers between devices with their start and end apart: 31, of which 16 were waited for; matrix products, arithmetic and copies ran while one was open for 2% of the time, Pallas kernels for 32%

profile of v4, /device:TPU:56, one launch (start us, length us, event | category | flops | bytes accessed | tf_op | source)
XLA Modules:
  0.0 178.1 jit_solution(8470613083126962938)
XLA Ops:
  0.7 1.8 slice.9.signs
  2.5 1.2 edges.3
  3.8 4.9 %collective-permute-start.1 = (f32[8,120,256]{2,1,0:T(8,128)S(1)}, f32[8,120,256]{2,1,0:T(8,128)S(1)}, u32[]{:S(2)}, u32[]{:S(2)}) collective-permute-start(f32[8,120,256]{2,1,0:T(8,128)S(1)} %get-tuple-element.60), channel_id=1, source_target_pairs={{4,8},{8,4},{12,16},{16,12},{20,24},{24,20},{28,32},{32,28},{36,40... | collective-permute-start | bytes 2949128 | tf_op jit(solution)/shard_map/ppermute | solution.py:589
  8.7 3.6 %fusion = (s32[12,8,32,256]{3,2,1,0:T(8,128)S(1)}, s32[12,8,32,256]{3,2,1,0:T(8,128)S(1)}) fusion(s32[32,8,32,256]{3,2,1,0:T(8,128)} %param.11), kind=kLoop, calls=%fused_computation.1 | loop fusion | bytes 12582912 | tf_op jit(solution)/shard_map/slice | solution.py:597
  12.5 1.5 edges.4
  14.1 2.8 %collective-permute-start.5 = (f32[12,120,256]{2,1,0:T(8,128)S(1)}, f32[12,120,256]{2,1,0:T(8,128)S(1)}, u32[]{:S(2)}, u32[]{:S(2)}) collective-permute-start(f32[12,120,256]{2,1,0:T(8,128)S(1)} %get-tuple-element.70), channel_id=1, source_target_pairs={{4,8},{8,4},{12,16},{16,12},{20,24},{24,20},{28,32},{32,28},{36,40... | collective-permute-start | bytes 4423688 | tf_op jit(solution)/shard_map/ppermute | solution.py:589
  17.0 3.2 %prepare.1 = (bf16[256,1536]{1,0:T(8,128)(2,1)S(1)}, bf16[256,1536]{1,0:T(8,128)(2,1)S(1)}, bf16[256,768]{1,0:T(8,128)(2,1)S(1)}, bf16[256,768]{1,0:T(8,128)(2,1)S(1)}) custom-call(s32[2]{0:T(128)S(1)} %pad_add_fusion.side, f32[8,8]{1,0:T(8,128)S(1)} %copy-done.7, f32[8,8]{1,0:T(8,128)S(1)} %copy-done.8, f32[256,512]{1,0:T(8,128)S(1)} %copy-done.3, ...), custom_call_target="tpu_custom_call" | custom-call | tf_op jit(solution)/shard_map/prepare/pallas_call | solution.py:139
  20.2 1.1 collective-permute-done.1.outer
  21.3 3.4 %first_stage.3 = (f32[8,8,32,256]{3,2,1,0:T(8,128)S(1)}, f32[8,32,128]{2,1,0:T(8,128)S(1)}, f32[8,32,128]{2,1,0:T(8,128)S(1)}, s32[2]{0:T(128)S(1)}) custom-call(s32[2]{0:T(128)S(1)} %pad_add_fusion.side, s32[8,8,32,256]{3,2,1,0:T(8,128)S(1)} %slice.9.signs, f32[8,32,256]{2,1,0:T(8,128)S(1)} %copy-done.1, f32[8,120,256]{2,1,0:T(8,128)S(1)} %collective-permute-done.inner, ...), custom_call_target="tpu_custom_call" | custom-call | flops 1610612736 | bytes 8388608 | tf_op jit(solution)/shard_map/first_stage/pallas_call | solution.py:220
  24.9 5.3 %collective-permute-start.3 = (f32[8,32,128]{2,1,0:T(8,128)S(1)}, f32[8,32,128]{2,1,0:T(8,128)S(1)}, u32[]{:S(2)}, u32[]{:S(2)}) collective-permute-start(f32[8,32,128]{2,1,0:T(8,128)S(1)} %get-tuple-element.65), channel_id=1, source_target_pairs={{1,2},{2,1},{5,6},{6,5},{9,10},{10,9},{13,14},{14,13},{17,18},{18,... | collective-permute-start | bytes 393224 | tf_op jit(solution)/shard_map/ppermute | solution.py:589
  30.3 1.5 edges.5
  31.9 4.4 %collective-permute-start.12 = (f32[12,120,256]{2,1,0:T(8,128)S(1)}, f32[12,120,256]{2,1,0:T(8,128)S(1)}, u32[]{:S(2)}, u32[]{:S(2)}) collective-permute-start(f32[12,120,256]{2,1,0:T(8,128)S(1)} %get-tuple-element.82), channel_id=1, source_target_pairs={{4,8},{8,4},{12,16},{16,12},{20,24},{24,20},{28,32},{32,28},{36,40... | collective-permute-start | bytes 4423688 | tf_op jit(solution)/shard_map/ppermute | solution.py:589
  36.3 4.6 %middle_stage.3 = (f32[8,8,32,256]{3,2,1,0:T(8,128)S(1)}, f32[8,32,128]{2,1,0:T(8,128)S(1)}, f32[8,32,128]{2,1,0:T(8,128)S(1)}, s32[2]{0:T(128)S(1)}) custom-call(s32[2]{0:T(128)S(1)} %get-tuple-element.62.side.ahead, f32[8,8,32,256]{3,2,1,0:T(8,128)S(1)} %get-tuple-element.63.tiles, f32[8,32,128]{2,1,0:T(8,128)S(1)} %collective-permute-done.2.near, ...), custom_call_target="tpu_custom_call" | custom-call | flops 2684354560 | bytes 8388608 | tf_op jit(solution)/shard_map/middle_stage/pallas_call | solution.py:271
  40.9 3.0 %collective-permute-start.7 = (f32[8,32,128]{2,1,0:T(8,128)S(1)}, f32[8,32,128]{2,1,0:T(8,128)S(1)}, u32[]{:S(2)}, u32[]{:S(2)}) collective-permute-start(f32[8,32,128]{2,1,0:T(8,128)S(1)} %get-tuple-element.74), channel_id=1, source_target_pairs={{1,2},{2,1},{5,6},{6,5},{9,10},{10,9},{13,14},{14,13},{17,18},{18,... | collective-permute-start | bytes 393224 | tf_op jit(solution)/shard_map/ppermute | solution.py:589
  44.0 4.6 %first_stage.4 = (f32[12,8,32,256]{3,2,1,0:T(8,128)S(1)}, f32[12,32,128]{2,1,0:T(8,128)S(1)}, f32[12,32,128]{2,1,0:T(8,128)S(1)}, s32[2]{0:T(128)S(1)}) custom-call(s32[2]{0:T(128)S(1)} %get-tuple-element.68.side, s32[12,8,32,256]{3,2,1,0:T(8,128)S(1)} %get-tuple-element.117.signs, f32[8,32,256]{2,1,0:T(8,128)S(1)} %copy-done.1, ...), custom_call_target="tpu_custom_call" | custom-call | flops 2415919104 | bytes 12582912 | tf_op jit(solution)/shard_map/first_stage/pallas_call | solution.py:220
  48.6 2.9 %last_column_stage.3 = (f32[8,8,32,256]{3,2,1,0:T(8,128)S(1)}, f32[8,120,256]{2,1,0:T(8,128)S(1)}, f32[8,120,256]{2,1,0:T(8,128)S(1)}, s32[2]{0:T(128)S(1)}) custom-call(s32[2]{0:T(128)S(1)} %get-tuple-element.71.side, f32[8,8,32,256]{3,2,1,0:T(8,128)S(1)} %get-tuple-element.72.tiles, f32[8,32,128]{2,1,0:T(8,128)S(1)} %collective-permute-done.6.near, ...), custom_call_target="tpu_custom_call" | custom-call | flops 1073741824 | bytes 8388608 | tf_op jit(solution)/shard_map/last_column_stage/pallas_call | solution.py:303
  51.9 2.8 %collective-permute-start.9 = (f32[12,32,128]{2,1,0:T(8,128)S(1)}, f32[12,32,128]{2,1,0:T(8,128)S(1)}, u32[]{:S(2)}, u32[]{:S(2)}) collective-permute-start(f32[12,32,128]{2,1,0:T(8,128)S(1)} %get-tuple-element.78), channel_id=1, source_target_pairs={{1,2},{2,1},{5,6},{6,5},{9,10},{10,9},{13,14},{14,13},{17,18},{18,... | collective-permute-start | bytes 589832 | tf_op jit(solution)/shard_map/ppermute | solution.py:589
  54.8 4.4 %collective-permute-done.8.near = f32[12,32,128]{2,1,0:T(8,128)S(1)} collective-permute-done((f32[12,32,128]{2,1,0:T(8,128)S(1)}, f32[12,32,128]{2,1,0:T(8,128)S(1)}, u32[]{:S(2)}, u32[]{:S(2)}) %collective-permute-start.8) | collective-permute-done | bytes 196640 | tf_op jit(solution)/shard_map/ppermute | solution.py:589
  59.2 1.9 %collective-permute-done.9.far = f32[12,32,128]{2,1,0:T(8,128)S(1)} collective-permute-done((f32[12,32,128]{2,1,0:T(8,128)S(1)}, f32[12,32,128]{2,1,0:T(8,128)S(1)}, u32[]{:S(2)}, u32[]{:S(2)}) %collective-permute-start.9) | collective-permute-done | bytes 196640 | tf_op jit(solution)/shard_map/ppermute | solution.py:589
  61.1 7.1 %middle_stage.4 = (f32[12,8,32,256]{3,2,1,0:T(8,128)S(1)}, f32[12,32,128]{2,1,0:T(8,128)S(1)}, f32[12,32,128]{2,1,0:T(8,128)S(1)}, s32[2]{0:T(128)S(1)}) custom-call(s32[2]{0:T(128)S(1)} %get-tuple-element.75.side, f32[12,8,32,256]{3,2,1,0:T(8,128)S(1)} %get-tuple-element.76.tiles, f32[12,32,128]{2,1,0:T(8,128)S(1)} %collective-permute-done.8.near, ...), custom_call_target="tpu_custom_call" | custom-call | flops 4026531840 | bytes 12582912 | tf_op jit(solution)/shard_map/middle_stage/pallas_call | solution.py:271
  68.2 2.8 %collective-permute-start.14 = (f32[12,32,128]{2,1,0:T(8,128)S(1)}, f32[12,32,128]{2,1,0:T(8,128)S(1)}, u32[]{:S(2)}, u32[]{:S(2)}) collective-permute-start(f32[12,32,128]{2,1,0:T(8,128)S(1)} %get-tuple-element.86), channel_id=1, source_target_pairs={{1,2},{2,1},{5,6},{6,5},{9,10},{10,9},{13,14},{14,13},{17,18},{18,... | collective-permute-start | bytes 589832 | tf_op jit(solution)/shard_map/ppermute | solution.py:589
  71.0 4.6 %first_stage.5 = (f32[12,8,32,256]{3,2,1,0:T(8,128)S(1)}, f32[12,32,128]{2,1,0:T(8,128)S(1)}, f32[12,32,128]{2,1,0:T(8,128)S(1)}, s32[2]{0:T(128)S(1)}) custom-call(s32[2]{0:T(128)S(1)} %get-tuple-element.80.side, s32[12,8,32,256]{3,2,1,0:T(8,128)S(1)} %get-tuple-element.116.signs, f32[8,32,256]{2,1,0:T(8,128)S(1)} %copy-done.1, ...), custom_call_target="tpu_custom_call" | custom-call | flops 2415919104 | bytes 12582912 | tf_op jit(solution)/shard_map/first_stage/pallas_call | solution.py:220
  76.6 3.6 %last_column_stage.4 = (f32[12,8,32,256]{3,2,1,0:T(8,128)S(1)}, f32[12,120,256]{2,1,0:T(8,128)S(1)}, f32[12,120,256]{2,1,0:T(8,128)S(1)}, s32[2]{0:T(128)S(1)}) custom-call(s32[2]{0:T(128)S(1)} %get-tuple-element.83.side, f32[12,8,32,256]{3,2,1,0:T(8,128)S(1)} %get-tuple-element.84.tiles, f32[12,32,128]{2,1,0:T(8,128)S(1)} %collective-permute-done.13.near, ...), custom_call_target="tpu_custom_call" | custom-call | flops 1610612736 | bytes 12582912 | tf_op jit(solution)/shard_map/last_column_stage/pallas_call | solution.py:303
  80.3 2.7 %collective-permute-start.18 = (f32[8,120,256]{2,1,0:T(8,128)S(1)}, f32[8,120,256]{2,1,0:T(8,128)S(1)}, u32[]{:S(2)}, u32[]{:S(2)}) collective-permute-start(f32[8,120,256]{2,1,0:T(8,128)S(1)} %get-tuple-element.94), channel_id=1, source_target_pairs={{4,8},{8,4},{12,16},{16,12},{20,24},{24,20},{28,32},{32,28},{36,40... | collective-permute-start | bytes 2949128 | tf_op jit(solution)/shard_map/ppermute | solution.py:589
  83.1 2.8 %collective-permute-start.16 = (f32[12,32,128]{2,1,0:T(8,128)S(1)}, f32[12,32,128]{2,1,0:T(8,128)S(1)}, u32[]{:S(2)}, u32[]{:S(2)}) collective-permute-start(f32[12,32,128]{2,1,0:T(8,128)S(1)} %get-tuple-element.90), channel_id=1, source_target_pairs={{1,2},{2,1},{5,6},{6,5},{9,10},{10,9},{13,14},{14,13},{17,18},{18,... | collective-permute-start | bytes 589832 | tf_op jit(solution)/shard_map/ppermute | solution.py:589
  86.0 4.5 %collective-permute-start.21 = (f32[12,120,256]{2,1,0:T(8,128)S(1)}, f32[12,120,256]{2,1,0:T(8,128)S(1)}, u32[]{:S(2)}, u32[]{:S(2)}) collective-permute-start(f32[12,120,256]{2,1,0:T(8,128)S(1)} %get-tuple-element.102), channel_id=1, source_target_pairs={{4,8},{8,4},{12,16},{16,12},{20,24},{24,20},{28,32},{32,28},{36,40... | collective-permute-start | bytes 4423688 | tf_op jit(solution)/shard_map/ppermute | solution.py:589
  90.5 1.0 collective-permute-done.16.far
  91.5 7.1 %middle_stage.5 = (f32[12,8,32,256]{3,2,1,0:T(8,128)S(1)}, f32[12,32,128]{2,1,0:T(8,128)S(1)}, f32[12,32,128]{2,1,0:T(8,128)S(1)}, s32[2]{0:T(128)S(1)}) custom-call(s32[2]{0:T(128)S(1)} %get-tuple-element.87.side, f32[12,8,32,256]{3,2,1,0:T(8,128)S(1)} %get-tuple-element.88.tiles, f32[12,32,128]{2,1,0:T(8,128)S(1)} %collective-permute-done.15.near, ...), custom_call_target="tpu_custom_call" | custom-call | flops 4026531840 | bytes 12582912 | tf_op jit(solution)/shard_map/middle_stage/pallas_call | solution.py:271
  98.7 2.7 %collective-permute-start.20 = (f32[12,32,128]{2,1,0:T(8,128)S(1)}, f32[12,32,128]{2,1,0:T(8,128)S(1)}, u32[]{:S(2)}, u32[]{:S(2)}) collective-permute-start(f32[12,32,128]{2,1,0:T(8,128)S(1)} %get-tuple-element.99), channel_id=1, source_target_pairs={{1,2},{2,1},{5,6},{6,5},{9,10},{10,9},{13,14},{14,13},{17,18},{18,... | collective-permute-start | bytes 589832 | tf_op jit(solution)/shard_map/ppermute | solution.py:589
  101.4 2.7 %sketch_stage.2 = (f32[8,8,32,256]{3,2,1,0:T(8,128)S(1)}, s32[2]{0:T(128)S(1)}) custom-call(s32[2]{0:T(128)S(1)} %get-tuple-element.92.side, f32[8,8,32,256]{3,2,1,0:T(8,128)S(1)} %get-tuple-element.93.tiles, f32[8,120,256]{2,1,0:T(8,128)S(1)} %collective-permute-done.10.ahead.inner, f32[8,120,256]{2,1,0:T(8,128)S(1)} %collective-permute-done.18.outer, ...), custom_call_target="tpu_custom_call" | custom-call | flops 1610612736 | bytes 8388608 | tf_op jit(solution)/shard_map/sketch_stage/pallas_call | solution.py:327
  104.3 1.9 %collective-permute-done.20.far = f32[12,32,128]{2,1,0:T(8,128)S(1)} collective-permute-done((f32[12,32,128]{2,1,0:T(8,128)S(1)}, f32[12,32,128]{2,1,0:T(8,128)S(1)}, u32[]{:S(2)}, u32[]{:S(2)}) %collective-permute-start.20) | collective-permute-done | bytes 196640 | tf_op jit(solution)/shard_map/ppermute | solution.py:589
  106.2 3.6 %last_column_stage.5 = (f32[12,8,32,256]{3,2,1,0:T(8,128)S(1)}, f32[12,120,256]{2,1,0:T(8,128)S(1)}, f32[12,120,256]{2,1,0:T(8,128)S(1)}, s32[2]{0:T(128)S(1)}) custom-call(s32[2]{0:T(128)S(1)} %get-tuple-element.96.side, f32[12,8,32,256]{3,2,1,0:T(8,128)S(1)} %get-tuple-element.97.tiles, f32[12,32,128]{2,1,0:T(8,128)S(1)} %collective-permute-done.19.near, ...), custom_call_target="tpu_custom_call" | custom-call | flops 1610612736 | bytes 12582912 | tf_op jit(solution)/shard_map/last_column_stage/pallas_call | solution.py:303
  110.0 3.3 %collective-permute-start.23 = (f32[12,120,256]{2,1,0:T(8,128)S(1)}, f32[12,120,256]{2,1,0:T(8,128)S(1)}, u32[]{:S(2)}, u32[]{:S(2)}) collective-permute-start(f32[12,120,256]{2,1,0:T(8,128)S(1)} %get-tuple-element.111), channel_id=1, source_target_pairs={{4,8},{8,4},{12,16},{16,12},{20,24},{24,20},{28,32},{32,28},{36,40... | collective-permute-start | bytes 4423688 | tf_op jit(solution)/shard_map/ppermute | solution.py:589
  113.6 3.7 %sketch_stage.3 = (f32[12,8,32,256]{3,2,1,0:T(8,128)S(1)}, s32[2]{0:T(128)S(1)}) custom-call(s32[2]{0:T(128)S(1)} %get-tuple-element.100.side, f32[12,8,32,256]{3,2,1,0:T(8,128)S(1)} %get-tuple-element.101.tiles, f32[12,120,256]{2,1,0:T(8,128)S(1)} %collective-permute-done.17.ahead.inner, f32[12,120,256]{2,1,0:T(8,128)S(1)} %collective-permute-done.21.outer, ...), custom_call_target="tpu_custom_call" | custom-call | flops 2415919104 | bytes 12582912 | tf_op jit(solution)/shard_map/sketch_stage/pallas_call | solution.py:327
  117.4 4.0 %early_gram_stage.1 = (f32[20,20]{1,0:T(8,128)S(1)}, s32[2]{0:T(128)S(1)}) custom-call(s32[2]{0:T(128)S(1)} %get-tuple-element.103.side, f32[8,32,8,256]{3,2,1,0:T(8,128)S(1)} %bitcast.8, f32[12,32,8,256]{3,2,1,0:T(8,128)S(1)} %bitcast.5), custom_call_target="tpu_custom_call" | custom-call | flops 2147483648 | bytes 8388608 | tf_op jit(solution)/shard_map/early_gram_stage/pallas_call | solution.py:393
  121.4 2.4 %sketch_main_stage.1 = (f32[12,256,256]{2,1,0:T(8,128)S(1)}, s32[2]{0:T(128)}) custom-call(s32[2]{0:T(128)S(1)} %get-tuple-element.107.side, f32[12,8,32,256]{3,2,1,0:T(8,128)S(1)} %get-tuple-element.108.tiles, bf16[256,1536]{1,0:T(8,128)(2,1)S(1)} %get-tuple-element.95.matrix), custom_call_target="tpu_custom_call" | custom-call | flops 1207959552 | bytes 6291456 | tf_op jit(solution)/shard_map/sketch_main_stage/pallas_call | solution.py:346
  123.7 9.0 %collective-permute-done.23.outer = f32[12,120,256]{2,1,0:T(8,128)S(1)} collective-permute-done((f32[12,120,256]{2,1,0:T(8,128)S(1)}, f32[12,120,256]{2,1,0:T(8,128)S(1)}, u32[]{:S(2)}, u32[]{:S(2)}) %collective-permute-start.23) | collective-permute-done | bytes 1474592 | tf_op jit(solution)/shard_map/ppermute | solution.py:589
  132.7 6.0 %gram_stage.1 = (f32[2,8,128]{2,1,0:T(8,128)S(1)}, f32[12,32,8,256]{3,2,1,0:T(8,128)S(1)}) custom-call(f32[20,20]{1,0:T(8,128)S(1)} %get-tuple-element.106.early, f32[12,256,256]{2,1,0:T(8,128)S(1)} %get-tuple-element.109.main, f32[12,120,256]{2,1,0:T(8,128)S(1)} %collective-permute-done.22.inner, f32[12,120,256]{2,1,0:T(8,128)S(1)} %collective-permute-done.23.outer, ...), custom_call_target="tpu_custom_call" | custom-call | flops 2147483648 | bytes 8388608 | tf_op jit(solution)/shard_map/gram_stage/pallas_call | solution.py:442
  138.8 1.2 collective-permute-done.24.other
  140.1 3.6 %collective-permute-done.25.other = f32[2,8,128]{2,1,0:T(8,128)S(1)} collective-permute-done((f32[2,8,128]{2,1,0:T(8,128)S(1)}, f32[2,8,128]{2,1,0:T(8,128)S(1)}, u32[]{:S(2)}, u32[]{:S(2)}) %collective-permute-start.25) | collective-permute-done | bytes 8224 | tf_op jit(solution)/shard_map/ppermute | solution.py:509
  143.9 5.1 %collective-permute-done.26.other = f32[2,8,128]{2,1,0:T(8,128)S(1)} collective-permute-done((f32[2,8,128]{2,1,0:T(8,128)S(1)}, f32[2,8,128]{2,1,0:T(8,128)S(1)}, u32[]{:S(2)}, u32[]{:S(2)}) %collective-permute-start.26) | collective-permute-done | bytes 8224 | tf_op jit(solution)/shard_map/ppermute | solution.py:509
  149.5 3.2 %collective-permute-done.27.other = f32[2,8,128]{2,1,0:T(8,128)S(1)} collective-permute-done((f32[2,8,128]{2,1,0:T(8,128)S(1)}, f32[2,8,128]{2,1,0:T(8,128)S(1)}, u32[]{:S(2)}, u32[]{:S(2)}) %collective-permute-start.27) | collective-permute-done | bytes 8224 | tf_op jit(solution)/shard_map/ppermute | solution.py:509
  152.7 1.0 collective-permute-start.28
  153.7 4.2 %collective-permute-done.28.other = f32[2,8,128]{2,1,0:T(8,128)S(1)} collective-permute-done((f32[2,8,128]{2,1,0:T(8,128)S(1)}, f32[2,8,128]{2,1,0:T(8,128)S(1)}, u32[]{:S(2)}, u32[]{:S(2)}) %collective-permute-start.28) | collective-permute-done | bytes 8224 | tf_op jit(solution)/shard_map/ppermute | solution.py:509
  158.0 3.6 %collective-permute-done.29.other = f32[2,8,128]{2,1,0:T(8,128)S(1)} collective-permute-done((f32[2,8,128]{2,1,0:T(8,128)S(1)}, f32[2,8,128]{2,1,0:T(8,128)S(1)}, u32[]{:S(2)}, u32[]{:S(2)}) %collective-permute-start.29) | collective-permute-done | bytes 8224 | tf_op jit(solution)/shard_map/ppermute | solution.py:509
  161.9 4.9 %collective-permute-done.30.other = f32[2,8,128]{2,1,0:T(8,128)S(1)} collective-permute-done((f32[2,8,128]{2,1,0:T(8,128)S(1)}, f32[2,8,128]{2,1,0:T(8,128)S(1)}, u32[]{:S(2)}, u32[]{:S(2)}) %collective-permute-start.30) | collective-permute-done | bytes 8224 | tf_op jit(solution)/shard_map/ppermute | solution.py:509
  166.9 4.6 %factor_stage.1 = (f32[32,32]{1,0:T(8,128)}, f32[32,32]{1,0:T(8,128)S(1)}) custom-call(f32[2,8,128]{2,1,0:T(8,128)S(1)} %merge.13.refs_0_), custom_call_target="tpu_custom_call" | custom-call | tf_op jit(solution)/shard_map/factor_stage/pallas_call | solution.py:547
  171.5 6.6 %basis_stage.1 = f32[32,32,8,256]{3,2,1,0:T(8,128)} custom-call(f32[32,32]{1,0:T(8,128)S(1)} %get-tuple-element.113.inverse, f32[8,32,8,256]{3,2,1,0:T(8,128)S(1)} %bitcast.10, f32[12,32,8,256]{3,2,1,0:T(8,128)S(1)} %bitcast.7, f32[12,32,8,256]{3,2,1,0:T(8,128)S(1)} %get-tuple-element.114.refs_2_), custom_call_target="tpu_custom_call" | custom-call | flops 3221225472 | bytes 16777216 | tf_op jit(solution)/shard_map/basis_stage/pallas_call | solution.py:575
  (64 shorter events, 4.3 us)
Async XLA Ops:
  0.6 1.9 %copy-start.1 = (f32[8,32,256]{2,1,0:T(8,128)S(1)}, f32[8,32,256]{2,1,0:T(8,128)}, u32[]{:S(2)}) copy-start(f32[8,32,256]{2,1,0:T(8,128)} %scale.17) | copy-start | bytes 786436
  3.7 16.5 %collective-permute-start = (f32[8,120,256]{2,1,0:T(8,128)S(1)}, f32[8,120,256]{2,1,0:T(8,128)S(1)}, u32[]{:S(2)}, u32[]{:S(2)}) collective-permute-start(f32[8,120,256]{2,1,0:T(8,128)S(1)} %get-tuple-element.59), channel_id=1, source_target_pairs={{0,4},{4,0},{8,12},{12,8},{16,20},{20,16},{24,28},{28,24},{32,36},... | collective-permute-start | bytes 2949128 | tf_op jit(solution)/shard_map/ppermute | solution.py:589
  3.8 17.5 %collective-permute-start.1 = (f32[8,120,256]{2,1,0:T(8,128)S(1)}, f32[8,120,256]{2,1,0:T(8,128)S(1)}, u32[]{:S(2)}, u32[]{:S(2)}) collective-permute-start(f32[8,120,256]{2,1,0:T(8,128)S(1)} %get-tuple-element.60), channel_id=1, source_target_pairs={{4,8},{8,4},{12,16},{16,12},{20,24},{24,20},{28,32},{32,28},{36,40... | collective-permute-start | bytes 2949128 | tf_op jit(solution)/shard_map/ppermute | solution.py:589
  12.4 4.5 %copy-start.2 = (f32[256,512]{1,0:T(8,128)S(1)}, f32[256,512]{1,0:T(8,128)}, u32[]{:S(2)}) copy-start(f32[256,512]{1,0:T(8,128)} %constant.40.clone.by_in) | copy-start | bytes 1572868
  12.4 4.5 %copy-start.3 = (f32[256,512]{1,0:T(8,128)S(1)}, f32[256,512]{1,0:T(8,128)}, u32[]{:S(2)}) copy-start(f32[256,512]{1,0:T(8,128)} %constant.39.clone.by_out) | copy-start | bytes 1572868
  12.4 4.5 %copy-start.4 = (f32[256,256]{1,0:T(8,128)S(1)}, f32[256,256]{1,0:T(8,128)}, u32[]{:S(2)}) copy-start(f32[256,256]{1,0:T(8,128)} %constant.43.clone.same) | copy-start | bytes 786436
  12.4 4.5 %copy-start.5 = (f32[256,8]{1,0:T(8,128)S(1)}, f32[256,8]{1,0:T(8,128)}, u32[]{:S(2)}) copy-start(f32[256,8]{1,0:T(8,128)} %constant.42.clone.spread) | copy-start | bytes 24580
  12.4 4.5 %copy-start.6 = (f32[8,512]{1,0:T(8,128)S(1)}, f32[8,512]{1,0:T(8,128)}, u32[]{:S(2)}) copy-start(f32[8,512]{1,0:T(8,128)} %constant.41.clone.pick) | copy-start | bytes 49156
  12.4 4.5 %copy-start.7 = (f32[8,8]{1,0:T(8,128)S(1)}, f32[8,8]{1,0:T(8,128)}, u32[]{:S(2)}) copy-start(f32[8,8]{1,0:T(8,128)} %factor.1) | copy-start | bytes 772
  12.5 4.5 %copy-start.8 = (f32[8,8]{1,0:T(8,128)S(1)}, f32[8,8]{1,0:T(8,128)}, u32[]{:S(2)}) copy-start(f32[8,8]{1,0:T(8,128)} %mix.1) | copy-start | bytes 772
  14.0 26.9 %collective-permute-start.4 = (f32[12,120,256]{2,1,0:T(8,128)S(1)}, f32[12,120,256]{2,1,0:T(8,128)S(1)}, u32[]{:S(2)}, u32[]{:S(2)}) collective-permute-start(f32[12,120,256]{2,1,0:T(8,128)S(1)} %get-tuple-element.69), channel_id=1, source_target_pairs={{0,4},{4,0},{8,12},{12,8},{16,20},{20,16},{24,28},{28,24},{32,36},... | collective-permute-start | bytes 4423688 | tf_op jit(solution)/shard_map/ppermute | solution.py:589
  14.1 29.9 %collective-permute-start.5 = (f32[12,120,256]{2,1,0:T(8,128)S(1)}, f32[12,120,256]{2,1,0:T(8,128)S(1)}, u32[]{:S(2)}, u32[]{:S(2)}) collective-permute-start(f32[12,120,256]{2,1,0:T(8,128)S(1)} %get-tuple-element.70), channel_id=1, source_target_pairs={{4,8},{8,4},{12,16},{16,12},{20,24},{24,20},{28,32},{32,28},{36,40... | collective-permute-start | bytes 4423688 | tf_op jit(solution)/shard_map/ppermute | solution.py:589
  21.3 14.9 %copy-start = (bf16[8,1024,256]{2,1,0:T(8,128)(2,1)S(1)}, bf16[8,1024,256]{2,1,0:T(8,128)(2,1)}, u32[]{:S(2)}) copy-start(bf16[8,1024,256]{2,1,0:T(8,128)(2,1)} %constant.38.clone.table) | copy-start | bytes 12582916
  24.7 11.5 %copy-start.9 = (f32[8,32,256]{2,1,0:T(8,128)S(1)}, f32[8,32,256]{2,1,0:T(8,128)}, u32[]{:S(2)}) copy-start(f32[8,32,256]{2,1,0:T(8,128)} %weights.5) | copy-start | bytes 786436
  24.7 7.1 %collective-permute-start.2 = (f32[8,32,128]{2,1,0:T(8,128)S(1)}, f32[8,32,128]{2,1,0:T(8,128)S(1)}, u32[]{:S(2)}, u32[]{:S(2)}) collective-permute-start(f32[8,32,128]{2,1,0:T(8,128)S(1)} %get-tuple-element.64), channel_id=1, source_target_pairs={{0,1},{1,0},{2,3},{3,2},{4,5},{5,4},{6,7},{7,6},{8,9},{9,8},{10,11... | collective-permute-start | bytes 393224 | tf_op jit(solution)/shard_map/ppermute | solution.py:589
  24.9 11.3 %collective-permute-start.3 = (f32[8,32,128]{2,1,0:T(8,128)S(1)}, f32[8,32,128]{2,1,0:T(8,128)S(1)}, u32[]{:S(2)}, u32[]{:S(2)}) collective-permute-start(f32[8,32,128]{2,1,0:T(8,128)S(1)} %get-tuple-element.65), channel_id=1, source_target_pairs={{1,2},{2,1},{5,6},{6,5},{9,10},{10,9},{13,14},{14,13},{17,18},{18,... | collective-permute-start | bytes 393224 | tf_op jit(solution)/shard_map/ppermute | solution.py:589
  31.8 39.2 %collective-permute-start.11 = (f32[12,120,256]{2,1,0:T(8,128)S(1)}, f32[12,120,256]{2,1,0:T(8,128)S(1)}, u32[]{:S(2)}, u32[]{:S(2)}) collective-permute-start(f32[12,120,256]{2,1,0:T(8,128)S(1)} %get-tuple-element.81), channel_id=1, source_target_pairs={{0,4},{4,0},{8,12},{12,8},{16,20},{20,16},{24,28},{28,24},{32,36},... | collective-permute-start | bytes 4423688 | tf_op jit(solution)/shard_map/ppermute | solution.py:589
  31.9 39.1 %collective-permute-start.12 = (f32[12,120,256]{2,1,0:T(8,128)S(1)}, f32[12,120,256]{2,1,0:T(8,128)S(1)}, u32[]{:S(2)}, u32[]{:S(2)}) collective-permute-start(f32[12,120,256]{2,1,0:T(8,128)S(1)} %get-tuple-element.82), channel_id=1, source_target_pairs={{4,8},{8,4},{12,16},{16,12},{20,24},{24,20},{28,32},{32,28},{36,40... | collective-permute-start | bytes 4423688 | tf_op jit(solution)/shard_map/ppermute | solution.py:589
  40.8 7.8 %collective-permute-start.6 = (f32[8,32,128]{2,1,0:T(8,128)S(1)}, f32[8,32,128]{2,1,0:T(8,128)S(1)}, u32[]{:S(2)}, u32[]{:S(2)}) collective-permute-start(f32[8,32,128]{2,1,0:T(8,128)S(1)} %get-tuple-element.73), channel_id=1, source_target_pairs={{0,1},{1,0},{2,3},{3,2},{4,5},{5,4},{6,7},{7,6},{8,9},{9,8},{10,11... | collective-permute-start | bytes 393224 | tf_op jit(solution)/shard_map/ppermute | solution.py:589
  40.9 7.7 %collective-permute-start.7 = (f32[8,32,128]{2,1,0:T(8,128)S(1)}, f32[8,32,128]{2,1,0:T(8,128)S(1)}, u32[]{:S(2)}, u32[]{:S(2)}) collective-permute-start(f32[8,32,128]{2,1,0:T(8,128)S(1)} %get-tuple-element.74), channel_id=1, source_target_pairs={{1,2},{2,1},{5,6},{6,5},{9,10},{10,9},{13,14},{14,13},{17,18},{18,... | collective-permute-start | bytes 393224 | tf_op jit(solution)/shard_map/ppermute | solution.py:589
  51.6 9.5 %collective-permute-start.10 = (f32[8,120,256]{2,1,0:T(8,128)S(1)}, f32[8,120,256]{2,1,0:T(8,128)S(1)}, u32[]{:S(2)}, u32[]{:S(2)}) collective-permute-start(f32[8,120,256]{2,1,0:T(8,128)S(1)} %get-tuple-element.79), channel_id=1, source_target_pairs={{0,4},{4,0},{8,12},{12,8},{16,20},{20,16},{24,28},{28,24},{32,36},... | collective-permute-start | bytes 2949128 | tf_op jit(solution)/shard_map/ppermute | solution.py:589
  51.8 7.3 %collective-permute-start.8 = (f32[12,32,128]{2,1,0:T(8,128)S(1)}, f32[12,32,128]{2,1,0:T(8,128)S(1)}, u32[]{:S(2)}, u32[]{:S(2)}) collective-permute-start(f32[12,32,128]{2,1,0:T(8,128)S(1)} %get-tuple-element.77), channel_id=1, source_target_pairs={{0,1},{1,0},{2,3},{3,2},{4,5},{5,4},{6,7},{7,6},{8,9},{9,8},{10,11... | collective-permute-start | bytes 589832 | tf_op jit(solution)/shard_map/ppermute | solution.py:589
  51.9 9.1 %collective-permute-start.9 = (f32[12,32,128]{2,1,0:T(8,128)S(1)}, f32[12,32,128]{2,1,0:T(8,128)S(1)}, u32[]{:S(2)}, u32[]{:S(2)}) collective-permute-start(f32[12,32,128]{2,1,0:T(8,128)S(1)} %get-tuple-element.78), channel_id=1, source_target_pairs={{1,2},{2,1},{5,6},{6,5},{9,10},{10,9},{13,14},{14,13},{17,18},{18,... | collective-permute-start | bytes 589832 | tf_op jit(solution)/shard_map/ppermute | solution.py:589
  68.1 7.5 %collective-permute-start.13 = (f32[12,32,128]{2,1,0:T(8,128)S(1)}, f32[12,32,128]{2,1,0:T(8,128)S(1)}, u32[]{:S(2)}, u32[]{:S(2)}) collective-permute-start(f32[12,32,128]{2,1,0:T(8,128)S(1)} %get-tuple-element.85), channel_id=1, source_target_pairs={{0,1},{1,0},{2,3},{3,2},{4,5},{5,4},{6,7},{7,6},{8,9},{9,8},{10,11... | collective-permute-start | bytes 589832 | tf_op jit(solution)/shard_map/ppermute | solution.py:589
  68.2 8.3 %collective-permute-start.14 = (f32[12,32,128]{2,1,0:T(8,128)S(1)}, f32[12,32,128]{2,1,0:T(8,128)S(1)}, u32[]{:S(2)}, u32[]{:S(2)}) collective-permute-start(f32[12,32,128]{2,1,0:T(8,128)S(1)} %get-tuple-element.86), channel_id=1, source_target_pairs={{1,2},{2,1},{5,6},{6,5},{9,10},{10,9},{13,14},{14,13},{17,18},{18,... | collective-permute-start | bytes 589832 | tf_op jit(solution)/shard_map/ppermute | solution.py:589
  80.2 11.3 %collective-permute-start.17 = (f32[12,120,256]{2,1,0:T(8,128)S(1)}, f32[12,120,256]{2,1,0:T(8,128)S(1)}, u32[]{:S(2)}, u32[]{:S(2)}) collective-permute-start(f32[12,120,256]{2,1,0:T(8,128)S(1)} %get-tuple-element.91), channel_id=1, source_target_pairs={{0,4},{4,0},{8,12},{12,8},{16,20},{20,16},{24,28},{28,24},{32,36},... | collective-permute-start | bytes 4423688 | tf_op jit(solution)/shard_map/ppermute | solution.py:589
  80.3 21.1 %collective-permute-start.18 = (f32[8,120,256]{2,1,0:T(8,128)S(1)}, f32[8,120,256]{2,1,0:T(8,128)S(1)}, u32[]{:S(2)}, u32[]{:S(2)}) collective-permute-start(f32[8,120,256]{2,1,0:T(8,128)S(1)} %get-tuple-element.94), channel_id=1, source_target_pairs={{4,8},{8,4},{12,16},{16,12},{20,24},{24,20},{28,32},{32,28},{36,40... | collective-permute-start | bytes 2949128 | tf_op jit(solution)/shard_map/ppermute | solution.py:589
  83.1 7.5 %collective-permute-start.15 = (f32[12,32,128]{2,1,0:T(8,128)S(1)}, f32[12,32,128]{2,1,0:T(8,128)S(1)}, u32[]{:S(2)}, u32[]{:S(2)}) collective-permute-start(f32[12,32,128]{2,1,0:T(8,128)S(1)} %get-tuple-element.89), channel_id=1, source_target_pairs={{0,1},{1,0},{2,3},{3,2},{4,5},{5,4},{6,7},{7,6},{8,9},{9,8},{10,11... | collective-permute-start | bytes 589832 | tf_op jit(solution)/shard_map/ppermute | solution.py:589
  83.1 8.4 %collective-permute-start.16 = (f32[12,32,128]{2,1,0:T(8,128)S(1)}, f32[12,32,128]{2,1,0:T(8,128)S(1)}, u32[]{:S(2)}, u32[]{:S(2)}) collective-permute-start(f32[12,32,128]{2,1,0:T(8,128)S(1)} %get-tuple-element.90), channel_id=1, source_target_pairs={{1,2},{2,1},{5,6},{6,5},{9,10},{10,9},{13,14},{14,13},{17,18},{18,... | collective-permute-start | bytes 589832 | tf_op jit(solution)/shard_map/ppermute | solution.py:589
  86.0 27.7 %collective-permute-start.21 = (f32[12,120,256]{2,1,0:T(8,128)S(1)}, f32[12,120,256]{2,1,0:T(8,128)S(1)}, u32[]{:S(2)}, u32[]{:S(2)}) collective-permute-start(f32[12,120,256]{2,1,0:T(8,128)S(1)} %get-tuple-element.102), channel_id=1, source_target_pairs={{4,8},{8,4},{12,16},{16,12},{20,24},{24,20},{28,32},{32,28},{36,40... | collective-permute-start | bytes 4423688 | tf_op jit(solution)/shard_map/ppermute | solution.py:589
  98.6 5.7 %collective-permute-start.19 = (f32[12,32,128]{2,1,0:T(8,128)S(1)}, f32[12,32,128]{2,1,0:T(8,128)S(1)}, u32[]{:S(2)}, u32[]{:S(2)}) collective-permute-start(f32[12,32,128]{2,1,0:T(8,128)S(1)} %get-tuple-element.98), channel_id=1, source_target_pairs={{0,1},{1,0},{2,3},{3,2},{4,5},{5,4},{6,7},{7,6},{8,9},{9,8},{10,11... | collective-permute-start | bytes 589832 | tf_op jit(solution)/shard_map/ppermute | solution.py:589
  98.7 7.6 %collective-permute-start.20 = (f32[12,32,128]{2,1,0:T(8,128)S(1)}, f32[12,32,128]{2,1,0:T(8,128)S(1)}, u32[]{:S(2)}, u32[]{:S(2)}) collective-permute-start(f32[12,32,128]{2,1,0:T(8,128)S(1)} %get-tuple-element.99), channel_id=1, source_target_pairs={{1,2},{2,1},{5,6},{6,5},{9,10},{10,9},{13,14},{14,13},{17,18},{18,... | collective-permute-start | bytes 589832 | tf_op jit(solution)/shard_map/ppermute | solution.py:589
  109.9 13.9 %collective-permute-start.22 = (f32[12,120,256]{2,1,0:T(8,128)S(1)}, f32[12,120,256]{2,1,0:T(8,128)S(1)}, u32[]{:S(2)}, u32[]{:S(2)}) collective-permute-start(f32[12,120,256]{2,1,0:T(8,128)S(1)} %get-tuple-element.110), channel_id=1, source_target_pairs={{0,4},{4,0},{8,12},{12,8},{16,20},{20,16},{24,28},{28,24},{32,36},... | collective-permute-start | bytes 4423688 | tf_op jit(solution)/shard_map/ppermute | solution.py:589
  110.0 22.8 %collective-permute-start.23 = (f32[12,120,256]{2,1,0:T(8,128)S(1)}, f32[12,120,256]{2,1,0:T(8,128)S(1)}, u32[]{:S(2)}, u32[]{:S(2)}) collective-permute-start(f32[12,120,256]{2,1,0:T(8,128)S(1)} %get-tuple-element.111), channel_id=1, source_target_pairs={{4,8},{8,4},{12,16},{16,12},{20,24},{24,20},{28,32},{32,28},{36,40... | collective-permute-start | bytes 4423688 | tf_op jit(solution)/shard_map/ppermute | solution.py:589
  138.7 1.2 collective-permute-start.24
  140.0 3.7 %collective-permute-start.25 = (f32[2,8,128]{2,1,0:T(8,128)S(1)}, f32[2,8,128]{2,1,0:T(8,128)S(1)}, u32[]{:S(2)}, u32[]{:S(2)}) collective-permute-start(f32[2,8,128]{2,1,0:T(8,128)S(1)} %merge.7.mine), channel_id=1, source_target_pairs={{0,8},{4,12},{8,0},{12,4},{16,24},{20,28},{24,16},{28,20},{32,40},... | collective-permute-start | bytes 24584 | tf_op jit(solution)/shard_map/ppermute | solution.py:509
  143.7 5.2 %collective-permute-start.26 = (f32[2,8,128]{2,1,0:T(8,128)S(1)}, f32[2,8,128]{2,1,0:T(8,128)S(1)}, u32[]{:S(2)}, u32[]{:S(2)}) collective-permute-start(f32[2,8,128]{2,1,0:T(8,128)S(1)} %merge.8.mine), channel_id=1, source_target_pairs={{0,16},{4,20},{8,24},{12,28},{16,0},{20,4},{24,8},{28,12},{32,48},... | collective-permute-start | bytes 24584 | tf_op jit(solution)/shard_map/ppermute | solution.py:509
  148.9 3.7 %collective-permute-start.27 = (f32[2,8,128]{2,1,0:T(8,128)S(1)}, f32[2,8,128]{2,1,0:T(8,128)S(1)}, u32[]{:S(2)}, u32[]{:S(2)}) collective-permute-start(f32[2,8,128]{2,1,0:T(8,128)S(1)} %merge.9.mine), channel_id=1, source_target_pairs={{0,32},{4,36},{8,40},{12,44},{16,48},{20,52},{24,56},{28,60},{32,0... | collective-permute-start | bytes 24584 | tf_op jit(solution)/shard_map/ppermute | solution.py:509
  152.7 5.2 %collective-permute-start.28 = (f32[2,8,128]{2,1,0:T(8,128)S(1)}, f32[2,8,128]{2,1,0:T(8,128)S(1)}, u32[]{:S(2)}, u32[]{:S(2)}) collective-permute-start(f32[2,8,128]{2,1,0:T(8,128)S(1)} %merge.10.mine), channel_id=1, source_target_pairs={{0,64},{4,68},{8,72},{12,76},{16,80},{20,84},{24,88},{28,92},{32,9... | collective-permute-start | bytes 24584 | tf_op jit(solution)/shard_map/ppermute | solution.py:509
  157.9 3.7 %collective-permute-start.29 = (f32[2,8,128]{2,1,0:T(8,128)S(1)}, f32[2,8,128]{2,1,0:T(8,128)S(1)}, u32[]{:S(2)}, u32[]{:S(2)}) collective-permute-start(f32[2,8,128]{2,1,0:T(8,128)S(1)} %merge.11.mine), channel_id=1, source_target_pairs={{0,1},{1,0},{2,3},{3,2},{4,5},{5,4},{6,7},{7,6},{8,9},{9,8},{10,11... | collective-permute-start | bytes 24584 | tf_op jit(solution)/shard_map/ppermute | solution.py:509
  161.6 5.2 %collective-permute-start.30 = (f32[2,8,128]{2,1,0:T(8,128)S(1)}, f32[2,8,128]{2,1,0:T(8,128)S(1)}, u32[]{:S(2)}, u32[]{:S(2)}) collective-permute-start(f32[2,8,128]{2,1,0:T(8,128)S(1)} %merge.12.mine), channel_id=1, source_target_pairs={{0,2},{1,3},{2,0},{3,1},{4,6},{5,7},{6,4},{7,5},{8,10},{9,11},{10,... | collective-permute-start | bytes 24584 | tf_op jit(solution)/shard_map/ppermute | solution.py:509
